TPU v7x, 256 devices: a whole 4x4x8 slice. The times are simulated.
256 devices in a mesh: grp: 16 (over z_lo, x, core), dev: 16 (over z_hi, y).
Axes of the slice: x: 4, y: 4, z: 8 (z_hi: 4, z_lo: 2; z = z_hi * 2 + z_lo), core: 2. Of those that a mesh axis runs over, the one named last changes fastest.
Arguments:
- patches: bfloat16 [512, 256, 384], P('dev', 'grp'), may hold values from -6 to 6
- tissue: int32 [512, 256], replicated, may hold values from 0 to 1, as said below
- region_slide: int32 [512], replicated, may hold values from 0 to 3, never falling along the last dimension, each value on 1 to 256 neighbouring positions
- w_up: bfloat16 [384, 1536], replicated, may hold values from -0.3125 to 0.3125
- w_down: bfloat16 [1536, 384], replicated, may hold values from -0.15625 to 0.15625
- w_embed: bfloat16 [384, 192], replicated, may hold values from -0.3125 to 0.3125
- w_query: bfloat16 [192, 192], replicated, may hold values from -0.4375 to 0.4375
- w_key: bfloat16 [192, 192], replicated, may hold values from -0.4375 to 0.4375
- w_value: bfloat16 [192, 192], replicated, may hold values from -0.4375 to 0.4375
- w_out: bfloat16 [192, 192], replicated, may hold values from -0.4375 to 0.4375
- att_v: float32 [192, 192], replicated, may hold values from -0.4375 to 0.4375
- att_u: float32 [192, 192], replicated, may hold values from -0.4375 to 0.4375
- att_w: float32 [192], replicated, may hold values from -0.4 to 0.4
- w_class: float32 [192, 3], replicated, may hold values from -0.4375 to 0.4375
- g_logits: float32 [4, 3], replicated, may hold values from -6 to 6
Outputs:
- logits: float32 [4, 3], replicated
- g_up: float32 [384, 1536], replicated
- g_down: float32 [1536, 384], replicated
- g_embed: float32 [384, 192], replicated
- g_query: float32 [192, 192], replicated
- g_key: float32 [192, 192], replicated
- g_value: float32 [192, 192], replicated
- g_out: float32 [192, 192], replicated
- g_att_v: float32 [192, 192], replicated
- g_att_u: float32 [192, 192], replicated
- g_att_w: float32 [192], replicated
- g_class: float32 [192, 3], replicated
Inputs may be any that keep to these rules, and one draw needn't show every extreme that they name: Each region has its own share of tissue patches, from none of its 256 patches to all of them. `region_slide`: slide numbers never fall along the regions, and every slide has a region.
All inputs are finite; a program needn't handle non-finite values.
Results may differ from a plain program's by a relative error of at most 0.019.
Values may be sent and summed in bfloat16 or wider, within the bound.
No kernel may reach another device: no remote copies, remote signals or barrier semaphores. Data moves between devices by JAX's collectives and lax.ppermute only.
A program may use at most 64 MiB of HBM per device.

v0:
```python
import math

import jax
import jax.numpy as jnp
from jax import lax
from jax.sharding import PartitionSpec as P

D1 = 384
HEADS = 6
HEAD_DIM = 32
PATCH = 256
SLIDES = 4


HIGHEST = lax.Precision.HIGHEST


def product(left_op, right_op):
    return jnp.dot(left_op, right_op, preferred_element_type=jnp.float32)


def gram_product(left_op, right_op):
    return lax.dot_general(
        left_op, right_op, (((0,), (0,)), ((), ())), preferred_element_type=jnp.float32
    )


def back_product(left_op, right_op):
    return lax.dot_general(
        left_op, right_op, (((1,), (1,)), ((), ())), preferred_element_type=jnp.float32
    )


def precise(left_op, right_op):
    return jnp.dot(left_op, right_op, precision=HIGHEST, preferred_element_type=jnp.float32)


def mix_heads(form, left_op, right_op):
    return jnp.einsum(form, left_op, right_op, preferred_element_type=jnp.float32)


def patch_forward(token_rows, tissue_rows, w_up, w_down, w_embed):
    pre_act = product(token_rows, w_up)
    hidden = jax.nn.gelu(pre_act).astype(jnp.bfloat16)
    middle = (token_rows.astype(jnp.float32) + product(hidden, w_down)).astype(jnp.bfloat16)
    features = (tissue_rows[:, None] * product(middle, w_embed)).astype(jnp.bfloat16)
    return (features, (pre_act, hidden, middle))


def patch_backward(token_rows, kept_patch, d_features, w_down, w_embed):
    pre_act, hidden, middle = kept_patch
    g_embed = gram_product(middle, d_features)
    d_middle = back_product(d_features, w_embed).astype(jnp.bfloat16)
    g_down = gram_product(hidden, d_middle)
    d_hidden = back_product(d_middle, w_down)
    pullback = jax.vjp(jax.nn.gelu, pre_act)[1]
    d_pre = pullback(d_hidden)[0].astype(jnp.bfloat16)
    g_up = gram_product(token_rows, d_pre)
    return (g_up, g_down, g_embed)


def region_forward(features, tissue_f, w_query, w_key, w_value, w_out):
    flat = features.reshape(-1, features.shape[2])
    split = (features.shape[0], PATCH, HEADS, HEAD_DIM)
    queries = product(flat, w_query).astype(jnp.bfloat16).reshape(split)
    key_heads = product(flat, w_key).astype(jnp.bfloat16).reshape(split)
    value_heads = product(flat, w_value).astype(jnp.bfloat16).reshape(split)
    scores = mix_heads("nqhd,nkhd->nhqk", queries, key_heads) * (1.0 / math.sqrt(HEAD_DIM))
    attn_probs = jax.nn.softmax(scores, axis=-1)
    attn_b = attn_probs.astype(jnp.bfloat16)
    attended = (
        mix_heads("nhqk,nkhd->nqhd", attn_b, value_heads).astype(jnp.bfloat16).reshape(flat.shape)
    )
    mixed = flat.astype(jnp.float32) + product(attended, w_out)
    tissue_count = jnp.maximum(jnp.sum(tissue_f, axis=1), 1.0)
    region = (
        jnp.sum(tissue_f[:, :, None] * mixed.reshape(features.shape), axis=1)
        / tissue_count[:, None]
    )
    return (region, (queries, key_heads, value_heads, attn_probs, attn_b, attended))


def region_backward(features, tissue_f, d_region, kept_region, w_query, w_key, w_value, w_out):
    queries, key_heads, value_heads, attn_probs, attn_b, attended = kept_region
    flat = features.reshape(-1, features.shape[2])
    tissue_count = jnp.maximum(jnp.sum(tissue_f, axis=1), 1.0)
    d_mixed = (
        (tissue_f[:, :, None] * d_region[:, None, :] / tissue_count[:, None, None])
        .astype(jnp.bfloat16)
        .reshape(flat.shape)
    )
    g_out = gram_product(attended, d_mixed)
    d_attended = back_product(d_mixed, w_out).astype(jnp.bfloat16).reshape(queries.shape)
    d_probs = mix_heads("nqhd,nkhd->nhqk", d_attended, value_heads)
    centered = d_probs - jnp.sum(attn_probs * d_probs, axis=-1, keepdims=True)
    d_scores = (attn_probs * centered * (1.0 / math.sqrt(HEAD_DIM))).astype(jnp.bfloat16)
    d_query = (
        mix_heads("nhqk,nkhd->nqhd", d_scores, key_heads).astype(jnp.bfloat16).reshape(flat.shape)
    )
    d_key = mix_heads("nhqk,nqhd->nkhd", d_scores, queries).astype(jnp.bfloat16).reshape(flat.shape)
    d_value = (
        mix_heads("nhqk,nqhd->nkhd", attn_b, d_attended).astype(jnp.bfloat16).reshape(flat.shape)
    )
    g_query = gram_product(flat, d_query)
    g_key = gram_product(flat, d_key)
    g_value = gram_product(flat, d_value)
    d_flat = (
        d_mixed.astype(jnp.float32)
        + back_product(d_query, w_query)
        + back_product(d_key, w_key)
        + back_product(d_value, w_value)
    )
    d_features = (tissue_f.reshape(-1, 1) * d_flat).astype(jnp.bfloat16)
    return (d_features, (g_query, g_key, g_value, g_out))


def slide_scores(region, att_v, att_u, att_w):
    tanh_part = jnp.tanh(precise(region, att_v))
    gate_part = jax.nn.sigmoid(precise(region, att_u))
    gated_act = tanh_part * gate_part
    return ((tanh_part, gate_part, gated_act), precise(gated_act, att_w))


def slide_backward(region, member, share, d_summary, summary, parts, att_v, att_u, att_w):
    tanh_part, gate_part, gated_act = parts
    d_own = precise(member, d_summary)
    own_summary = precise(member, summary)
    d_score = share * jnp.sum(d_own * (region - own_summary), axis=1)
    d_gated = d_score[:, None] * att_w[None, :]
    d_pre_v = d_gated * gate_part * (1.0 - tanh_part * tanh_part)
    d_pre_u = d_gated * tanh_part * gate_part * (1.0 - gate_part)
    d_region = share[:, None] * d_own + precise(d_pre_v, att_v.T) + precise(d_pre_u, att_u.T)
    g_att_v = precise(region.T, d_pre_v)
    g_att_u = precise(region.T, d_pre_u)
    g_att_w = precise(d_score, gated_act)
    return (d_region, (g_att_v, g_att_u, g_att_w))


def body(
    patches,
    tissue,
    region_slide,
    w_up,
    w_down,
    w_embed,
    w_query,
    w_key,
    w_value,
    w_out,
    att_v,
    att_u,
    att_w,
    w_class,
    g_logits,
):
    groups = lax.axis_size("grp")
    pos_local = patches.shape[1]
    per_dev = patches.shape[0] // groups
    width = w_embed.shape[1]
    grp_index = lax.axis_index("grp")
    dev_index = lax.axis_index("dev")
    first_row = (dev_index * groups + grp_index) * per_dev
    own_tissue = lax.dynamic_slice_in_dim(tissue, first_row, per_dev, 0).astype(jnp.float32)
    own_slide = lax.dynamic_slice_in_dim(region_slide, first_row, per_dev, 0)
    local_tissue = lax.dynamic_slice(
        tissue,
        (dev_index * (per_dev * groups), grp_index * pos_local),
        (per_dev * groups, pos_local),
    ).astype(jnp.float32)
    token_rows = patches.reshape(-1, D1)
    local_features, kept_patch = patch_forward(
        token_rows, local_tissue.reshape(-1), w_up, w_down, w_embed
    )
    features = lax.all_to_all(
        local_features.reshape(per_dev * groups, pos_local, width),
        "grp",
        split_axis=0,
        concat_axis=1,
        tiled=True,
    )
    region, kept_region = region_forward(features, own_tissue, w_query, w_key, w_value, w_out)
    member = (own_slide[:, None] == jnp.arange(SLIDES, dtype=jnp.int32)[None, :]).astype(
        jnp.float32
    )
    parts, region_score = slide_scores(region, att_v, att_u, att_w)
    weight = jnp.exp(region_score)
    local_total = precise(weight, member)
    local_sum = precise(member.T, weight[:, None] * region)
    slide_total, slide_sum = lax.psum((local_total, local_sum), ("grp", "dev"))
    summary = slide_sum / slide_total[:, None]
    logits = precise(summary, w_class)
    g_class = precise(summary.T, g_logits)
    d_summary = precise(g_logits, w_class.T)
    share = weight / precise(member, slide_total)
    d_region, slide_grads = slide_backward(
        region, member, share, d_summary, summary, parts, att_v, att_u, att_w
    )
    d_features, region_grads = region_backward(
        features, own_tissue, d_region, kept_region, w_query, w_key, w_value, w_out
    )
    returned = lax.all_to_all(
        d_features.reshape(per_dev, PATCH, width), "grp", split_axis=1, concat_axis=0, tiled=True
    )
    patch_grads = patch_backward(
        token_rows, kept_patch, returned.reshape(-1, width), w_down, w_embed
    )
    part_up, part_down, part_embed = patch_grads
    part_query, part_key, part_value, part_out = region_grads
    part_att_v, part_att_u, part_att_w = slide_grads
    summed = lax.psum(
        (
            part_up,
            part_down,
            part_embed,
            part_query,
            part_key,
            part_value,
            part_out,
            part_att_v,
            part_att_u,
            part_att_w,
        ),
        ("grp", "dev"),
    )
    g_up, g_down, g_embed, g_query, g_key, g_value, g_out, g_att_v, g_att_u, g_att_w = summed
    return (
        logits,
        g_up,
        g_down,
        g_embed,
        g_query,
        g_key,
        g_value,
        g_out,
        g_att_v,
        g_att_u,
        g_att_w,
        g_class,
    )


def solution(mesh):
    placed = (
        P("dev", "grp", None),
        P(),
        P(),
        P(),
        P(),
        P(),
        P(),
        P(),
        P(),
        P(),
        P(),
        P(),
        P(),
        P(),
        P(),
    )
    return jax.shard_map(
        body,
        mesh=mesh,
        in_specs=placed,
        out_specs=(P(), P(), P(), P(), P(), P(), P(), P(), P(), P(), P(), P()),
        check_vma=False,
    )
```

profile of v0, /device:TPU:1, one launch (start us, length us, event | category | flops | bytes accessed | tf_op | source)
XLA Modules:
  0.0 468.2 jit_solution(2516572465442675007)
XLA Ops:
  7.2 0.9 dynamic-slice_convert_fusion
  8.5 2.1 fusion.124
  10.6 1.2 fusion.30
  12.5 0.8 copy.67
  13.4 7.2 %all-to-all-start = ((bf16[32,16,192]{2,1,0:T(8,128)(2,1)}), bf16[32,16,192]{2,1,0:T(8,128)(2,1)S(1)}, u32[]{:S(2)}, u32[]{:S(2)}) async-start(bf16[32,16,192]{2,1,0:T(8,128)(2,1)} %bitcast.1), calls=%async_computation | async-start | bytes 524288 | tf_op jit(solution)/shard_map/all_to_all | solution.py:174
  20.5 0.8 fusion.112
  21.4 0.8 dynamic_slice.9
  23.5 0.8 fusion.84
  24.3 3.4 all-to-all-done
  28.9 2.9 fusion.113
  32.4 2.3 fusion.46
  35.4 1.0 multiply_reduce_fusion.2
  36.5 1.2 fusion.51
  37.7 1.2 fusion.122
  38.9 0.8 fusion.53
  39.7 0.9 convolution_bitcast_fusion.2
  40.6 0.9 fusion.81
  41.5 78.5 %all-reduce = (f32[4,192]{1,0:T(4,128)S(1)}, f32[4]{0:T(128)S(1)}) all-reduce(f32[4,192]{1,0:T(4,128)S(1)} %fusion.81, f32[4]{0:T(128)S(1)} %convolution_bitcast_fusion.2), channel_id=1, replica_groups=mesh['grp'=16,'dev'=16] {'grp','dev'}, use_global_device_ids=true, to_apply=%region_4.0 | all-reduce | flops 772 | bytes 6176 | tf_op jit(solution)/shard_map/psum | solution.py:189
  120.0 1.0 fusion.52
  121.0 0.9 fusion.123
  121.9 1.8 fusion.105
  123.7 1.2 convolution_add_fusion.6
  124.9 1.2 convolution_add_fusion.5
  126.7 0.7 copy-done.5
  127.4 1.1 convolution_convert_fusion.1
  128.6 3.1 fusion.47
  131.8 2.3 fusion.61
  134.1 6.5 %fusion.40 = bf16[2,256,6,32]{1,3,2,0:T(8,128)(2,1)} fusion(f32[2,6,256,256]{2,3,1,0:T(8,128)} %fusion.61, bf16[2,256,6,32]{1,0,3,2:T(2,128)(2,1)S(1)} %copy-done.12, f32[2,6,256,256]{2,3,1,0:T(8,128)} %get-tuple-element.62, f32[2,6,256]{2,1,0:T(8,128)S(1)} %copy-done.45), kind=kOutput, calls=%fused_computation.50 | convolution fusion | flops 55938304 | bytes 6696960 | tf_op jit(solution)/shard_map/nhqk,nqhd->nkhd/dot_general | solution.py:39
  140.6 5.8 %fusion.43 = bf16[2,256,6,32]{1,3,2,0:T(8,128)(2,1)S(1)} fusion(f32[2,6,256,256]{2,3,1,0:T(8,128)} %fusion.61, bf16[2,256,6,32]{1,0,3,2:T(2,128)(2,1)S(1)} %copy-done.14, f32[2,6,256,256]{2,3,1,0:T(8,128)} %get-tuple-element.62, f32[2,6,256]{2,1,0:T(8,128)S(1)} %copy-done.45), kind=kOutput, calls=%fused_computation.51 | convolution fusion | flops 55938304 | bytes 6696960 | tf_op jit(solution)/shard_map/nhqk,nkhd->nqhd/dot_general | solution.py:39
  146.8 1.1 copy.87
  148.0 1.1 copy.84
  149.4 1.3 convolution_add_fusion.3
  150.6 0.9 fusion.129
  151.8 0.9 fusion.130
  153.0 1.1 copy.88
  154.1 4.3 all-to-all-start.1
  158.5 0.9 fusion.131
  159.4 1.8 fusion.108
  161.2 0.9 fusion.128
  162.2 3.4 all-to-all-done.1
  165.9 1.0 fusion.127
  167.0 4.7 %fusion.111 = f32[1536,384]{1,0:T(8,128)} fusion(bf16[512,384]{1,0:T(8,128)(2,1)S(1)} %convolution_convert_fusion, f32[512,1536]{1,0:T(8,128)} %copy-done.1), kind=kOutput, calls=%fused_computation.126 | convolution fusion | flops 611057664 | bytes 5898240 | tf_op jit(solution)/shard_map/dot_general | solution.py:23
  171.7 6.4 %convolution_bitcast_fusion = f32[384,1536]{0,1:T(8,128)} fusion(bf16[512,384]{1,0:T(8,128)(2,1)S(1)} %bitcast.159, f32[512,1536]{1,0:T(8,128)} %copy-done.1, bf16[512,384]{1,0:T(8,128)(2,1)S(1)} %convolution_convert_fusion, bf16[1536,384]{1,0:T(8,128)(2,1)S(1)} %copy-done.42), kind=kOutput, calls=%fused_computation.16 | convolution fusion | flops 1223688192 | bytes 7471104 | tf_op jit(solution)/shard_map/dot_general | solution.py:23
  178.8 73.9 %psum.95 = f32[192]{0:T(256)} all-reduce(f32[192]{0:T(256)S(1)} %bitcast.177), channel_id=1, replica_groups=mesh['grp'=16,'dev'=16] {'grp','dev'}, use_global_device_ids=true, to_apply=%region_17.0 | all-reduce | flops 192 | bytes 1536 | tf_op jit(solution)/shard_map/psum | solution.py:210
  252.8 0.8 fusion.132
  254.3 197.7 %all-reduce.4.cloned.1.call-done = (f32[384,1536]{0,1:T(8,128)}, f32[1536,384]{1,0:T(8,128)}, f32[384,192]{0,1:T(8,128)}, f32[192,192]{1,0:T(8,128)}, f32[192,19...) async-done(((f32[384,1536]{0,1:T(8,128)}, f32[1536,384]{1,0:T(8,128)}, f32[384,192]{0,1:T(8,128)}, ...) | async-done | bytes 5898256 | tf_op jit(solution)/shard_map/psum | solution.py:210
  451.9 3.2 copy.92
  455.2 1.4 copy.149
  (139 shorter events, 13.3 us)
Async XLA Ops:
  7.2 1.3 copy-start
  8.5 2.1 copy-start.3
  8.5 2.1 copy-start.41
  10.6 1.6 copy-start.1
  10.6 1.6 copy-start.4
  10.6 12.8 %copy-start.30 = (f32[192,3]{0,1:T(4,128)S(1)}, f32[192,3]{0,1:T(4,128)}, u32[]{:S(2)}) copy-start(f32[192,3]{0,1:T(4,128)} %param.28) | copy-start | bytes 6916
  10.6 12.8 %copy-start.39 = (f32[4,3]{1,0:T(4,128)S(1)}, f32[4,3]{1,0:T(4,128)}, u32[]{:S(2)}) copy-start(f32[4,3]{1,0:T(4,128)} %param.29) | copy-start | bytes 148
  10.6 17.2 %copy-start.22 = (bf16[192,192]{1,0:T(8,128)(2,1)S(1)}, bf16[192,192]{1,0:T(8,128)(2,1)}, u32[]{:S(2)}) copy-start(bf16[192,192]{1,0:T(8,128)(2,1)} %param.21) | copy-start | bytes 221188
  12.2 16.0 %copy-start.6 = (bf16[192,192]{1,0:T(8,128)(2,1)S(1)}, bf16[192,192]{1,0:T(8,128)(2,1)}, u32[]{:S(2)}) copy-start(bf16[192,192]{1,0:T(8,128)(2,1)} %param.22) | copy-start | bytes 221188
  12.2 16.3 %copy-start.8 = (bf16[192,192]{1,0:T(8,128)(2,1)S(1)}, bf16[192,192]{1,0:T(8,128)(2,1)}, u32[]{:S(2)}) copy-start(bf16[192,192]{1,0:T(8,128)(2,1)} %param.23) | copy-start | bytes 221188
  13.4 14.3 %all-to-all-start = ((bf16[32,16,192]{2,1,0:T(8,128)(2,1)}), bf16[32,16,192]{2,1,0:T(8,128)(2,1)S(1)}, u32[]{:S(2)}, u32[]{:S(2)}) async-start(bf16[32,16,192]{2,1,0:T(8,128)(2,1)} %bitcast.1), calls=%async_computation | async-start | bytes 524288 | tf_op jit(solution)/shard_map/all_to_all | solution.py:174
  21.3 6.8 %copy-start.26 = (f32[2,256]{1,0:T(2,128)}, f32[2,256]{1,0:T(2,128)S(1)}, u32[]{:S(2)}) copy-start(f32[2,256]{1,0:T(2,128)S(1)} %get-tuple-element.60) | copy-start | bytes 6148
  21.4 6.8 %copy-start.28 = (f32[2]{0:T(128)}, f32[2]{0:T(128)S(1)}, u32[]{:S(2)}) copy-start(f32[2]{0:T(128)S(1)} %broadcast_maximum_fusion) | copy-start | bytes 28
  22.1 5.6 %copy-start.43 = (s32[2]{0:T(128)}, s32[2]{0:T(128)S(1)}, u32[]{:S(2)}) copy-start(s32[2]{0:T(128)S(1)} %dynamic_slice.9) | copy-start | bytes 28
  28.2 6.4 %copy-start.11 = (bf16[2,256,6,32]{1,0,3,2:T(2,128)(2,1)}, bf16[2,256,6,32]{1,0,3,2:T(2,128)(2,1)S(1)}, u32[]{:S(2)}) copy-start(bf16[2,256,6,32]{1,0,3,2:T(2,128)(2,1)S(1)} %reshape.150) | copy-start | bytes 589828
  28.6 6.1 %copy-start.13 = (bf16[2,256,6,32]{1,0,3,2:T(2,128)(2,1)}, bf16[2,256,6,32]{1,0,3,2:T(2,128)(2,1)S(1)}, u32[]{:S(2)}) copy-start(bf16[2,256,6,32]{1,0,3,2:T(2,128)(2,1)S(1)} %reshape.151) | copy-start | bytes 589828
  32.4 2.5 copy-start.21
  36.4 92.2 %copy-start.45 = (f32[2,6,256]{2,1,0:T(8,128)S(1)}, f32[2,6,256]{2,1,0:T(8,128)}, u32[]{:S(2)}) copy-start(f32[2,6,256]{2,1,0:T(8,128)} %copy-done.44) | copy-start | bytes 36868
  36.5 89.7 %copy-start.25 = (f32[2,192]{1,0:T(2,128)}, f32[2,192]{1,0:T(2,128)S(1)}, u32[]{:S(2)}) copy-start(f32[2,192]{1,0:T(2,128)S(1)} %copy.75) | copy-start | bytes 4612
  37.7 88.5 %copy-start.23 = (f32[2,192]{1,0:T(2,128)}, f32[2,192]{1,0:T(2,128)S(1)}, u32[]{:S(2)}) copy-start(f32[2,192]{1,0:T(2,128)S(1)} %fusion.51) | copy-start | bytes 4612
  38.9 0.8 copy-start.37
  38.9 87.3 %copy-start.24 = (f32[2,192]{1,0:T(2,128)}, f32[2,192]{1,0:T(2,128)S(1)}, u32[]{:S(2)}) copy-start(f32[2,192]{1,0:T(2,128)S(1)} %get-tuple-element.64) | copy-start | bytes 4612
  120.0 6.2 %copy-start.32 = (f32[4,192]{1,0:T(4,128)}, f32[4,192]{1,0:T(4,128)S(1)}, u32[]{:S(2)}) copy-start(f32[4,192]{1,0:T(4,128)S(1)} %broadcast_divide_fusion.1) | copy-start | bytes 9220
  121.9 4.3 copy-start.34
  126.7 0.7 copy-start.5
  131.8 2.3 copy-start.12
  134.1 6.5 %copy-start.14 = (bf16[2,256,6,32]{1,0,3,2:T(2,128)(2,1)S(1)}, bf16[2,256,6,32]{1,0,3,2:T(2,128)(2,1)}, u32[]{:S(2)}) copy-start(bf16[2,256,6,32]{1,0,3,2:T(2,128)(2,1)} %copy-done.13) | copy-start | bytes 589828
  140.6 5.9 %copy-start.27 = (f32[2,256]{1,0:T(2,128)S(1)}, f32[2,256]{1,0:T(2,128)}, u32[]{:S(2)}) copy-start(f32[2,256]{1,0:T(2,128)} %copy-done.26) | copy-start | bytes 6148
  140.6 5.9 %copy-start.29 = (f32[2]{0:T(128)S(1)}, f32[2]{0:T(128)}, u32[]{:S(2)}) copy-start(f32[2]{0:T(128)} %copy-done.28) | copy-start | bytes 28
  146.5 5.1 %copy-start.7 = (bf16[192,192]{1,0:T(8,128)(2,1)S(1)}, bf16[192,192]{1,0:T(8,128)(2,1)}, u32[]{:S(2)}) copy-start(bf16[192,192]{1,0:T(8,128)(2,1)} %param.22) | copy-start | bytes 221188
  147.9 4.8 %copy-start.9 = (bf16[192,192]{1,0:T(8,128)(2,1)S(1)}, bf16[192,192]{1,0:T(8,128)(2,1)}, u32[]{:S(2)}) copy-start(bf16[192,192]{1,0:T(8,128)(2,1)} %param.23) | copy-start | bytes 221188
  147.9 4.8 %copy-start.36 = (f32[1,2,2,128]{3,1,2,0:T(2,128)S(1)}, f32[1,2,2,128]{3,1,2,0:T(2,128)}, u32[]{:S(2)}) copy-start(f32[1,2,2,128]{3,1,2,0:T(2,128)} %copy.99) | copy-start | bytes 6148
  154.1 11.5 %all-to-all-start.1 = ((bf16[2,256,192]{2,0,1:T(2,128)(2,1)}), bf16[2,256,192]{2,0,1:T(2,128)(2,1)S(1)}, u32[]{:S(2)}, u32[]{:S(2)}) async-start(bf16[2,256,192]{2,0,1:T(2,128)(2,1)} %copy.88), calls=%async_computation.1 | async-start | bytes 524288 | tf_op jit(solution)/shard_map/all_to_all | solution.py:201
  158.4 293.5 %all-reduce.4.cloned.1.call-start = ((), (), s32[]{:S(2)}) async-start(), calls=%async_computation.2 | async-start | bytes 12386304 | tf_op jit(solution)/shard_map/psum | solution.py:210
  167.0 4.7 %copy-start.42 = (bf16[1536,384]{1,0:T(8,128)(2,1)S(1)}, bf16[1536,384]{1,0:T(8,128)(2,1)}, u32[]{:S(2)}) copy-start(bf16[1536,384]{1,0:T(8,128)(2,1)} %param.19) | copy-start | bytes 3538948
  178.0 0.6 copy-start.35
  178.0 0.7 copy-start.38
  178.0 74.7 %copy-start.33 = (f32[4,192]{1,0:T(4,128)S(1)}, f32[4,192]{1,0:T(4,128)}, u32[]{:S(2)}) copy-start(f32[4,192]{1,0:T(4,128)} %copy-done.32) | copy-start | bytes 9220
  178.0 74.7 %copy-start.40 = (f32[4,3]{1,0:T(4,128)S(1)}, f32[4,3]{1,0:T(4,128)}, u32[]{:S(2)}) copy-start(f32[4,3]{1,0:T(4,128)} %param.29) | copy-start | bytes 148
  178.0 75.5 %copy-start.31 = (f32[192,3]{0,1:T(4,128)S(1)}, f32[192,3]{0,1:T(4,128)}, u32[]{:S(2)}) copy-start(f32[192,3]{0,1:T(4,128)} %param.28) | copy-start | bytes 6916
  451.9 3.2 copy-start.2
  455.1 1.5 copy-start.10
  455.1 2.2 copy-start.20
  455.1 2.9 copy-start.19
  455.1 3.5 copy-start.18
  455.1 4.2 copy-start.17
  455.2 4.9 %copy-start.16 = (f32[192,192]{1,0:T(8,128)S(1)}, f32[192,192]{1,0:T(8,128)}, u32[]{:S(2)}) copy-start(f32[192,192]{1,0:T(8,128)} %get-tuple-element.75) | copy-start | bytes 442372
  455.2 5.5 %copy-start.15 = (f32[192,192]{1,0:T(8,128)S(1)}, f32[192,192]{1,0:T(8,128)}, u32[]{:S(2)}) copy-start(f32[192,192]{1,0:T(8,128)} %get-tuple-element.76) | copy-start | bytes 442372
  (1 other events, 0.6 us)
Sparse Core Ops, SparseCore 0:
  178.2 273.6 all-reduce.3
where the time goes:
time: 470 us; the launch traced here: 468 us
  waiting for transfers between devices  205 us (44%)
  blocking collectives  152 us (32%)
  matrix products  61.8 us (13%)
  local copies, waits for them, and re-layouts  20.3 us (4%)
  between operations  14.7 us (3%)
  starting transfers between devices  11.6 us (2%)
    psum x1, waiting for transfers between devices, body(): lax.psum((part_up, part_down, part_embed, part_query, part_key, part_valu...  198 us
    psum x1, blocking collectives, body(): slide_total, slide_sum = lax.psum((local_total, local_sum), ('grp', 'dev'))  78.5 us
    psum x1, blocking collectives, body(): lax.psum((part_up, part_down, part_embed, part_query, part_key, part_valu...  73.9 us
    dot_general x5, matrix products, mix_heads(): jnp.einsum(form, left_op, right_op, preferred_element_type=jnp.float32)  20.1 us
    dot_general x7, matrix products, gram_product(): lax.dot_general(left_op, right_op, (((0,), (0,)), ((), ())), preferred_el...  15.8 us
    dot_general x16, matrix products, precise(): jnp.dot(left_op, right_op, precision=HIGHEST, preferred_element_type=jnp....  15.4 us
    unnamed x110, local copies, waits for them, and re-layouts  13.6 us
  transfers between devices with their start and end apart: 3, of which 3 were waited for; matrix products, arithmetic and copies ran while one was open for 2% of the time, Pallas kernels for 0%

commit v1 on v0

v1 whole, which is shorter than its diff:
```python
import math

import jax
import jax.numpy as jnp
from jax import lax
from jax.experimental import pallas as pl
from jax.experimental.pallas import tpu as pltpu
from jax.sharding import Mesh, PartitionSpec as P

D1 = 384
F1 = 1536
HEADS = 6
HEAD_DIM = 32
D2 = 192
PATCH = 256
SLIDES = 4
GRP = 16
OWN = 2
SCALE = 1.0 / math.sqrt(HEAD_DIM)
GELU_C = math.sqrt(2.0 / math.pi)
GELU_A = 0.044715

BF = jnp.bfloat16
F32 = jnp.float32
HIGHEST = lax.Precision.HIGHEST
VMEM_LIMIT = 48 * 1024 * 1024

CHUNKS = 32
HALF = CHUNKS // 2
CH_ROWS = 384


def nn(a, b, precision=None):
    return jnp.dot(a, b, precision=precision, preferred_element_type=F32)


def nt(a, b, precision=None):
    return lax.dot_general(
        a, b, (((1,), (1,)), ((), ())), precision=precision, preferred_element_type=F32
    )


def tn(a, b, precision=None):
    return lax.dot_general(
        a, b, (((0,), (0,)), ((), ())), precision=precision, preferred_element_type=F32
    )


def params():
    return pltpu.CompilerParams(vmem_limit_bytes=VMEM_LIMIT)


def patch_forward_kernel(x_ref, wu_ref, wd_ref, we_ref, feat_ref, hid_ref, gp_ref, mid_ref, acc):
    step = pl.program_id(0)
    x = x_ref[...]
    pre = nn(x, wu_ref[...])
    sq = pre * pre
    t = jnp.tanh(GELU_C * (pre + GELU_A * (pre * sq)))
    half_up = 0.5 + 0.5 * t
    hid = (pre * half_up).astype(BF)
    hid_ref[...] = hid
    slope = (0.5 * GELU_C) * (1.0 - t * t) * (1.0 + (3.0 * GELU_A) * sq)
    gp_ref[...] = (half_up + pre * slope).astype(BF)
    part = nn(hid, wd_ref[...])

    @pl.when(step == 0)
    def _():
        acc[...] = x.astype(F32) + part

    @pl.when(step > 0)
    def _():
        acc[...] += part

    @pl.when(step == pl.num_programs(0) - 1)
    def _():
        mid = acc[...].astype(BF)
        mid_ref[...] = mid
        feat_ref[...] = nn(mid, we_ref[...]).astype(BF)


def patch_forward(tokens, w_up, w_down, w_embed):
    rows = tokens.shape[0]
    steps = 3
    fb = F1 // steps
    whole = lambda i: (0, 0)
    return pl.pallas_call(
        patch_forward_kernel,
        grid=(steps,),
        in_specs=[
            pl.BlockSpec((rows, D1), whole),
            pl.BlockSpec((D1, fb), lambda i: (0, i)),
            pl.BlockSpec((fb, D1), lambda i: (i, 0)),
            pl.BlockSpec((D1, D2), whole),
        ],
        out_specs=[
            pl.BlockSpec((rows, D2), whole),
            pl.BlockSpec((rows, fb), lambda i: (0, i)),
            pl.BlockSpec((rows, fb), lambda i: (0, i)),
            pl.BlockSpec((rows, D1), whole),
        ],
        out_shape=[
            jax.ShapeDtypeStruct((rows, D2), BF),
            jax.ShapeDtypeStruct((rows, F1), BF),
            jax.ShapeDtypeStruct((rows, F1), BF),
            jax.ShapeDtypeStruct((rows, D1), BF),
        ],
        scratch_shapes=[pltpu.VMEM((rows, D1), F32)],
        compiler_params=params(),
        name="patch_forward",
    )(tokens, w_up, w_down, w_embed)


def tissue_row(idx_ref, tis_ref, r):
    return tis_ref[pl.ds(idx_ref[1] + r, 1), :].astype(F32)


def column_of(row, width):
    return jnp.broadcast_to(row, (PATCH, row.shape[1])).T[:, :width]


def head_mask(h, shape, dim):
    return (lax.broadcasted_iota(jnp.int32, shape, dim) // HEAD_DIM == h).astype(F32)


def region_forward_kernel(
    idx_ref, slide_ref, f_ref, tis_ref, wq_ref, wk_ref, wv_ref, wo_ref, av_ref, au_ref, aw_ref,
    p_ref, x_ref, q_ref, k_ref, v_ref, se_ref, asum_ref, reg_ref, tanh_ref, gate_ref, w_ref,
    part_ref,
):
    r = pl.program_id(0)
    trow = tissue_row(idx_ref, tis_ref, r)
    tcol = column_of(trow, D2)
    x = (f_ref[...].reshape(PATCH, D2).astype(F32) * tcol).astype(BF)
    x_ref[0] = x
    q = nn(x, wq_ref[...]).astype(BF)
    k = nn(x, wk_ref[...])
    v = nn(x, wv_ref[...]).astype(BF)
    q_ref[0] = q
    k_ref[0] = k.astype(BF)
    v_ref[0] = v
    spread = jnp.zeros((PATCH, D2), F32)
    for h in range(HEADS):
        mask = head_mask(h, (1, D2), 1)
        st = nt((k * mask).astype(BF), q) * SCALE
        top = jnp.max(st, axis=0, keepdims=True)
        ex = jnp.exp(st - top)
        total = jnp.sum(ex, axis=0, keepdims=True)
        pb = (ex * (1.0 / total)).astype(BF)
        p_ref[0, pl.ds(h * PATCH, PATCH), :] = pb
        spread = spread + nn(pb, (tcol * mask).astype(BF))
    se_ref[0] = spread
    asum = jnp.sum(spread * v.astype(F32), axis=0, keepdims=True)
    xsum = jnp.sum(x.astype(F32), axis=0, keepdims=True)
    count = jnp.maximum(jnp.sum(trow, axis=1, keepdims=True), 1.0)
    mixed = xsum + nn(jnp.broadcast_to(asum, (8, D2)), wo_ref[...].astype(F32), HIGHEST)[0:1]

    @pl.when(r == 0)
    def _():
        lane = lax.broadcasted_iota(jnp.int32, (8, PATCH), 1)
        reg_ref[...] = jnp.where(lane < D2, 0.0, 1.0)
        asum_ref[...] = jnp.zeros_like(asum_ref)

    asum_ref[pl.ds(r, 1), :] = asum
    reg_ref[pl.ds(r, 1), pl.ds(0, D2)] = mixed / count

    @pl.when(r == OWN - 1)
    def _():
        region = reg_ref[:, pl.ds(0, D2)]
        tanh_part = jnp.tanh(nn(region, av_ref[...], HIGHEST))
        gate_part = jax.nn.sigmoid(nn(region, au_ref[...], HIGHEST))
        tanh_ref[...] = tanh_part
        gate_ref[...] = gate_part
        score = jnp.sum(tanh_part * gate_part * aw_ref[...], axis=1, keepdims=True)
        weight = jnp.exp(score)
        w_ref[...] = jnp.broadcast_to(weight, w_ref.shape)
        wide = reg_ref[...] * weight
        slot = lax.broadcasted_iota(jnp.int32, (SLIDES, 1), 0)
        sums = jnp.zeros((SLIDES, PATCH), F32)
        for i in range(OWN):
            own = (slot == slide_ref[idx_ref[0] + i]).astype(F32)
            sums = sums + own * wide[i : i + 1]
        both = jnp.concatenate([sums[:, :128], sums[:, 128:]], axis=0)
        part_ref[...] = jnp.broadcast_to(both[None], part_ref.shape)


def region_forward(idx, slide, got, tissue, w_query, w_key, w_value, w_out, att_v, att_u, att_w):
    sq = pl.BlockSpec((D2, D2), lambda r, *_: (0, 0))
    row8 = lambda width: pl.BlockSpec((8, width), lambda r, *_: (0, 0))
    per_region = lambda rows, width: pl.BlockSpec((1, rows, width), lambda r, *_: (r, 0, 0))
    tok = lambda dt: jax.ShapeDtypeStruct((OWN, PATCH, D2), dt)
    return pl.pallas_call(
        region_forward_kernel,
        grid_spec=pltpu.PrefetchScalarGridSpec(
            num_scalar_prefetch=2,
            grid=(OWN,),
            in_specs=[
                pl.BlockSpec((GRP, 1, PATCH // GRP, D2), lambda r, *_: (0, r, 0, 0)),
                pl.BlockSpec((8, PATCH), lambda r, idx, _: (idx[2], 0)),
                sq, sq, sq, sq, sq, sq,
                pl.BlockSpec((1, D2), lambda r, *_: (0, 0)),
            ],
            out_specs=[
                per_region(HEADS * PATCH, PATCH),
                per_region(PATCH, D2),
                per_region(PATCH, D2),
                per_region(PATCH, D2),
                per_region(PATCH, D2),
                per_region(PATCH, D2),
                row8(D2),
                row8(PATCH),
                row8(D2),
                row8(D2),
                row8(128),
                pl.BlockSpec((CHUNKS, 8, 128), lambda r, *_: (0, 0, 0)),
            ],
        ),
        out_shape=[
            jax.ShapeDtypeStruct((OWN, HEADS * PATCH, PATCH), BF),
            tok(BF), tok(BF), tok(BF), tok(BF), tok(F32),
            jax.ShapeDtypeStruct((8, D2), F32),
            jax.ShapeDtypeStruct((8, PATCH), F32),
            jax.ShapeDtypeStruct((8, D2), F32),
            jax.ShapeDtypeStruct((8, D2), F32),
            jax.ShapeDtypeStruct((8, 128), F32),
            jax.ShapeDtypeStruct((CHUNKS, 8, 128), F32),
        ],
        compiler_params=params(),
        name="region_forward",
    )(idx, slide, got, tissue, w_query, w_key, w_value, w_out, att_v, att_u, att_w)


def region_backward_kernel(
    idx_ref, slide_ref, z_ref, tis_ref, wq_ref, wk_ref, wv_ref, wo_ref, av_ref, au_ref, aw_ref,
    wc_ref, gl_ref,
    p_ref, x_ref, q_ref, k_ref, v_ref, se_ref, asum_ref, reg_ref, tanh_ref, gate_ref, w_ref,
    df_ref, rest_ref, logits_ref, gc_ref,
    dm_s, da_s, kt_s, dqt_s, gq_s, gk_s, gv_s,
):
    r = pl.program_id(0)
    trow = tissue_row(idx_ref, tis_ref, r)
    tcol = column_of(trow, D2)

    def put(slot, grad, fill=None):
        low = 2 * D2 * slot
        rest_ref[pl.ds(low, D2), :] = grad[:, :128].astype(BF)
        if fill is None:
            fill = jnp.zeros((D2, 64), F32)
        high = jnp.concatenate([grad[:, 128:], fill], axis=1)
        rest_ref[pl.ds(low + D2, D2), :] = high.astype(BF)

    @pl.when(r == 0)
    def _():
        z = jnp.sum(z_ref[...], axis=0)
        low, high = z[0:SLIDES], z[SLIDES:]
        total = high[:, 64:65]
        summary = jnp.concatenate([low, high[:, :64]], axis=1) / total
        wc = wc_ref[...]
        gl = gl_ref[...]
        logits_ref[...] = nn(summary, wc, HIGHEST)
        gc_ref[...] = tn(summary, gl, HIGHEST)
        d_summary = nt(gl, wc, HIGHEST)
        slot = lax.broadcasted_iota(jnp.int32, (SLIDES, 1), 0)
        row = lax.broadcasted_iota(jnp.int32, (8, 1), 0)
        d_own = jnp.zeros((8, D2), F32)
        own_summary = jnp.zeros((8, D2), F32)
        own_total = jnp.ones((8, 1), F32)
        count = jnp.ones((8, 1), F32)
        for i in range(OWN):
            mine = slot == slide_ref[idx_ref[0] + i]
            pick = lambda a: jnp.sum(jnp.where(mine, a, 0.0), axis=0, keepdims=True)
            d_own = jnp.where(row == i, pick(d_summary), d_own)
            own_summary = jnp.where(row == i, pick(summary), own_summary)
            own_total = jnp.where(row == i, pick(total), own_total)
            t_i = tissue_row(idx_ref, tis_ref, i)
            count = jnp.where(
                row == i, jnp.maximum(jnp.sum(t_i, axis=1, keepdims=True), 1.0), count
            )
        region = reg_ref[:, pl.ds(0, D2)]
        tanh_part = tanh_ref[...]
        gate_part = gate_ref[...]
        share = jnp.where(row < OWN, w_ref[:, 0:1] / own_total, 0.0)
        d_score = share * jnp.sum(d_own * (region - own_summary), axis=1, keepdims=True)
        d_gated = d_score * aw_ref[...]
        d_pre_v = d_gated * gate_part * (1.0 - tanh_part * tanh_part)
        d_pre_u = d_gated * tanh_part * gate_part * (1.0 - gate_part)
        d_region = (
            share * d_own + nt(d_pre_v, av_ref[...], HIGHEST) + nt(d_pre_u, au_ref[...], HIGHEST)
        )
        dm = (d_region / count).astype(BF)
        dm_s[...] = dm.astype(F32)
        da_s[...] = nt(dm, wo_ref[...])
        put(3, tn(asum_ref[...], dm.astype(F32), HIGHEST))
        put(4, tn(region, d_pre_v, HIGHEST))
        put(
            5,
            tn(region, d_pre_u, HIGHEST),
            tn(tanh_part * gate_part, jnp.broadcast_to(d_score, (8, 64)), HIGHEST),
        )
        gq_s[...] = jnp.zeros_like(gq_s)
        gk_s[...] = jnp.zeros_like(gk_s)
        gv_s[...] = jnp.zeros_like(gv_s)

    x = x_ref[0]
    q = q_ref[0].astype(F32)
    v = v_ref[0]
    kt_s[...] = k_ref[0].astype(F32).T.astype(BF)
    dm = dm_s[pl.ds(r, 1), :]
    da = da_s[pl.ds(r, 1), :].astype(BF).astype(F32)
    da_col = jnp.broadcast_to(da, (128, D2)).T
    dk = jnp.zeros((PATCH, D2), F32)
    for h in range(HEADS):
        one_head = (da_col * head_mask(h, (D2, 1), 0)).astype(BF)
        e = nn(v, one_head)
        e = jnp.concatenate([e, e], axis=1)
        pt = p_ref[0, pl.ds(h * PATCH, PATCH), :].astype(F32)
        pe = pt * e
        ds = (pe - pt * jnp.sum(pe, axis=0, keepdims=True)).astype(BF)
        dk = dk + nn(ds, (q * head_mask(h, (1, D2), 1)).astype(BF))
        dqt_s[pl.ds(h * HEAD_DIM, HEAD_DIM), :] = nn(kt_s[pl.ds(h * HEAD_DIM, HEAD_DIM), :], ds)
    dq = (dqt_s[...] * (trow * SCALE)).T.astype(BF)
    dk = (dk * SCALE).astype(BF)
    dv = (se_ref[0] * da).astype(BF)
    xt = x.astype(F32).T.astype(BF)
    gq_s[...] += nn(xt, dq)
    gk_s[...] += nn(xt, dk)
    gv_s[...] += nn(xt, dv)
    d_flat = dm + nt(dq, wq_ref[...]) + nt(dk, wk_ref[...]) + nt(dv, wv_ref[...])
    df_ref[...] = (tcol * d_flat).astype(BF).reshape(df_ref.shape)

    @pl.when(r == OWN - 1)
    def _():
        put(0, gq_s[...])
        put(1, gk_s[...])
        put(2, gv_s[...])


def region_backward(idx, slide, z, tissue, weights, kept):
    sq = pl.BlockSpec((D2, D2), lambda r, *_: (0, 0))
    row8 = lambda width: pl.BlockSpec((8, width), lambda r, *_: (0, 0))
    per_region = lambda rows, width: pl.BlockSpec((1, rows, width), lambda r, *_: (r, 0, 0))
    return pl.pallas_call(
        region_backward_kernel,
        grid_spec=pltpu.PrefetchScalarGridSpec(
            num_scalar_prefetch=2,
            grid=(OWN,),
            in_specs=[
                pl.BlockSpec((8, 8, 128), lambda r, *_: (0, 0, 0)),
                pl.BlockSpec((8, PATCH), lambda r, idx, _: (idx[2], 0)),
                sq, sq, sq, sq, sq, sq,
                pl.BlockSpec((1, D2), lambda r, *_: (0, 0)),
                pl.BlockSpec((D2, 3), lambda r, *_: (0, 0)),
                pl.BlockSpec((SLIDES, 3), lambda r, *_: (0, 0)),
                per_region(HEADS * PATCH, PATCH),
                per_region(PATCH, D2),
                per_region(PATCH, D2),
                per_region(PATCH, D2),
                per_region(PATCH, D2),
                per_region(PATCH, D2),
                row8(D2),
                row8(PATCH),
                row8(D2),
                row8(D2),
                row8(128),
            ],
            out_specs=[
                pl.BlockSpec((GRP, 1, PATCH // GRP, D2), lambda r, *_: (0, r, 0, 0)),
                pl.BlockSpec((12 * D2, 128), lambda r, *_: (0, 0)),
                pl.BlockSpec((SLIDES, 3), lambda r, *_: (0, 0)),
                pl.BlockSpec((D2, 3), lambda r, *_: (0, 0)),
            ],
            scratch_shapes=[
                pltpu.VMEM((8, D2), F32),
                pltpu.VMEM((8, D2), F32),
                pltpu.VMEM((D2, PATCH), BF),
                pltpu.VMEM((D2, PATCH), F32),
                pltpu.VMEM((D2, D2), F32),
                pltpu.VMEM((D2, D2), F32),
                pltpu.VMEM((D2, D2), F32),
            ],
        ),
        out_shape=[
            jax.ShapeDtypeStruct((GRP, OWN, PATCH // GRP, D2), BF),
            jax.ShapeDtypeStruct((12 * D2, 128), BF),
            jax.ShapeDtypeStruct((SLIDES, 3), F32),
            jax.ShapeDtypeStruct((D2, 3), F32),
        ],
        compiler_params=params(),
        name="region_backward",
    )(idx, slide, z, tissue, *weights, *kept)


STEPS4 = 4
FB4 = F1 // STEPS4


def patch_backward_kernel(
    idx_ref, df_ref, x_ref, mid_ref, hid_ref, gp_ref, we_ref, wd_ref, rest_ref,
    mine_ref, other_ref,
    pack, dmid_s, sems,
):
    step = pl.program_id(0)

    @pl.when(step == 0)
    def _():
        df = df_ref[...]
        dmid_s[...] = nt(df, we_ref[...]).astype(BF)
        g_embed = tn(mid_ref[...], df)
        for j in range(24):
            pack[j, pl.ds(288, 96), :] = rest_ref[pl.ds(96 * j, 96), :]
        high = jnp.concatenate([g_embed[:, 128:], jnp.zeros((D1, 64), F32)], axis=1)
        for j in range(4):
            pack[24 + j, pl.ds(288, 96), :] = g_embed[96 * j : 96 * j + 96, :128].astype(BF)
            pack[28 + j, pl.ds(288, 96), :] = high[96 * j : 96 * j + 96].astype(BF)

    dmid = dmid_s[...]
    d_pre = (nt(dmid, wd_ref[...]) * gp_ref[...].astype(F32)).astype(BF)
    g_down = tn(hid_ref[...], dmid).astype(BF)
    g_up = tn(x_ref[...], d_pre).astype(BF)
    for j in range(8):
        for l in range(3):
            block = g_up[48 * j : 48 * j + 48, 128 * l : 128 * l + 128]
            pack[4 * j + step, pl.ds(48 * l, 48), :] = block
            block = g_down[48 * j : 48 * j + 48, 128 * l : 128 * l + 128]
            pack[8 * step + j, pl.ds(144 + 48 * l, 48), :] = block

    @pl.when(step == pl.num_programs(0) - 1)
    def _():
        core = idx_ref[3]
        keep = pltpu.make_async_copy(pack.at[pl.ds(core * HALF, HALF)], mine_ref, sems.at[0])
        send = pltpu.make_async_copy(
            pack.at[pl.ds((1 - core) * HALF, HALF)], other_ref, sems.at[1]
        )
        send.start()
        keep.start()
        send.wait()
        keep.wait()


def patch_backward(idx, df, tokens, mid, hid, gp, w_embed, w_down, rest):
    rows = tokens.shape[0]
    whole = lambda i, *_: (0, 0)
    return pl.pallas_call(
        patch_backward_kernel,
        grid_spec=pltpu.PrefetchScalarGridSpec(
            num_scalar_prefetch=1,
            grid=(STEPS4,),
            in_specs=[
                pl.BlockSpec((rows, D2), whole),
                pl.BlockSpec((rows, D1), whole),
                pl.BlockSpec((rows, D1), whole),
                pl.BlockSpec((rows, FB4), lambda i, *_: (0, i)),
                pl.BlockSpec((rows, FB4), lambda i, *_: (0, i)),
                pl.BlockSpec((D1, D2), whole),
                pl.BlockSpec((FB4, D1), lambda i, *_: (i, 0)),
                pl.BlockSpec((12 * D2, 128), whole),
            ],
            out_specs=[
                pl.BlockSpec(memory_space=pl.ANY),
                pl.BlockSpec(memory_space=pl.ANY),
            ],
            scratch_shapes=[
                pltpu.VMEM((CHUNKS, CH_ROWS, 128), BF),
                pltpu.VMEM((rows, D1), BF),
                pltpu.SemaphoreType.DMA((2,)),
            ],
        ),
        out_shape=[
            jax.ShapeDtypeStruct((HALF, CH_ROWS, 128), BF),
            jax.ShapeDtypeStruct((HALF, CH_ROWS, 128), BF),
        ],
        compiler_params=params(),
        name="patch_backward",
    )(idx, df, tokens, mid, hid, gp, w_embed, w_down, rest)


def unpack_kernel(
    idx_ref, mine_ref, other_ref,
    up_ref, down_ref, embed_ref, q_ref, k_ref, v_ref, o_ref, av_ref, au_ref, aw_ref,
    pack, sems,
):
    core = idx_ref[3]
    keep = pltpu.make_async_copy(mine_ref, pack.at[pl.ds(core * HALF, HALF)], sems.at[0])
    got = pltpu.make_async_copy(other_ref, pack.at[pl.ds((1 - core) * HALF, HALF)], sems.at[1])
    keep.start()
    got.start()
    keep.wait()
    got.wait()
    for j in range(CHUNKS):
        for l in range(3):
            lanes = pl.ds(384 * (j % 4) + 128 * l, 128)
            up_ref[pl.ds(48 * (j // 4), 48), lanes] = pack[j, pl.ds(48 * l, 48), :].astype(F32)
            lanes = pl.ds(128 * l, 128)
            down_ref[pl.ds(48 * j, 48), lanes] = pack[j, pl.ds(144 + 48 * l, 48), :].astype(F32)
    for slot, ref in enumerate((q_ref, k_ref, v_ref, o_ref, av_ref, au_ref)):
        for i in range(2):
            rows = pl.ds(96 * i, 96)
            ref[rows, pl.ds(0, 128)] = pack[4 * slot + i, pl.ds(288, 96), :].astype(F32)
            ref[rows, pl.ds(128, 64)] = pack[4 * slot + 2 + i, pl.ds(288, 96), :][:, :64].astype(F32)
    tail = jnp.concatenate(
        [pack[22, pl.ds(288, 96), :].astype(F32), pack[23, pl.ds(288, 96), :].astype(F32)], axis=0
    )
    aw_ref[...] = tail.T[64:65, :]
    for i in range(4):
        rows = pl.ds(96 * i, 96)
        embed_ref[rows, pl.ds(0, 128)] = pack[24 + i, pl.ds(288, 96), :].astype(F32)
        embed_ref[rows, pl.ds(128, 64)] = pack[28 + i, pl.ds(288, 96), :][:, :64].astype(F32)


def unpack(idx, mine, other):
    square = jax.ShapeDtypeStruct((D2, D2), F32)
    vm = pl.BlockSpec(memory_space=pltpu.VMEM)
    return pl.pallas_call(
        unpack_kernel,
        in_specs=[
            pl.BlockSpec(memory_space=pltpu.SMEM),
            pl.BlockSpec(memory_space=pl.ANY),
            pl.BlockSpec(memory_space=pl.ANY),
        ],
        out_specs=[vm] * 10,
        out_shape=[
            jax.ShapeDtypeStruct((D1, F1), F32),
            jax.ShapeDtypeStruct((F1, D1), F32),
            jax.ShapeDtypeStruct((D1, D2), F32),
            square, square, square, square, square, square,
            jax.ShapeDtypeStruct((1, D2), F32),
        ],
        scratch_shapes=[
            pltpu.VMEM((CHUNKS, CH_ROWS, 128), BF),
            pltpu.SemaphoreType.DMA((2,)),
        ],
        compiler_params=params(),
        name="unpack",
    )(idx, mine, other)


GRP_AXES = ("zl", "x", "c")
DEV_AXES = ("zh", "y")
XY = ("y", "x")
XYC = ("y", "x", "c")
Z = ("zh", "zl")


def exchange(x, axes):
    return lax.all_to_all(x, axes, split_axis=0, concat_axis=0, tiled=True)


def swap_cores(x):
    return lax.ppermute(x, "c", [(0, 1), (1, 0)])


def spread(x, n):
    return jnp.broadcast_to(x[None], (n,) + x.shape)


def add_up(x):
    return jnp.sum(x.astype(F32), axis=0).astype(x.dtype)


def body(
    patches, tissue, region_slide, w_up, w_down, w_embed, w_query, w_key, w_value, w_out,
    att_v, att_u, att_w, w_class, g_logits,
):
    grp = lax.axis_index(GRP_AXES)
    dev = lax.axis_index(DEV_AXES)
    core = lax.axis_index("c")
    first = (dev * GRP + grp) * OWN
    idx = jnp.stack([first, first % 8, first // 8, core]).astype(jnp.int32)
    tokens = patches.reshape(-1, D1)
    att_row = att_w.reshape(1, D2)
    feat, hid, gp, mid = patch_forward(tokens, w_up, w_down, w_embed)
    got = exchange(feat.reshape(GRP, -1, D2), GRP_AXES)
    got = got.reshape(GRP, OWN, PATCH // GRP, D2)
    *kept, part = region_forward(
        idx, region_slide, got, tissue, w_query, w_key, w_value, w_out, att_v, att_u, att_row
    )
    z = add_up(exchange(part, XYC))
    z = exchange(spread(z, 8), Z)
    df, rest, logits, g_class = region_backward(
        idx, region_slide, z, tissue,
        (w_query, w_key, w_value, w_out, att_v, att_u, att_row, w_class, g_logits), kept,
    )
    back = exchange(df.reshape(GRP, -1, D2), GRP_AXES).reshape(-1, D2)
    mine, other = patch_backward(idx, back, tokens, mid, hid, gp, w_embed, w_down, rest)
    half = (mine.astype(F32) + swap_cores(other).astype(F32)).astype(BF)
    chunk = add_up(exchange(half, XY))
    piece = add_up(exchange(chunk.reshape(8, CH_ROWS // 8, 128), Z))
    chunk = exchange(spread(piece, 8), Z).reshape(CH_ROWS, 128)
    half = exchange(spread(chunk, HALF), XY)
    up, down, embed, query, key, value, out, gv, gu, gw = unpack(idx, half, swap_cores(half))
    return (
        logits, up, down, embed, query, key, value, out, gv, gu, gw.reshape(D2), g_class,
    )


def solution(mesh):
    fine = Mesh(mesh.devices.reshape(2, 4, 2, 4, 4), GRP_AXES + DEV_AXES)
    placed = (P(DEV_AXES, GRP_AXES, None),) + (P(),) * 14
    return jax.shard_map(
        body,
        mesh=fine,
        in_specs=placed,
        out_specs=(P(),) * 12,
        check_vma=False,
    )
```

time: 470 us -> 184 us (0.39)
  waiting for transfers between devices: 205 us -> 18.7 us
  matrix products: 61.8 us -> 0 us
  blocking collectives: 152 us -> 92.1 us
  Pallas kernels: 0 us -> 27 us
  between operations: 14.7 us -> 0.82 us
  starting transfers between devices: 11.6 us -> 20.3 us
    psum x1 -> x0, waiting for transfers between devices: 198 us -> none  [body(): lax.psum((part_up, part_down, part_embed, part_query, part_key, part_valu...]
    psum x2 -> x0, blocking collectives: 152 us -> none  [the longest x1 78.5 us: body(): slide_total, slide_sum = lax.psum((local_total, local_sum), ('grp', 'dev'))]
    all_to_all x0 -> x6, blocking collectives: none -> 92.1 us  [exchange(): return lax.all_to_all(x, axes, split_axis=0, concat_axis=0, tiled=True)]
    dot_general x40 -> x0, matrix products: 58.9 us -> none  [the longest x5 20.1 us: mix_heads(): jnp.einsum(form, left_op, right_op, preferred_element_type=jnp.float32)]
    pallas_call x0 -> x5, Pallas kernels: none -> 27 us  [the longest x1 8.26 us: region_backward(): pl.pallas_call(region_backward_kernel, grid_spec=pltpu.PrefetchScalarGrid...]
    unnamed x110 -> x72, local copies, waits for them, and re-layouts: 13.6 us -> 22.7 us
    all_to_all x2, waiting for transfers between devices: 6.84 us -> 13.3 us  [exchange(): return lax.all_to_all(x, axes, split_axis=0, concat_axis=0, tiled=True)]
    ppermute x0 -> x2, starting transfers between devices: none -> 5.67 us  [swap_cores(): return lax.ppermute(x, 'c', [(0, 1), (1, 0)])]
  transfers between devices with their start and end apart: 3 -> 4, of which waited for: 3 -> 4; matrix products, arithmetic and copies ran while one was open for 2% -> 1% of each run, Pallas kernels for 0% -> 0%
where the time goes in v1:
time: 184 us; the launch traced here: 183 us
  blocking collectives  92.1 us (50%)
  Pallas kernels  27 us (15%)
  local copies, waits for them, and re-layouts  23.7 us (13%)
  starting transfers between devices  20.3 us (11%)
  waiting for transfers between devices  18.7 us (10%)
    all_to_all x6, blocking collectives, exchange(): return lax.all_to_all(x, axes, split_axis=0, concat_axis=0, tiled=True)  92.1 us
    unnamed x72, local copies, waits for them, and re-layouts  22.7 us
    all_to_all x2, starting transfers between devices, exchange(): return lax.all_to_all(x, axes, split_axis=0, concat_axis=0, tiled=True)  14.6 us
    all_to_all x2, waiting for transfers between devices, exchange(): return lax.all_to_all(x, axes, split_axis=0, concat_axis=0, tiled=True)  13.3 us
    pallas_call x1, Pallas kernels, region_backward(): pl.pallas_call(region_backward_kernel, grid_spec=pltpu.PrefetchScalarGrid...  8.26 us
    pallas_call x1, Pallas kernels, patch_backward(): pl.pallas_call(patch_backward_kernel, grid_spec=pltpu.PrefetchScalarGridS...  6.06 us
    ppermute x2, starting transfers between devices, swap_cores(): return lax.ppermute(x, 'c', [(0, 1), (1, 0)])  5.67 us
    ppermute x2, waiting for transfers between devices, swap_cores(): return lax.ppermute(x, 'c', [(0, 1), (1, 0)])  5.4 us
  transfers between devices with their start and end apart: 4, of which 4 were waited for; matrix products, arithmetic and copies ran while one was open for 1% of the time, Pallas kernels for 0%

profile of v1, /device:TPU:1, one launch (start us, length us, event | category | flops | bytes accessed | tf_op | source)
XLA Modules:
  0.0 183.3 jit_solution(7897611788508047752)
XLA Ops:
  0.6 1.0 copy.32.we_ref
  1.7 1.3 copy-done
  3.0 1.0 copy-done.4
  4.0 1.3 copy-done.6
  5.3 5.0 %patch_forward.1 = (bf16[512,192]{1,0:T(8,128)(2,1)}, bf16[512,1536]{1,0:T(8,128)(2,1)S(1)}, bf16[512,1536]{1,0:T(8,128)(2,1)}, bf16[512,384]{1,0:T(8,128)(2,1)S(1)}) custom-call(bf16[512,384]{1,0:T(8,128)(2,1)S(1)} %bitcast.13, bf16[384,1536]{1,0:T(8,128)(2,1)S(1)} %copy-done.6, bf16[1536,384]{1,0:T(8,128)(2,1)S(1)} %copy-done, ...), custom_call_target="tpu_custom_call" | custom-call | tf_op jit(solution)/shard_map/patch_forward/pallas_call | solution.py:86
  10.3 1.1 copy-done.3
  11.4 7.3 %all-to-all-start = ((bf16[16,32,192]{2,1,0:T(8,128)(2,1)}), bf16[16,32,192]{2,1,0:T(8,128)(2,1)S(1)}, u32[]{:S(2)}, u32[]{:S(2)}) async-start(bf16[16,32,192]{2,1,0:T(8,128)(2,1)} %bitcast.5), calls=%async_computation | async-start | bytes 524288 | tf_op jit(solution)/shard_map/all_to_all | solution.py:544
  18.8 7.1 %all-to-all-done = bf16[16,32,192]{2,1,0:T(8,128)(2,1)S(1)} async-done(((bf16[16,32,192]{2,1,0:T(8,128)(2,1)}), bf16[16,32,192]{2,1,0:T(8,128)(2,1)S(1)}, u32[]{:S(2)}, u32[]{:S(2)}) %all-to-all-start) | async-done | bytes 196640 | tf_op jit(solution)/shard_map/all_to_all | solution.py:544
  26.0 0.9 copy-done.11
  26.9 0.9 copy-done.13
  27.7 0.9 copy-done.15
  28.6 0.9 copy-done.17
  29.5 4.2 %region_forward.1 = (bf16[2,1536,256]{2,1,0:T(8,128)(2,1)S(1)}, bf16[2,256,192]{2,1,0:T(8,128)(2,1)S(1)}, bf16[2,256,192]{2,1,0:T(8,128)(2,1)S(1)}, bf16[2,256,1...) custom-call(s32[4]{0:T(128)S(1)} %pad_add_fusion.idx_ref, ...), custom_call_target="tpu_custom_call" | custom-call | tf_op jit(solution)/shard_map/region_forward/pallas_call | solution.py:191
  33.7 0.7 copy-done.20
  34.4 0.7 copy-done.22
  35.1 0.7 copy-done.24
  35.8 0.7 copy-done.26
  36.5 13.4 %all_to_all.40 = f32[32,8,128]{2,1,0:T(8,128)S(1)} all-to-all(f32[32,8,128]{2,1,0:T(8,128)S(1)} %get-tuple-element.45), channel_id=1, replica_groups=mesh['zl'=2,'x'=4,'c'=2,'zh'=4,'y'=4] {'y','x','c'}, dimensions={0} | all-to-all | bytes 262144 | tf_op jit(solution)/shard_map/all_to_all | solution.py:544
  50.0 0.6 broadcast_in_dim.8
  50.6 7.3 %all-to-all-start.2 = ((f32[8,8,128]{2,1,0:T(8,128)}), f32[8,8,128]{2,1,0:T(8,128)S(1)}, u32[]{:S(2)}, u32[]{:S(2)}) async-start(f32[8,8,128]{2,1,0:T(8,128)} %broadcast_in_dim.8), calls=%async_computation.2 | async-start | bytes 65536 | tf_op jit(solution)/shard_map/all_to_all | solution.py:544
  57.9 0.8 copy.33.wc_ref
  58.7 6.2 %all-to-all-done.2.z_ref = f32[8,8,128]{2,1,0:T(8,128)S(1)} async-done(((f32[8,8,128]{2,1,0:T(8,128)}), f32[8,8,128]{2,1,0:T(8,128)S(1)}, u32[]{:S(2)}, u32[]{:S(2)}) %all-to-all-start.2) | async-done | bytes 32800 | tf_op jit(solution)/shard_map/all_to_all | solution.py:544
  64.9 0.9 copy-done.12
  65.8 0.9 copy-done.14
  66.7 0.9 copy-done.16
  67.6 0.9 copy-done.18
  68.5 0.9 copy-done.19
  69.4 0.9 copy-done.21
  70.3 0.9 copy-done.23
  71.3 0.9 copy-done.25
  72.2 0.9 copy-done.27
  73.2 8.3 %region_backward.1 = (bf16[16,2,16,192]{3,2,1,0:T(8,128)(2,1)S(1)}, bf16[2304,128]{1,0:T(8,128)(2,1)S(1)}, f32[4,3]{1,0:T(4,128)}, f32[192,3]{1,0:T(8,128)S(1)}) custom-call(s32[4]{0:T(128)S(1)} %pad_add_fusion.idx_ref, s32[512]{0:T(512)S(1)} %copy-done.30, f32[8,8,128]{2,1,0:T(8,128)S(1)} %all-to-all-done.2.z_ref, s32[512,256]{1,0:T(8,128)S(1)} %copy-done.2, ...), custom_call_target="tpu_custom_call" | custom-call | tf_op jit(solution)/shard_map/region_backward/pallas_call | solution.py:341
  81.5 11.4 %all_to_all.41 = bf16[16,32,192]{2,1,0:T(8,128)(2,1)S(1)} all-to-all(bf16[16,32,192]{2,1,0:T(8,128)(2,1)S(1)} %bitcast.17), channel_id=1, replica_groups=mesh['zl'=2,'x'=4,'c'=2,'zh'=4,'y'=4] {'zl','x','c'}, dimensions={0} | all-to-all | bytes 393216 | tf_op jit(solution)/shard_map/all_to_all | solution.py:544
  92.9 6.1 %patch_backward.1 = (bf16[16,384,128]{2,1,0:T(8,128)(2,1)S(1)}, bf16[16,384,128]{2,1,0:T(8,128)(2,1)S(1)}) custom-call(s32[4]{0:T(128)S(1)} %pad_add_fusion.idx_ref, bf16[512,192]{1,0:T(8,128)(2,1)S(1)} %bitcast.16, bf16[512,384]{1,0:T(8,128)(2,1)S(1)} %bitcast.14, bf16[512,384]{1,0:T(8,128)(2,1)S(1)} %copy-done.10, bf16[512,1536]{1,0:T(8,128)(2,1)} %copy-done.3, ...), custom_call_target="tpu_custom_call" | custom-call | tf_op jit(solution)/shard_map/patch_backward/pallas_call | solution.py:442
  98.9 1.1 collective-permute-start
  100.0 3.0 %collective-permute-done = bf16[16,384,128]{2,1,0:T(8,128)(2,1)S(1)} collective-permute-done((bf16[16,384,128]{2,1,0:T(8,128)(2,1)S(1)}, bf16[16,384,128]{2,1,0:T(8,128)(2,1)S(1)}, u32[]{:S(2)}, u32[]{:S(2)}) %collective-permute-start) | collective-permute-done | bytes 1572896 | tf_op jit(solution)/shard_map/ppermute | solution.py:548
  103.0 0.4 add_convert_fusion
  103.4 24.8 %all_to_all.42 = bf16[16,384,128]{2,1,0:T(8,128)(2,1)S(1)} all-to-all(bf16[16,384,128]{2,1,0:T(8,128)(2,1)S(1)} %add_convert_fusion), channel_id=1, replica_groups=mesh['zl'=2,'x'=4,'c'=2,'zh'=4,'y'=4] {'y','x'}, dimensions={0} | all-to-all | bytes 3145728 | tf_op jit(solution)/shard_map/all_to_all | solution.py:544
  128.2 0.2 reduce_sum.34
  128.4 10.0 %all_to_all.43 = bf16[8,48,128]{2,1,0:T(8,128)(2,1)S(1)} all-to-all(bf16[8,48,128]{2,1,0:T(8,128)(2,1)S(1)} %bitcast.20), channel_id=1, replica_groups=mesh['zl'=2,'x'=4,'c'=2,'zh'=4,'y'=4] {'zh','zl'}, dimensions={0} | all-to-all | bytes 196608 | tf_op jit(solution)/shard_map/all_to_all | solution.py:544
  138.4 10.0 %all_to_all.44 = bf16[8,48,128]{2,1,0:T(8,128)(2,1)S(1)} all-to-all(bf16[8,48,128]{2,1,0:T(8,128)(2,1)S(1)} %broadcast_in_dim.9), channel_id=1, replica_groups=mesh['zl'=2,'x'=4,'c'=2,'zh'=4,'y'=4] {'zh','zl'}, dimensions={0} | all-to-all | bytes 196608 | tf_op jit(solution)/shard_map/all_to_all | solution.py:544
  148.5 0.3 broadcast_in_dim.22
  148.8 22.6 %all_to_all.45.mine_ref = bf16[16,384,128]{2,1,0:T(8,128)(2,1)S(1)} all-to-all(bf16[16,384,128]{2,1,0:T(8,128)(2,1)S(1)} %broadcast_in_dim.22), channel_id=1, replica_groups=mesh['zl'=2,'x'=4,'c'=2,'zh'=4,'y'=4] {'y','x'}, dimensions={0} | all-to-all | bytes 3145728 | tf_op jit(solution)/shard_map/all_to_all | solution.py:544
  171.3 4.6 %collective-permute-start.1 = (bf16[16,384,128]{2,1,0:T(8,128)(2,1)S(1)}, bf16[16,384,128]{2,1,0:T(8,128)(2,1)S(1)}, u32[]{:S(2)}, u32[]{:S(2)}) collective-permute-start(bf16[16,384,128]{2,1,0:T(8,128)(2,1)S(1)} %all_to_all.45.mine_ref), channel_id=1, source_target_pairs={{0,16},{16,0},{1,17},{17,1},{2,18},{18,2},{3,19},{19,3},{4,20},{20... | collective-permute-start | bytes 4718600 | tf_op jit(solution)/shard_map/ppermute | solution.py:548
  175.9 0.7 copy.36
  176.6 2.4 %collective-permute-done.1.other_ref = bf16[16,384,128]{2,1,0:T(8,128)(2,1)S(1)} collective-permute-done((bf16[16,384,128]{2,1,0:T(8,128)(2,1)S(1)}, bf16[16,384,128]{2,1,0:T(8,128)(2,1)S(1)}, u32[]{:S(2)}, u32[]{:S(2)}) %collective-permute-start.1) | collective-permute-done | bytes 1572896 | tf_op jit(solution)/shard_map/ppermute | solution.py:548
  179.0 3.5 %unpack.1 = (f32[384,1536]{1,0:T(8,128)}, f32[1536,384]{1,0:T(8,128)}, f32[384,192]{1,0:T(8,128)S(1)}, f32[192,192]{1,0:T(8,128)}, f32[192,192]{1,0:T(8,128)}, /...) custom-call(s32[4]{0:T(128)S(1)} %pad_add_fusion.idx_ref, ...), custom_call_target="tpu_custom_call" | custom-call | tf_op jit(solution)/shard_map/unpack/pallas_call | solution.py:512
  182.5 0.9 copy.35
  (51 shorter events, 0.2 us)
Async XLA Ops:
  1.7 1.3 copy-start
  3.0 1.0 copy-start.4
  4.0 1.3 copy-start.6
  5.2 20.7 %copy-start.2 = (s32[512,256]{1,0:T(8,128)S(1)}, s32[512,256]{1,0:T(8,128)}, u32[]{:S(2)}) copy-start(s32[512,256]{1,0:T(8,128)} %tis_ref.3) | copy-start | bytes 1572868
  5.2 20.7 %copy-start.7 = (f32[192,192]{1,0:T(8,128)S(1)}, f32[192,192]{1,0:T(8,128)}, u32[]{:S(2)}) copy-start(f32[192,192]{1,0:T(8,128)} %av_ref.3) | copy-start | bytes 442372
  5.2 20.7 %copy-start.8 = (f32[192,192]{1,0:T(8,128)S(1)}, f32[192,192]{1,0:T(8,128)}, u32[]{:S(2)}) copy-start(f32[192,192]{1,0:T(8,128)} %au_ref.3) | copy-start | bytes 442372
  5.2 20.7 %copy-start.30 = (s32[512]{0:T(512)S(1)}, s32[512]{0:T(512)}, u32[]{:S(2)}) copy-start(s32[512]{0:T(512)} %slide_ref.3) | copy-start | bytes 6148
  5.2 20.7 %copy-start.31 = (f32[192]{0:T(256)S(1)}, f32[192]{0:T(256)}, u32[]{:S(2)}) copy-start(f32[192]{0:T(256)} %param.27) | copy-start | bytes 2308
  10.3 1.1 copy-start.3
  11.4 14.5 %copy-start.9 = (bf16[512,384]{1,0:T(8,128)(2,1)}, bf16[512,384]{1,0:T(8,128)(2,1)S(1)}, u32[]{:S(2)}) copy-start(bf16[512,384]{1,0:T(8,128)(2,1)S(1)} %get-tuple-element.59.mid_ref) | copy-start | bytes 1179652
  11.4 46.5 %copy-start.33 = (f32[192,3]{0,1:T(4,128)S(1)}, f32[192,3]{0,1:T(4,128)}, u32[]{:S(2)}) copy-start(f32[192,3]{0,1:T(4,128)} %param.28) | copy-start | bytes 6916
  11.4 53.5 %copy-start.32 = (f32[4,3]{1,0:T(4,128)S(1)}, f32[4,3]{1,0:T(4,128)}, u32[]{:S(2)}) copy-start(f32[4,3]{1,0:T(4,128)} %gl_ref.1) | copy-start | bytes 148
  11.4 14.5 %all-to-all-start = ((bf16[16,32,192]{2,1,0:T(8,128)(2,1)}), bf16[16,32,192]{2,1,0:T(8,128)(2,1)S(1)}, u32[]{:S(2)}, u32[]{:S(2)}) async-start(bf16[16,32,192]{2,1,0:T(8,128)(2,1)} %bitcast.5), calls=%async_computation | async-start | bytes 524288 | tf_op jit(solution)/shard_map/all_to_all | solution.py:544
  26.0 0.9 copy-start.11
  26.9 0.9 copy-start.13
  27.7 0.9 copy-start.15
  28.6 0.9 copy-start.17
  33.7 0.7 copy-start.20
  34.4 0.7 copy-start.22
  35.1 0.7 copy-start.24
  35.8 0.7 copy-start.26
  50.6 14.3 %all-to-all-start.2 = ((f32[8,8,128]{2,1,0:T(8,128)}), f32[8,8,128]{2,1,0:T(8,128)S(1)}, u32[]{:S(2)}, u32[]{:S(2)}) async-start(f32[8,8,128]{2,1,0:T(8,128)} %broadcast_in_dim.8), calls=%async_computation.2 | async-start | bytes 65536 | tf_op jit(solution)/shard_map/all_to_all | solution.py:544
  64.9 0.9 copy-start.12
  65.8 0.9 copy-start.14
  66.7 0.9 copy-start.16
  67.6 0.9 copy-start.18
  68.5 0.9 copy-start.19
  69.4 0.9 copy-start.21
  70.3 0.9 copy-start.23
  71.3 0.9 copy-start.25
  72.2 0.9 copy-start.27
  73.2 19.6 %copy-start.1 = (bf16[1536,384]{1,0:T(8,128)(2,1)S(1)}, bf16[1536,384]{1,0:T(8,128)(2,1)}, u32[]{:S(2)}) copy-start(bf16[1536,384]{1,0:T(8,128)(2,1)} %wd_ref.3) | copy-start | bytes 3538948
  73.2 19.6 %copy-start.5 = (bf16[32,16,384]{2,1,0:T(8,128)(2,1)S(1)}, bf16[32,16,384]{2,1,0:T(8,128)(2,1)}, u32[]{:S(2)}) copy-start(bf16[32,16,384]{2,1,0:T(8,128)(2,1)} %param.15) | copy-start | bytes 1179652
  73.2 19.7 %copy-start.10 = (bf16[512,384]{1,0:T(8,128)(2,1)S(1)}, bf16[512,384]{1,0:T(8,128)(2,1)}, u32[]{:S(2)}) copy-start(bf16[512,384]{1,0:T(8,128)(2,1)} %copy-done.9) | copy-start | bytes 1179652
  81.5 11.4 %copy-start.28 = (f32[192,3]{1,0:T(8,128)}, f32[192,3]{1,0:T(8,128)S(1)}, u32[]{:S(2)}) copy-start(f32[192,3]{1,0:T(8,128)S(1)} %get-tuple-element.99) | copy-start | bytes 6916
  98.9 4.1 %collective-permute-start = (bf16[16,384,128]{2,1,0:T(8,128)(2,1)S(1)}, bf16[16,384,128]{2,1,0:T(8,128)(2,1)S(1)}, u32[]{:S(2)}, u32[]{:S(2)}) collective-permute-start(bf16[16,384,128]{2,1,0:T(8,128)(2,1)S(1)} %get-tuple-element.64), channel_id=1, source_target_pairs={{0,16},{16,0},{1,17},{17,1},{2,18},{18,2},{3,19},{19,3},{4,20},{20... | collective-permute-start | bytes 4718600 | tf_op jit(solution)/shard_map/ppermute | solution.py:548
  148.8 27.2 %copy-start.29 = (f32[192,3]{1,0:T(8,128)S(1)}, f32[192,3]{1,0:T(8,128)}, u32[]{:S(2)}) copy-start(f32[192,3]{1,0:T(8,128)} %copy-done.28) | copy-start | bytes 6916
  171.3 7.6 %collective-permute-start.1 = (bf16[16,384,128]{2,1,0:T(8,128)(2,1)S(1)}, bf16[16,384,128]{2,1,0:T(8,128)(2,1)S(1)}, u32[]{:S(2)}, u32[]{:S(2)}) collective-permute-start(bf16[16,384,128]{2,1,0:T(8,128)(2,1)S(1)} %all_to_all.45.mine_ref), channel_id=1, source_target_pairs={{0,16},{16,0},{1,17},{17,1},{2,18},{18,2},{3,19},{19,3},{4,20},{20... | collective-permute-start | bytes 4718600 | tf_op jit(solution)/shard_map/ppermute | solution.py:548

commit v2 on v1

--- a/solution.py
+++ b/solution.py
@@ -23,11 +23,15 @@
 BF = jnp.bfloat16
 F32 = jnp.float32
 HIGHEST = lax.Precision.HIGHEST
-VMEM_LIMIT = 48 * 1024 * 1024
-
-CHUNKS = 32
-HALF = CHUNKS // 2
-CH_ROWS = 384
+MIB = 1024 * 1024
+
+HALF_ROWS = 6144
+DOWN_AT = 2304
+REST_AT = 4608
+REST_ROWS = 1152
+EMBED_AT = REST_AT + REST_ROWS
+PAD_AT = EMBED_AT + 288
+PEERS = 32
 
 
 def nn(a, b, precision=None):
@@ -46,8 +50,24 @@
     )
 
 
-def params():
-    return pltpu.CompilerParams(vmem_limit_bytes=VMEM_LIMIT)
+def params(mib=32):
+    return pltpu.CompilerParams(vmem_limit_bytes=mib * MIB)
+
+
+def fetch_all(srcs, dsts, sems):
+    copies = [
+        pltpu.make_async_copy(src, dst, sems.at[i]) for i, (src, dst) in enumerate(zip(srcs, dsts))
+    ]
+    for copy in copies:
+        copy.start()
+    for copy in copies:
+        copy.wait()
+
+
+def weight_scratch():
+    return [pltpu.VMEM((D2, D2), BF)] * 4 + [pltpu.VMEM((D2, D2), F32)] * 2 + [
+        pltpu.SemaphoreType.DMA((6,))
+    ]
 
 
 def patch_forward_kernel(x_ref, wu_ref, wd_ref, we_ref, feat_ref, hid_ref, gp_ref, mid_ref, acc):
@@ -75,7 +95,7 @@
     def _():
         mid = acc[...].astype(BF)
         mid_ref[...] = mid
-        feat_ref[...] = nn(mid, we_ref[...]).astype(BF)
+        feat_ref[...] = nt(mid, we_ref[...]).astype(BF)
 
 
 def patch_forward(tokens, w_up, w_down, w_embed):
@@ -90,7 +110,7 @@
             pl.BlockSpec((rows, D1), whole),
             pl.BlockSpec((D1, fb), lambda i: (0, i)),
             pl.BlockSpec((fb, D1), lambda i: (i, 0)),
-            pl.BlockSpec((D1, D2), whole),
+            pl.BlockSpec((D2, D1), whole),
         ],
         out_specs=[
             pl.BlockSpec((rows, D2), whole),
@@ -105,7 +125,7 @@
             jax.ShapeDtypeStruct((rows, D1), BF),
         ],
         scratch_shapes=[pltpu.VMEM((rows, D1), F32)],
-        compiler_params=params(),
+        compiler_params=params(60),
         name="patch_forward",
     )(tokens, w_up, w_down, w_embed)
 
@@ -123,11 +143,21 @@
 
 
 def region_forward_kernel(
-    idx_ref, slide_ref, f_ref, tis_ref, wq_ref, wk_ref, wv_ref, wo_ref, av_ref, au_ref, aw_ref,
+    idx_ref, slide_ref, f_ref, tis_ref, wq_in, wk_in, wv_in, wo_in, av_in, au_in, aw_ref,
     p_ref, x_ref, q_ref, k_ref, v_ref, se_ref, asum_ref, reg_ref, tanh_ref, gate_ref, w_ref,
     part_ref,
+    wq_ref, wk_ref, wv_ref, wo_ref, av_ref, au_ref, wsems,
 ):
     r = pl.program_id(0)
+
+    @pl.when(r == 0)
+    def _():
+        fetch_all(
+            (wq_in, wk_in, wv_in, wo_in, av_in, au_in),
+            (wq_ref, wk_ref, wv_ref, wo_ref, av_ref, au_ref),
+            wsems,
+        )
+
     trow = tissue_row(idx_ref, tis_ref, r)
     tcol = column_of(trow, D2)
     x = (f_ref[...].reshape(PATCH, D2).astype(F32) * tcol).astype(BF)
@@ -184,7 +214,7 @@
 
 
 def region_forward(idx, slide, got, tissue, w_query, w_key, w_value, w_out, att_v, att_u, att_w):
-    sq = pl.BlockSpec((D2, D2), lambda r, *_: (0, 0))
+    sq = pl.BlockSpec(memory_space=pltpu.HBM)
     row8 = lambda width: pl.BlockSpec((8, width), lambda r, *_: (0, 0))
     per_region = lambda rows, width: pl.BlockSpec((1, rows, width), lambda r, *_: (r, 0, 0))
     tok = lambda dt: jax.ShapeDtypeStruct((OWN, PATCH, D2), dt)
@@ -211,8 +241,9 @@
                 row8(D2),
                 row8(D2),
                 row8(128),
-                pl.BlockSpec((CHUNKS, 8, 128), lambda r, *_: (0, 0, 0)),
+                pl.BlockSpec((PEERS, 8, 128), lambda r, *_: (0, 0, 0)),
             ],
+            scratch_shapes=weight_scratch(),
         ),
         out_shape=[
             jax.ShapeDtypeStruct((OWN, HEADS * PATCH, PATCH), BF),
@@ -222,43 +253,49 @@
             jax.ShapeDtypeStruct((8, D2), F32),
             jax.ShapeDtypeStruct((8, D2), F32),
             jax.ShapeDtypeStruct((8, 128), F32),
-            jax.ShapeDtypeStruct((CHUNKS, 8, 128), F32),
+            jax.ShapeDtypeStruct((PEERS, 8, 128), F32),
         ],
-        compiler_params=params(),
+        compiler_params=params(60),
         name="region_forward",
     )(idx, slide, got, tissue, w_query, w_key, w_value, w_out, att_v, att_u, att_w)
 
 
 def region_backward_kernel(
-    idx_ref, slide_ref, z_ref, tis_ref, wq_ref, wk_ref, wv_ref, wo_ref, av_ref, au_ref, aw_ref,
+    idx_ref, slide_ref, z_ref, tis_ref, wq_in, wk_in, wv_in, wo_in, av_in, au_in, aw_ref,
     wc_ref, gl_ref,
     p_ref, x_ref, q_ref, k_ref, v_ref, se_ref, asum_ref, reg_ref, tanh_ref, gate_ref, w_ref,
     df_ref, rest_ref, logits_ref, gc_ref,
     dm_s, da_s, kt_s, dqt_s, gq_s, gk_s, gv_s,
+    wq_ref, wk_ref, wv_ref, wo_ref, av_ref, au_ref, wsems,
 ):
     r = pl.program_id(0)
     trow = tissue_row(idx_ref, tis_ref, r)
     tcol = column_of(trow, D2)
 
     def put(slot, grad, fill=None):
-        low = 2 * D2 * slot
-        rest_ref[pl.ds(low, D2), :] = grad[:, :128].astype(BF)
-        if fill is None:
-            fill = jnp.zeros((D2, 64), F32)
-        high = jnp.concatenate([grad[:, 128:], fill], axis=1)
-        rest_ref[pl.ds(low + D2, D2), :] = high.astype(BF)
+        for half in range(2):
+            rows = grad[96 * half : 96 * half + 96]
+            rest_ref[half, pl.ds(192 * slot, 96), :] = rows[:, :128].astype(BF)
+            tail = jnp.zeros((96, 64), F32) if fill is None else fill
+            high = jnp.concatenate([rows[:, 128:], tail], axis=1)
+            rest_ref[half, pl.ds(192 * slot + 96, 96), :] = high.astype(BF)
 
     @pl.when(r == 0)
     def _():
+        fetch_all(
+            (wq_in, wk_in, wv_in, wo_in, av_in, au_in),
+            (wq_ref, wk_ref, wv_ref, wo_ref, av_ref, au_ref),
+            wsems,
+        )
         z = jnp.sum(z_ref[...], axis=0)
         low, high = z[0:SLIDES], z[SLIDES:]
         total = high[:, 64:65]
         summary = jnp.concatenate([low, high[:, :64]], axis=1) / total
         wc = wc_ref[...]
         gl = gl_ref[...]
-        logits_ref[...] = nn(summary, wc, HIGHEST)
-        gc_ref[...] = tn(summary, gl, HIGHEST)
-        d_summary = nt(gl, wc, HIGHEST)
+        logits_ref[...] = nt(summary, wc, HIGHEST)
+        gc_ref[...] = tn(gl, summary, HIGHEST)
+        d_summary = nn(gl, wc, HIGHEST)
         slot = lax.broadcasted_iota(jnp.int32, (SLIDES, 1), 0)
         row = lax.broadcasted_iota(jnp.int32, (8, 1), 0)
         d_own = jnp.zeros((8, D2), F32)
@@ -291,11 +328,9 @@
         da_s[...] = nt(dm, wo_ref[...])
         put(3, tn(asum_ref[...], dm.astype(F32), HIGHEST))
         put(4, tn(region, d_pre_v, HIGHEST))
-        put(
-            5,
-            tn(region, d_pre_u, HIGHEST),
-            tn(tanh_part * gate_part, jnp.broadcast_to(d_score, (8, 64)), HIGHEST),
-        )
+        g_aw = tn(tanh_part * gate_part, jnp.broadcast_to(d_score, (8, 64)), HIGHEST)
+        lane = lax.broadcasted_iota(jnp.int32, (96, 64), 1)
+        put(5, tn(region, d_pre_u, HIGHEST), jnp.where(lane == 0, g_aw[:96], g_aw[96:]))
         gq_s[...] = jnp.zeros_like(gq_s)
         gk_s[...] = jnp.zeros_like(gk_s)
         gv_s[...] = jnp.zeros_like(gv_s)
@@ -335,7 +370,7 @@
 
 
 def region_backward(idx, slide, z, tissue, weights, kept):
-    sq = pl.BlockSpec((D2, D2), lambda r, *_: (0, 0))
+    sq = pl.BlockSpec(memory_space=pltpu.HBM)
     row8 = lambda width: pl.BlockSpec((8, width), lambda r, *_: (0, 0))
     per_region = lambda rows, width: pl.BlockSpec((1, rows, width), lambda r, *_: (r, 0, 0))
     return pl.pallas_call(
@@ -348,7 +383,7 @@
                 pl.BlockSpec((8, PATCH), lambda r, idx, _: (idx[2], 0)),
                 sq, sq, sq, sq, sq, sq,
                 pl.BlockSpec((1, D2), lambda r, *_: (0, 0)),
-                pl.BlockSpec((D2, 3), lambda r, *_: (0, 0)),
+                pl.BlockSpec((3, D2), lambda r, *_: (0, 0)),
                 pl.BlockSpec((SLIDES, 3), lambda r, *_: (0, 0)),
                 per_region(HEADS * PATCH, PATCH),
                 per_region(PATCH, D2),
@@ -364,9 +399,9 @@
             ],
             out_specs=[
                 pl.BlockSpec((GRP, 1, PATCH // GRP, D2), lambda r, *_: (0, r, 0, 0)),
-                pl.BlockSpec((12 * D2, 128), lambda r, *_: (0, 0)),
+                pl.BlockSpec((2, REST_ROWS, 128), lambda r, *_: (0, 0, 0)),
                 pl.BlockSpec((SLIDES, 3), lambda r, *_: (0, 0)),
-                pl.BlockSpec((D2, 3), lambda r, *_: (0, 0)),
+                pl.BlockSpec((3, D2), lambda r, *_: (0, 0)),
             ],
             scratch_shapes=[
                 pltpu.VMEM((8, D2), F32),
@@ -376,15 +411,15 @@
                 pltpu.VMEM((D2, D2), F32),
                 pltpu.VMEM((D2, D2), F32),
                 pltpu.VMEM((D2, D2), F32),
-            ],
+            ] + weight_scratch(),
         ),
         out_shape=[
             jax.ShapeDtypeStruct((GRP, OWN, PATCH // GRP, D2), BF),
-            jax.ShapeDtypeStruct((12 * D2, 128), BF),
+            jax.ShapeDtypeStruct((2, REST_ROWS, 128), BF),
             jax.ShapeDtypeStruct((SLIDES, 3), F32),
-            jax.ShapeDtypeStruct((D2, 3), F32),
+            jax.ShapeDtypeStruct((3, D2), F32),
         ],
-        compiler_params=params(),
+        compiler_params=params(60),
         name="region_backward",
     )(idx, slide, z, tissue, *weights, *kept)
 
@@ -399,41 +434,71 @@
     pack, dmid_s, sems,
 ):
     step = pl.program_id(0)
+    core = idx_ref[3]
+
+    def up_copies(i):
+        rows = pl.ds(pl.multiple_of(576 * i, 64), 576)
+        return (
+            pltpu.make_async_copy(pack.at[core, rows], mine_ref.at[rows], sems.at[2 * i]),
+            pltpu.make_async_copy(pack.at[1 - core, rows], other_ref.at[rows], sems.at[2 * i + 1]),
+        )
+
+    def down_copy(i, dst):
+        rows = pl.ds(pl.multiple_of(DOWN_AT + 1152 * lax.rem(i, 2), 128), 1152)
+        return pltpu.make_async_copy(pack.at[i // 2, rows], dst.at[rows], sems.at[8 + i])
+
+    def rest_copies():
+        rows = pl.ds(REST_AT, HALF_ROWS - REST_AT)
+        return (
+            pltpu.make_async_copy(pack.at[core, rows], mine_ref.at[rows], sems.at[12]),
+            pltpu.make_async_copy(pack.at[1 - core, rows], other_ref.at[rows], sems.at[13]),
+        )
 
     @pl.when(step == 0)
     def _():
         df = df_ref[...]
-        dmid_s[...] = nt(df, we_ref[...]).astype(BF)
-        g_embed = tn(mid_ref[...], df)
-        for j in range(24):
-            pack[j, pl.ds(288, 96), :] = rest_ref[pl.ds(96 * j, 96), :]
-        high = jnp.concatenate([g_embed[:, 128:], jnp.zeros((D1, 64), F32)], axis=1)
-        for j in range(4):
-            pack[24 + j, pl.ds(288, 96), :] = g_embed[96 * j : 96 * j + 96, :128].astype(BF)
-            pack[28 + j, pl.ds(288, 96), :] = high[96 * j : 96 * j + 96].astype(BF)
+        dmid_s[...] = nn(df, we_ref[...]).astype(BF)
+        g_embed = tn(df, mid_ref[...]).astype(BF)
+        for half in range(2):
+            pack[half, pl.ds(REST_AT, REST_ROWS), :] = rest_ref[half]
+            for l in range(3):
+                block = g_embed[96 * half : 96 * half + 96, 128 * l : 128 * l + 128]
+                pack[half, pl.ds(EMBED_AT + 96 * l, 96), :] = block
+            pack[half, pl.ds(PAD_AT, 96), :] = jnp.zeros((96, 128), BF)
+        for copy in rest_copies():
+            copy.start()
 
     dmid = dmid_s[...]
     d_pre = (nt(dmid, wd_ref[...]) * gp_ref[...].astype(F32)).astype(BF)
+    g_up = tn(x_ref[...], d_pre).astype(BF)
+    for half in range(2):
+        for l in range(3):
+            block = g_up[192 * half : 192 * half + 192, 128 * l : 128 * l + 128]
+            pack[half, pl.ds(pl.multiple_of(576 * step + 192 * l, 64), 192), :] = block
+    for copy in up_copies(step):
+        copy.start()
     g_down = tn(hid_ref[...], dmid).astype(BF)
-    g_up = tn(x_ref[...], d_pre).astype(BF)
-    for j in range(8):
-        for l in range(3):
-            block = g_up[48 * j : 48 * j + 48, 128 * l : 128 * l + 128]
-            pack[4 * j + step, pl.ds(48 * l, 48), :] = block
-            block = g_down[48 * j : 48 * j + 48, 128 * l : 128 * l + 128]
-            pack[8 * step + j, pl.ds(144 + 48 * l, 48), :] = block
+    at = DOWN_AT + 1152 * lax.rem(step, 2)
+    for l in range(3):
+        rows = pl.ds(pl.multiple_of(at + 384 * l, 128), 384)
+        pack[step // 2, rows, :] = g_down[:, 128 * l : 128 * l + 128]
+
+    @pl.when(step // 2 == core)
+    def _():
+        down_copy(step, mine_ref).start()
+
+    @pl.when(step // 2 != core)
+    def _():
+        down_copy(step, other_ref).start()
 
     @pl.when(step == pl.num_programs(0) - 1)
     def _():
-        core = idx_ref[3]
-        keep = pltpu.make_async_copy(pack.at[pl.ds(core * HALF, HALF)], mine_ref, sems.at[0])
-        send = pltpu.make_async_copy(
-            pack.at[pl.ds((1 - core) * HALF, HALF)], other_ref, sems.at[1]
-        )
-        send.start()
-        keep.start()
-        send.wait()
-        keep.wait()
+        for copy in rest_copies():
+            copy.wait()
+        for i in range(STEPS4):
+            for copy in up_copies(i):
+                copy.wait()
+            down_copy(i, mine_ref).wait()
 
 
 def patch_backward(idx, df, tokens, mid, hid, gp, w_embed, w_down, rest):
@@ -450,92 +515,82 @@
                 pl.BlockSpec((rows, D1), whole),
                 pl.BlockSpec((rows, FB4), lambda i, *_: (0, i)),
                 pl.BlockSpec((rows, FB4), lambda i, *_: (0, i)),
-                pl.BlockSpec((D1, D2), whole),
+                pl.BlockSpec((D2, D1), whole),
                 pl.BlockSpec((FB4, D1), lambda i, *_: (i, 0)),
-                pl.BlockSpec((12 * D2, 128), whole),
+                pl.BlockSpec((2, REST_ROWS, 128), lambda i, *_: (0, 0, 0)),
             ],
             out_specs=[
                 pl.BlockSpec(memory_space=pl.ANY),
                 pl.BlockSpec(memory_space=pl.ANY),
             ],
             scratch_shapes=[
-                pltpu.VMEM((CHUNKS, CH_ROWS, 128), BF),
+                pltpu.VMEM((2, HALF_ROWS, 128), BF),
                 pltpu.VMEM((rows, D1), BF),
-                pltpu.SemaphoreType.DMA((2,)),
+                pltpu.SemaphoreType.DMA((14,)),
             ],
         ),
         out_shape=[
-            jax.ShapeDtypeStruct((HALF, CH_ROWS, 128), BF),
-            jax.ShapeDtypeStruct((HALF, CH_ROWS, 128), BF),
+            jax.ShapeDtypeStruct((HALF_ROWS, 128), BF),
+            jax.ShapeDtypeStruct((HALF_ROWS, 128), BF),
         ],
-        compiler_params=params(),
+        compiler_params=params(58),
         name="patch_backward",
     )(idx, df, tokens, mid, hid, gp, w_embed, w_down, rest)
 
 
-def unpack_kernel(
-    idx_ref, mine_ref, other_ref,
-    up_ref, down_ref, embed_ref, q_ref, k_ref, v_ref, o_ref, av_ref, au_ref, aw_ref,
-    pack, sems,
-):
-    core = idx_ref[3]
-    keep = pltpu.make_async_copy(mine_ref, pack.at[pl.ds(core * HALF, HALF)], sems.at[0])
-    got = pltpu.make_async_copy(other_ref, pack.at[pl.ds((1 - core) * HALF, HALF)], sems.at[1])
-    keep.start()
-    got.start()
-    keep.wait()
-    got.wait()
-    for j in range(CHUNKS):
+def unpack_kernel(idx_ref, src_ref, *refs):
+    up_ref, down_ref, embed_ref, q_ref, k_ref, v_ref, o_ref, av_ref, au_ref, aw_ref = refs[-10:]
+    for l in range(12):
+        up_ref[:, pl.ds(128 * l, 128)] = src_ref[pl.ds(192 * l, 192), :].astype(F32)
+    for i in range(2):
         for l in range(3):
-            lanes = pl.ds(384 * (j % 4) + 128 * l, 128)
-            up_ref[pl.ds(48 * (j // 4), 48), lanes] = pack[j, pl.ds(48 * l, 48), :].astype(F32)
-            lanes = pl.ds(128 * l, 128)
-            down_ref[pl.ds(48 * j, 48), lanes] = pack[j, pl.ds(144 + 48 * l, 48), :].astype(F32)
+            rows = src_ref[pl.ds(DOWN_AT + 1152 * i + 384 * l, 384), :]
+            down_ref[pl.ds(384 * i, 384), pl.ds(128 * l, 128)] = rows.astype(F32)
     for slot, ref in enumerate((q_ref, k_ref, v_ref, o_ref, av_ref, au_ref)):
-        for i in range(2):
-            rows = pl.ds(96 * i, 96)
-            ref[rows, pl.ds(0, 128)] = pack[4 * slot + i, pl.ds(288, 96), :].astype(F32)
-            ref[rows, pl.ds(128, 64)] = pack[4 * slot + 2 + i, pl.ds(288, 96), :][:, :64].astype(F32)
-    tail = jnp.concatenate(
-        [pack[22, pl.ds(288, 96), :].astype(F32), pack[23, pl.ds(288, 96), :].astype(F32)], axis=0
-    )
-    aw_ref[...] = tail.T[64:65, :]
-    for i in range(4):
-        rows = pl.ds(96 * i, 96)
-        embed_ref[rows, pl.ds(0, 128)] = pack[24 + i, pl.ds(288, 96), :].astype(F32)
-        embed_ref[rows, pl.ds(128, 64)] = pack[28 + i, pl.ds(288, 96), :][:, :64].astype(F32)
-
-
-def unpack(idx, mine, other):
+        at = REST_AT + 192 * slot
+        ref[:, pl.ds(0, 128)] = src_ref[pl.ds(at, 96), :].astype(F32)
+        ref[:, pl.ds(128, 64)] = src_ref[pl.ds(at + 96, 96), :][:, :64].astype(F32)
+    for l in range(3):
+        embed_ref[:, pl.ds(128 * l, 128)] = src_ref[pl.ds(EMBED_AT + 96 * l, 96), :].astype(F32)
+    tail = src_ref[pl.ds(EMBED_AT - 96, 96), :].astype(F32).T
+    aw_ref[:, pl.ds(0, 96)] = tail[64:65, :]
+    aw_ref[:, pl.ds(96, 96)] = tail[65:66, :]
+
+
+def unpack(idx, src, which, earlier=()):
     square = jax.ShapeDtypeStruct((D2, D2), F32)
-    vm = pl.BlockSpec(memory_space=pltpu.VMEM)
+    half = lambda rows, width: pl.BlockSpec((rows, width), lambda i, idx: (idx[which], 0))
+    hbm = pl.BlockSpec(memory_space=pltpu.HBM)
     return pl.pallas_call(
         unpack_kernel,
-        in_specs=[
-            pl.BlockSpec(memory_space=pltpu.SMEM),
-            pl.BlockSpec(memory_space=pl.ANY),
-            pl.BlockSpec(memory_space=pl.ANY),
-        ],
-        out_specs=[vm] * 10,
+        grid_spec=pltpu.PrefetchScalarGridSpec(
+            num_scalar_prefetch=1,
+            grid=(1,),
+            in_specs=[pl.BlockSpec((HALF_ROWS, 128), lambda i, idx: (0, 0))] + [hbm] * len(earlier),
+            out_specs=[
+                half(D1 // 2, F1),
+                half(F1 // 2, D1),
+                half(D2 // 2, D1),
+            ]
+            + [half(D2 // 2, D2)] * 6
+            + [pl.BlockSpec((1, D2), lambda i, idx: (0, 0))],
+        ),
         out_shape=[
             jax.ShapeDtypeStruct((D1, F1), F32),
             jax.ShapeDtypeStruct((F1, D1), F32),
-            jax.ShapeDtypeStruct((D1, D2), F32),
+            jax.ShapeDtypeStruct((D2, D1), F32),
             square, square, square, square, square, square,
             jax.ShapeDtypeStruct((1, D2), F32),
         ],
-        scratch_shapes=[
-            pltpu.VMEM((CHUNKS, CH_ROWS, 128), BF),
-            pltpu.SemaphoreType.DMA((2,)),
-        ],
+        input_output_aliases={2 + i: i for i in range(len(earlier))},
         compiler_params=params(),
         name="unpack",
-    )(idx, mine, other)
+    )(idx, src, *earlier)
 
 
 GRP_AXES = ("zl", "x", "c")
 DEV_AXES = ("zh", "y")
-XY = ("y", "x")
+ZLXY = ("y", "zl", "x")
 XYC = ("y", "x", "c")
 Z = ("zh", "zl")
 
@@ -550,6 +605,16 @@
 
 def spread(x, n):
     return jnp.broadcast_to(x[None], (n,) + x.shape)
+
+
+def add_pair(x, y):
+    return (x.astype(F32) + y.astype(F32)).astype(x.dtype)
+
+
+def add_over_zh(x):
+    for flip in (1, 3):
+        x = add_pair(x, lax.ppermute(x, "zh", [(i, i ^ flip) for i in range(4)]))
+    return x
 
 
 def add_up(x):
@@ -564,10 +629,10 @@
     dev = lax.axis_index(DEV_AXES)
     core = lax.axis_index("c")
     first = (dev * GRP + grp) * OWN
-    idx = jnp.stack([first, first % 8, first // 8, core]).astype(jnp.int32)
+    idx = jnp.stack([first, first % 8, first // 8, core, 1 - core]).astype(jnp.int32)
     tokens = patches.reshape(-1, D1)
     att_row = att_w.reshape(1, D2)
-    feat, hid, gp, mid = patch_forward(tokens, w_up, w_down, w_embed)
+    feat, hid, gp, mid = patch_forward(tokens, w_up, w_down, w_embed.T)
     got = exchange(feat.reshape(GRP, -1, D2), GRP_AXES)
     got = got.reshape(GRP, OWN, PATCH // GRP, D2)
     *kept, part = region_forward(
@@ -577,18 +642,19 @@
     z = exchange(spread(z, 8), Z)
     df, rest, logits, g_class = region_backward(
         idx, region_slide, z, tissue,
-        (w_query, w_key, w_value, w_out, att_v, att_u, att_row, w_class, g_logits), kept,
+        (w_query, w_key, w_value, w_out, att_v, att_u, att_row, w_class.T, g_logits), kept,
     )
     back = exchange(df.reshape(GRP, -1, D2), GRP_AXES).reshape(-1, D2)
-    mine, other = patch_backward(idx, back, tokens, mid, hid, gp, w_embed, w_down, rest)
-    half = (mine.astype(F32) + swap_cores(other).astype(F32)).astype(BF)
-    chunk = add_up(exchange(half, XY))
-    piece = add_up(exchange(chunk.reshape(8, CH_ROWS // 8, 128), Z))
-    chunk = exchange(spread(piece, 8), Z).reshape(CH_ROWS, 128)
-    half = exchange(spread(chunk, HALF), XY)
-    up, down, embed, query, key, value, out, gv, gu, gw = unpack(idx, half, swap_cores(half))
+    mine, other = patch_backward(idx, back, tokens, mid, hid, gp, w_embed.T, w_down, rest)
+    half = add_pair(mine, swap_cores(other))
+    chunk = add_up(exchange(half.reshape(PEERS, -1, 128), ZLXY))
+    chunk = add_over_zh(chunk)
+    half = exchange(spread(chunk, PEERS), ZLXY).reshape(HALF_ROWS, 128)
+    other = swap_cores(half)
+    grads = unpack(idx, other, 4, unpack(idx, half, 3))
+    up, down, embed, query, key, value, out, gv, gu, gw = grads
     return (
-        logits, up, down, embed, query, key, value, out, gv, gu, gw.reshape(D2), g_class,
+        logits, up, down, embed.T, query, key, value, out, gv, gu, gw.reshape(D2), g_class.T,
     )
 
 

time: 184 us -> 166 us (0.902)
  local copies, waits for them, and re-layouts: 23.7 us -> 1.72 us
  Pallas kernels: 27 us -> 38.3 us
  starting transfers between devices: 20.3 us -> 13.5 us
  blocking collectives: 92.1 us -> 89.1 us
    unnamed x72 -> x4, local copies, waits for them, and re-layouts: 22.7 us -> 0.71 us
    ppermute x0 -> x2, waiting for transfers between devices: none -> 9.26 us  [add_over_zh(): x = add_pair(x, lax.ppermute(x, 'zh', [(i, i ^ flip) for i in range(4)]))]
    all_to_all x2 -> x1, starting transfers between devices: 14.6 us -> 7.19 us  [exchange(): return lax.all_to_all(x, axes, split_axis=0, concat_axis=0, tiled=True)]
    all_to_all x2 -> x1, waiting for transfers between devices: 13.3 us -> 6.51 us  [exchange(): return lax.all_to_all(x, axes, split_axis=0, concat_axis=0, tiled=True)]
    pallas_call x1, Pallas kernels: 4.16 us -> 7.67 us  [region_forward(): pl.pallas_call(region_forward_kernel, grid_spec=pltpu.PrefetchScalarGridS...]
    all_to_all x6 -> x5, blocking collectives: 92.1 us -> 89.1 us  [exchange(): return lax.all_to_all(x, axes, split_axis=0, concat_axis=0, tiled=True)]
    pallas_call x1, Pallas kernels: 8.26 us -> 11.2 us  [region_backward(): pl.pallas_call(region_backward_kernel, grid_spec=pltpu.PrefetchScalarGrid...]
    pallas_call x1, Pallas kernels: 6.06 us -> 8.09 us  [patch_backward(): pl.pallas_call(patch_backward_kernel, grid_spec=pltpu.PrefetchScalarGridS...]
  transfers between devices with their start and end apart: 4 -> 5, of which waited for: 4 -> 5; matrix products, arithmetic and copies ran while one was open for 1% -> 0% of each run, Pallas kernels for 0% -> 1%
where the time goes in v2:
time: 166 us; the launch traced here: 165 us
  blocking collectives  89.1 us (54%)
  Pallas kernels  38.3 us (23%)
  waiting for transfers between devices  19.7 us (12%)
  starting transfers between devices  13.5 us (8%)
  other arithmetic  2.11 us (1%)
  local copies, waits for them, and re-layouts  1.72 us (1%)
    all_to_all x5, blocking collectives, exchange(): return lax.all_to_all(x, axes, split_axis=0, concat_axis=0, tiled=True)  89.1 us
    pallas_call x1, Pallas kernels, region_backward(): pl.pallas_call(region_backward_kernel, grid_spec=pltpu.PrefetchScalarGrid...  11.2 us
    ppermute x2, waiting for transfers between devices, add_over_zh(): x = add_pair(x, lax.ppermute(x, 'zh', [(i, i ^ flip) for i in range(4)]))  9.26 us
    pallas_call x1, Pallas kernels, patch_backward(): pl.pallas_call(patch_backward_kernel, grid_spec=pltpu.PrefetchScalarGridS...  8.09 us
    pallas_call x1, Pallas kernels, region_forward(): pl.pallas_call(region_forward_kernel, grid_spec=pltpu.PrefetchScalarGridS...  7.67 us
    all_to_all x1, starting transfers between devices, exchange(): return lax.all_to_all(x, axes, split_axis=0, concat_axis=0, tiled=True)  7.19 us
    pallas_call x1, Pallas kernels, patch_forward(): pl.pallas_call(patch_forward_kernel, grid=(steps,), in_specs=[pl.BlockSpe...  6.74 us
    all_to_all x1, waiting for transfers between devices, exchange(): return lax.all_to_all(x, axes, split_axis=0, concat_axis=0, tiled=True)  6.51 us
  transfers between devices with their start and end apart: 5, of which 5 were waited for; matrix products, arithmetic and copies ran while one was open for 0% of the time, Pallas kernels for 1%

profile of v2, /device:TPU:1, one launch (start us, length us, event | category | flops | bytes accessed | tf_op | source)
XLA Modules:
  0.0 165.2 jit_solution(11633724032505879248)
XLA Ops:
  0.6 6.7 %patch_forward.1 = (bf16[512,192]{1,0:T(8,128)(2,1)}, bf16[512,1536]{1,0:T(8,128)(2,1)}, bf16[512,1536]{1,0:T(8,128)(2,1)}, bf16[512,384]{1,0:T(8,128)(2,1)}) custom-call(bf16[512,384]{1,0:T(8,128)(2,1)} %bitcast.21, bf16[384,1536]{1,0:T(8,128)(2,1)} %wu_ref.1, bf16[1536,384]{1,0:T(8,128)(2,1)} %wd_ref.3, bf16[192,384]{1,0:T(8,128)(2,1)} %bitcast.25), custom_call_target="tpu_custom_call" | custom-call | tf_op jit(solution)/shard_map/patch_forward/pallas_call | solution.py:106
  7.4 7.2 %all-to-all-start = ((bf16[16,32,192]{2,1,0:T(8,128)(2,1)}), bf16[16,32,192]{2,1,0:T(8,128)(2,1)S(1)}, u32[]{:S(2)}, u32[]{:S(2)}) async-start(bf16[16,32,192]{2,1,0:T(8,128)(2,1)} %bitcast.28), calls=%async_computation | async-start | bytes 524288 | tf_op jit(solution)/shard_map/all_to_all | solution.py:599
  14.6 0.7 stack.23.idx_ref
  15.2 6.5 %all-to-all-done = bf16[16,32,192]{2,1,0:T(8,128)(2,1)S(1)} async-done(((bf16[16,32,192]{2,1,0:T(8,128)(2,1)}), bf16[16,32,192]{2,1,0:T(8,128)(2,1)S(1)}, u32[]{:S(2)}, u32[]{:S(2)}) %all-to-all-start) | async-done | bytes 196640 | tf_op jit(solution)/shard_map/all_to_all | solution.py:599
  21.7 0.0 copy-start.1
  21.7 0.7 copy-done.1
  22.4 7.7 %region_forward.1 = (bf16[2,1536,256]{2,1,0:T(8,128)(2,1)}, bf16[2,256,192]{2,1,0:T(8,128)(2,1)}, bf16[2,256,192]{2,1,0:T(8,128)(2,1)}, bf16[2,256,192]{2,1,0:T(...) custom-call(s32[5]{0:T(128)} %stack.23.idx_ref, ...), custom_call_target="tpu_custom_call" | custom-call | tf_op jit(solution)/shard_map/region_forward/pallas_call | solution.py:221
  30.1 13.7 %all_to_all.30 = f32[32,8,128]{2,1,0:T(8,128)S(1)} all-to-all(f32[32,8,128]{2,1,0:T(8,128)} %get-tuple-element.55), channel_id=1, replica_groups=mesh['zl'=2,'x'=4,'c'=2,'zh'=4,'y'=4] {'y','x','c'}, dimensions={0} | all-to-all | bytes 262144 | tf_op jit(solution)/shard_map/all_to_all | solution.py:599
  43.8 14.2 %all_to_all.31.z_ref = f32[8,8,128]{2,1,0:T(8,128)} all-to-all(f32[8,8,128]{2,1,0:T(8,128)S(1)} %broadcast_in_dim.4), channel_id=1, replica_groups=mesh['zl'=2,'x'=4,'c'=2,'zh'=4,'y'=4] {'zh','zl'}, dimensions={0} | all-to-all | bytes 65536 | tf_op jit(solution)/shard_map/all_to_all | solution.py:599
  58.0 11.2 %region_backward.1 = (bf16[16,2,16,192]{3,2,1,0:T(8,128)(2,1)}, bf16[2,1152,128]{2,1,0:T(8,128)(2,1)}, f32[4,3]{1,0:T(4,128)}, f32[3,192]{1,0:T(4,128)}) custom-call(s32[5]{0:T(128)} %stack.23.idx_ref, s32[512]{0:T(512)} %slide_ref.3, f32[8,8,128]{2,1,0:T(8,128)} %all_to_all.31.z_ref, s32[512,256]{1,0:T(8,128)} %tis_ref.3, bf16[192,192]{1,0:T(8,128)(2,1)} %wq_in.3, ...), custom_call_target="tpu_custom_call" | custom-call | tf_op jit(solution)/shard_map/region_backward/pallas_call | solution.py:376
  69.2 13.0 %all_to_all.32 = bf16[16,32,192]{2,1,0:T(8,128)(2,1)} all-to-all(bf16[16,32,192]{2,1,0:T(8,128)(2,1)} %bitcast.29), channel_id=1, replica_groups=mesh['zl'=2,'x'=4,'c'=2,'zh'=4,'y'=4] {'zl','x','c'}, dimensions={0} | all-to-all | bytes 393216 | tf_op jit(solution)/shard_map/all_to_all | solution.py:599
  82.2 8.1 %patch_backward.1 = (bf16[6144,128]{1,0:T(8,128)(2,1)}, bf16[6144,128]{1,0:T(8,128)(2,1)}) custom-call(s32[5]{0:T(128)} %stack.23.idx_ref, bf16[512,192]{1,0:T(8,128)(2,1)} %bitcast.24, bf16[512,384]{1,0:T(8,128)(2,1)} %bitcast.22, bf16[512,384]{1,0:T(8,128)(2,1)} %get-tuple-element.69.mid_ref, bf16[512,1536]{1,0:T(8,128)(2,1)} %get-tuple-element.70.hid_ref, ...), custom_call_target="tpu_custom_call" | custom-call | tf_op jit(solution)/shard_map/patch_backward/pallas_call | solution.py:507
  90.3 1.1 collective-permute-start
  91.4 3.2 %collective-permute-done = bf16[6144,128]{1,0:T(8,128)(2,1)S(1)} collective-permute-done((bf16[6144,128]{1,0:T(8,128)(2,1)}, bf16[6144,128]{1,0:T(8,128)(2,1)S(1)}, u32[]{:S(2)}, u32[]{:S(2)}) %collective-permute-start) | collective-permute-done | bytes 1572896 | tf_op jit(solution)/shard_map/ppermute | solution.py:603
  94.6 1.8 %add_convert_fusion = bf16[6144,128]{1,0:T(8,128)(2,1)S(1)} fusion(bf16[6144,128]{1,0:T(8,128)(2,1)S(1)} %collective-permute-done, bf16[6144,128]{1,0:T(8,128)(2,1)} %get-tuple-element.73), kind=kLoop, calls=%fused_computation | loop fusion | flops 3145728 | bytes 4718592 | tf_op jit(solution)/shard_map/convert_element_type | solution.py:611
  96.4 24.5 %all_to_all.33 = bf16[32,192,128]{2,1,0:T(8,128)(2,1)S(1)} all-to-all(bf16[32,192,128]{2,1,0:T(8,128)(2,1)S(1)} %bitcast.20), channel_id=1, replica_groups=mesh['zl'=2,'x'=4,'c'=2,'zh'=4,'y'=4] {'y','zl','x'}, dimensions={0} | all-to-all | bytes 3145728 | tf_op jit(solution)/shard_map/all_to_all | solution.py:599
  120.9 0.2 reduce_sum.22
  121.1 0.2 collective-permute-start.1
  121.4 4.2 %collective-permute-done.1 = bf16[192,128]{1,0:T(8,128)(2,1)S(1)} collective-permute-done((bf16[192,128]{1,0:T(8,128)(2,1)S(1)}, bf16[192,128]{1,0:T(8,128)(2,1)S(1)}, u32[]{:S(2)}, u32[]{:S(2)}) %collective-permute-start.1) | collective-permute-done | bytes 49184 | tf_op jit(solution)/shard_map/ppermute | solution.py:616
  125.6 0.1 collective-permute-start.2
  125.7 5.0 %collective-permute-done.2 = bf16[192,128]{1,0:T(8,128)(2,1)S(1)} collective-permute-done((bf16[192,128]{1,0:T(8,128)(2,1)S(1)}, bf16[192,128]{1,0:T(8,128)(2,1)S(1)}, u32[]{:S(2)}, u32[]{:S(2)}) %collective-permute-start.2) | collective-permute-done | bytes 49184 | tf_op jit(solution)/shard_map/ppermute | solution.py:616
  130.8 0.3 broadcast_in_dim.5
  131.1 0.0 copy-start
  131.1 23.8 %all_to_all.34 = bf16[32,192,128]{2,1,0:T(8,128)(2,1)S(1)} all-to-all(bf16[32,192,128]{2,1,0:T(8,128)(2,1)S(1)} %broadcast_in_dim.5), channel_id=1, replica_groups=mesh['zl'=2,'x'=4,'c'=2,'zh'=4,'y'=4] {'y','zl','x'}, dimensions={0} | all-to-all | bytes 3145728 | tf_op jit(solution)/shard_map/all_to_all | solution.py:599
  155.0 4.9 %collective-permute-start.3 = (bf16[6144,128]{1,0:T(8,128)(2,1)S(1)}, bf16[6144,128]{1,0:T(8,128)(2,1)S(1)}, u32[]{:S(2)}, u32[]{:S(2)}) collective-permute-start(bf16[6144,128]{1,0:T(8,128)(2,1)S(1)} %bitcast.18), channel_id=1, source_target_pairs={{0,16},{16,0},{1,17},{17,1},{2,18},{18,2},{3,19},{19,3},{4,20},{20... | collective-permute-start | bytes 4718600 | tf_op jit(solution)/shard_map/ppermute | solution.py:603
  159.8 0.0 copy-done
  159.8 2.3 %unpack.2 = (f32[384,1536]{1,0:T(8,128)}, f32[1536,384]{1,0:T(8,128)}, f32[192,384]{1,0:T(8,128)}, f32[192,192]{1,0:T(8,128)}, f32[192,192]{1,0:T(8,128)}, /*ind...) custom-call(s32[5]{0:T(128)S(1)} %copy-done, ...), custom_call_target="tpu_custom_call" | custom-call | tf_op jit(solution)/shard_map/unpack/pallas_call | solution.py:564
  162.2 0.7 collective-permute-done.3.src_ref
  162.9 2.3 %unpack.3 = (f32[384,1536]{1,0:T(8,128)}, f32[1536,384]{1,0:T(8,128)}, f32[192,384]{1,0:T(8,128)}, f32[192,192]{1,0:T(8,128)}, f32[192,192]{1,0:T(8,128)}, /*ind...) custom-call(s32[5]{0:T(128)S(1)} %copy-done, ...), custom_call_target="tpu_custom_call", output_to_operand_aliasing={{0}: (2, {}), {1}: (3, {}), {2}: (4, {}), {3}: (5, {}), {4}... | custom-call | tf_op jit(solution)/shard_map/unpack/pallas_call | solution.py:564
  (4 shorter events, 0.1 us)
Async XLA Ops:
  7.4 14.4 %all-to-all-start = ((bf16[16,32,192]{2,1,0:T(8,128)(2,1)}), bf16[16,32,192]{2,1,0:T(8,128)(2,1)S(1)}, u32[]{:S(2)}, u32[]{:S(2)}) async-start(bf16[16,32,192]{2,1,0:T(8,128)(2,1)} %bitcast.28), calls=%async_computation | async-start | bytes 524288 | tf_op jit(solution)/shard_map/all_to_all | solution.py:599
  21.7 0.7 copy-start.1
  90.3 4.3 %collective-permute-start = (bf16[6144,128]{1,0:T(8,128)(2,1)}, bf16[6144,128]{1,0:T(8,128)(2,1)S(1)}, u32[]{:S(2)}, u32[]{:S(2)}) collective-permute-start(bf16[6144,128]{1,0:T(8,128)(2,1)} %get-tuple-element.74), channel_id=1, source_target_pairs={{0,16},{16,0},{1,17},{17,1},{2,18},{18,2},{3,19},{19,3},{4,20},{20... | collective-permute-start | bytes 4718600 | tf_op jit(solution)/shard_map/ppermute | solution.py:603
  121.1 4.4 %collective-permute-start.1 = (bf16[192,128]{1,0:T(8,128)(2,1)S(1)}, bf16[192,128]{1,0:T(8,128)(2,1)S(1)}, u32[]{:S(2)}, u32[]{:S(2)}) collective-permute-start(bf16[192,128]{1,0:T(8,128)(2,1)S(1)} %reduce_sum.22), channel_id=1, source_target_pairs={{0,4},{4,0},{8,12},{12,8},{1,5},{5,1},{9,13},{13,9},{2,6},{6,2},{1... | collective-permute-start | bytes 147464 | tf_op jit(solution)/shard_map/ppermute | solution.py:616
  125.6 5.1 %collective-permute-start.2 = (bf16[192,128]{1,0:T(8,128)(2,1)S(1)}, bf16[192,128]{1,0:T(8,128)(2,1)S(1)}, u32[]{:S(2)}, u32[]{:S(2)}) collective-permute-start(bf16[192,128]{1,0:T(8,128)(2,1)S(1)} %add_convert_fusion.2), channel_id=1, source_target_pairs={{0,12},{4,8},{8,4},{12,0},{1,13},{5,9},{9,5},{13,1},{2,14},{6,10},... | collective-permute-start | bytes 147464 | tf_op jit(solution)/shard_map/ppermute | solution.py:616
  131.1 28.7 %copy-start = (s32[5]{0:T(128)S(1)}, s32[5]{0:T(128)}, u32[]{:S(2)}) copy-start(s32[5]{0:T(128)} %stack.23.idx_ref) | copy-start | bytes 64
  155.0 7.9 %collective-permute-start.3 = (bf16[6144,128]{1,0:T(8,128)(2,1)S(1)}, bf16[6144,128]{1,0:T(8,128)(2,1)S(1)}, u32[]{:S(2)}, u32[]{:S(2)}) collective-permute-start(bf16[6144,128]{1,0:T(8,128)(2,1)S(1)} %bitcast.18), channel_id=1, source_target_pairs={{0,16},{16,0},{1,17},{17,1},{2,18},{18,2},{3,19},{19,3},{4,20},{20... | collective-permute-start | bytes 4718600 | tf_op jit(solution)/shard_map/ppermute | solution.py:603

commit v3 on v2

--- a/solution.py
+++ b/solution.py
@@ -241,7 +241,7 @@
                 row8(D2),
                 row8(D2),
                 row8(128),
-                pl.BlockSpec((PEERS, 8, 128), lambda r, *_: (0, 0, 0)),
+                pl.BlockSpec((GRP, 8, 128), lambda r, *_: (0, 0, 0)),
             ],
             scratch_shapes=weight_scratch(),
         ),
@@ -253,7 +253,7 @@
             jax.ShapeDtypeStruct((8, D2), F32),
             jax.ShapeDtypeStruct((8, D2), F32),
             jax.ShapeDtypeStruct((8, 128), F32),
-            jax.ShapeDtypeStruct((PEERS, 8, 128), F32),
+            jax.ShapeDtypeStruct((GRP, 8, 128), F32),
         ],
         compiler_params=params(60),
         name="region_forward",
@@ -261,25 +261,17 @@
 
 
 def region_backward_kernel(
-    idx_ref, slide_ref, z_ref, tis_ref, wq_in, wk_in, wv_in, wo_in, av_in, au_in, aw_ref,
+    idx_ref, slide_ref, tis_ref, wq_in, wk_in, wv_in, wo_in, av_in, au_in, aw_ref,
     wc_ref, gl_ref,
     p_ref, x_ref, q_ref, k_ref, v_ref, se_ref, asum_ref, reg_ref, tanh_ref, gate_ref, w_ref,
-    df_ref, rest_ref, logits_ref, gc_ref,
-    dm_s, da_s, kt_s, dqt_s, gq_s, gk_s, gv_s,
+    df_ref, grad_ref, rows_ref,
+    da_s, kt_s, dqt_s,
     wq_ref, wk_ref, wv_ref, wo_ref, av_ref, au_ref, wsems,
 ):
     r = pl.program_id(0)
     trow = tissue_row(idx_ref, tis_ref, r)
     tcol = column_of(trow, D2)
 
-    def put(slot, grad, fill=None):
-        for half in range(2):
-            rows = grad[96 * half : 96 * half + 96]
-            rest_ref[half, pl.ds(192 * slot, 96), :] = rows[:, :128].astype(BF)
-            tail = jnp.zeros((96, 64), F32) if fill is None else fill
-            high = jnp.concatenate([rows[:, 128:], tail], axis=1)
-            rest_ref[half, pl.ds(192 * slot + 96, 96), :] = high.astype(BF)
-
     @pl.when(r == 0)
     def _():
         fetch_all(
@@ -287,27 +279,16 @@
             (wq_ref, wk_ref, wv_ref, wo_ref, av_ref, au_ref),
             wsems,
         )
-        z = jnp.sum(z_ref[...], axis=0)
-        low, high = z[0:SLIDES], z[SLIDES:]
-        total = high[:, 64:65]
-        summary = jnp.concatenate([low, high[:, :64]], axis=1) / total
-        wc = wc_ref[...]
-        gl = gl_ref[...]
-        logits_ref[...] = nt(summary, wc, HIGHEST)
-        gc_ref[...] = tn(gl, summary, HIGHEST)
-        d_summary = nn(gl, wc, HIGHEST)
+        d_summary = nn(gl_ref[...], wc_ref[...], HIGHEST)
         slot = lax.broadcasted_iota(jnp.int32, (SLIDES, 1), 0)
         row = lax.broadcasted_iota(jnp.int32, (8, 1), 0)
         d_own = jnp.zeros((8, D2), F32)
-        own_summary = jnp.zeros((8, D2), F32)
-        own_total = jnp.ones((8, 1), F32)
         count = jnp.ones((8, 1), F32)
         for i in range(OWN):
             mine = slot == slide_ref[idx_ref[0] + i]
-            pick = lambda a: jnp.sum(jnp.where(mine, a, 0.0), axis=0, keepdims=True)
-            d_own = jnp.where(row == i, pick(d_summary), d_own)
-            own_summary = jnp.where(row == i, pick(summary), own_summary)
-            own_total = jnp.where(row == i, pick(total), own_total)
+            d_own = jnp.where(
+                row == i, jnp.sum(jnp.where(mine, d_summary, 0.0), axis=0, keepdims=True), d_own
+            )
             t_i = tissue_row(idx_ref, tis_ref, i)
             count = jnp.where(
                 row == i, jnp.maximum(jnp.sum(t_i, axis=1, keepdims=True), 1.0), count
@@ -315,63 +296,59 @@
         region = reg_ref[:, pl.ds(0, D2)]
         tanh_part = tanh_ref[...]
         gate_part = gate_ref[...]
-        share = jnp.where(row < OWN, w_ref[:, 0:1] / own_total, 0.0)
-        d_score = share * jnp.sum(d_own * (region - own_summary), axis=1, keepdims=True)
-        d_gated = d_score * aw_ref[...]
-        d_pre_v = d_gated * gate_part * (1.0 - tanh_part * tanh_part)
-        d_pre_u = d_gated * tanh_part * gate_part * (1.0 - gate_part)
-        d_region = (
-            share * d_own + nt(d_pre_v, av_ref[...], HIGHEST) + nt(d_pre_u, au_ref[...], HIGHEST)
+        pre_v = aw_ref[...] * gate_part * (1.0 - tanh_part * tanh_part)
+        pre_u = aw_ref[...] * tanh_part * gate_part * (1.0 - gate_part)
+        second = nt(pre_v, av_ref[...], HIGHEST) + nt(pre_u, au_ref[...], HIGHEST)
+        own = jnp.sum(d_own * region, axis=1, keepdims=True)
+        dm = (d_own / count, second / count)
+        kept = (
+            region, asum_ref[...], tanh_part * gate_part, pre_v, pre_u, dm[0], dm[1],
+            jnp.broadcast_to(w_ref[:, 0:1], (8, D2)), jnp.broadcast_to(own, (8, D2)),
         )
-        dm = (d_region / count).astype(BF)
-        dm_s[...] = dm.astype(F32)
-        da_s[...] = nt(dm, wo_ref[...])
-        put(3, tn(asum_ref[...], dm.astype(F32), HIGHEST))
-        put(4, tn(region, d_pre_v, HIGHEST))
-        g_aw = tn(tanh_part * gate_part, jnp.broadcast_to(d_score, (8, 64)), HIGHEST)
-        lane = lax.broadcasted_iota(jnp.int32, (96, 64), 1)
-        put(5, tn(region, d_pre_u, HIGHEST), jnp.where(lane == 0, g_aw[:96], g_aw[96:]))
-        gq_s[...] = jnp.zeros_like(gq_s)
-        gk_s[...] = jnp.zeros_like(gk_s)
-        gv_s[...] = jnp.zeros_like(gv_s)
+        for i, value in enumerate(kept):
+            rows_ref[pl.ds(8 * i, 8), :] = value
+        for j in range(2):
+            da_s[pl.ds(8 * j, 8), :] = nt(dm[j].astype(BF), wo_ref[...])
 
     x = x_ref[0]
     q = q_ref[0].astype(F32)
     v = v_ref[0]
     kt_s[...] = k_ref[0].astype(F32).T.astype(BF)
-    dm = dm_s[pl.ds(r, 1), :]
-    da = da_s[pl.ds(r, 1), :].astype(BF).astype(F32)
-    da_col = jnp.broadcast_to(da, (128, D2)).T
-    dk = jnp.zeros((PATCH, D2), F32)
+    dm = [rows_ref[pl.ds(8 * (5 + j) + r, 1), :] for j in range(2)]
+    da = [da_s[pl.ds(8 * j + r, 1), :].astype(BF).astype(F32) for j in range(2)]
+    da_col = jnp.concatenate([jnp.broadcast_to(d, (128, D2)) for d in da], axis=0).T
+    dk = [jnp.zeros((PATCH, D2), F32) for _ in range(2)]
     for h in range(HEADS):
-        one_head = (da_col * head_mask(h, (D2, 1), 0)).astype(BF)
-        e = nn(v, one_head)
-        e = jnp.concatenate([e, e], axis=1)
+        e = nn(v, (da_col * head_mask(h, (D2, 1), 0)).astype(BF))
         pt = p_ref[0, pl.ds(h * PATCH, PATCH), :].astype(F32)
-        pe = pt * e
-        ds = (pe - pt * jnp.sum(pe, axis=0, keepdims=True)).astype(BF)
-        dk = dk + nn(ds, (q * head_mask(h, (1, D2), 1)).astype(BF))
-        dqt_s[pl.ds(h * HEAD_DIM, HEAD_DIM), :] = nn(kt_s[pl.ds(h * HEAD_DIM, HEAD_DIM), :], ds)
-    dq = (dqt_s[...] * (trow * SCALE)).T.astype(BF)
-    dk = (dk * SCALE).astype(BF)
-    dv = (se_ref[0] * da).astype(BF)
+        q_head = (q * head_mask(h, (1, D2), 1)).astype(BF)
+        k_head = kt_s[pl.ds(h * HEAD_DIM, HEAD_DIM), :]
+        for j in range(2):
+            e_j = e[:, 128 * j : 128 * j + 128]
+            pe = pt * jnp.concatenate([e_j, e_j], axis=1)
+            ds = (pe - pt * jnp.sum(pe, axis=0, keepdims=True)).astype(BF)
+            dk[j] = dk[j] + nn(ds, q_head)
+            dqt_s[j, pl.ds(h * HEAD_DIM, HEAD_DIM), :] = nn(k_head, ds)
     xt = x.astype(F32).T.astype(BF)
-    gq_s[...] += nn(xt, dq)
-    gk_s[...] += nn(xt, dk)
-    gv_s[...] += nn(xt, dv)
-    d_flat = dm + nt(dq, wq_ref[...]) + nt(dk, wk_ref[...]) + nt(dv, wv_ref[...])
-    df_ref[...] = (tcol * d_flat).astype(BF).reshape(df_ref.shape)
-
-    @pl.when(r == OWN - 1)
-    def _():
-        put(0, gq_s[...])
-        put(1, gk_s[...])
-        put(2, gv_s[...])
-
-
-def region_backward(idx, slide, z, tissue, weights, kept):
+    for j in range(2):
+        dq = (dqt_s[j] * (trow * SCALE)).T.astype(BF)
+        dk_j = (dk[j] * SCALE).astype(BF)
+        dv = (se_ref[0] * da[j]).astype(BF)
+        grad_ref[0, 0, j] = nn(xt, dq)
+        grad_ref[0, 1, j] = nn(xt, dk_j)
+        grad_ref[0, 2, j] = nn(xt, dv)
+        d_flat = dm[j] + nt(dq, wq_ref[...]) + nt(dk_j, wk_ref[...]) + nt(dv, wv_ref[...])
+        d_flat = (tcol * d_flat).astype(BF).reshape(GRP, PATCH // GRP, D2)
+        df_ref[:, j, :, pl.ds(0, D2)] = d_flat
+        df_ref[:, j, :, pl.ds(D2, 64)] = jnp.zeros((GRP, PATCH // GRP, 64), BF)
+
+
+BLOCKS = 2 * OWN + 1
+
+
+def region_backward(idx, slide, tissue, weights, kept):
     sq = pl.BlockSpec(memory_space=pltpu.HBM)
-    row8 = lambda width: pl.BlockSpec((8, width), lambda r, *_: (0, 0))
+    whole = lambda rows, width: pl.BlockSpec((rows, width), lambda r, *_: (0, 0))
     per_region = lambda rows, width: pl.BlockSpec((1, rows, width), lambda r, *_: (r, 0, 0))
     return pl.pallas_call(
         region_backward_kernel,
@@ -379,59 +356,169 @@
             num_scalar_prefetch=2,
             grid=(OWN,),
             in_specs=[
-                pl.BlockSpec((8, 8, 128), lambda r, *_: (0, 0, 0)),
                 pl.BlockSpec((8, PATCH), lambda r, idx, _: (idx[2], 0)),
                 sq, sq, sq, sq, sq, sq,
-                pl.BlockSpec((1, D2), lambda r, *_: (0, 0)),
-                pl.BlockSpec((3, D2), lambda r, *_: (0, 0)),
-                pl.BlockSpec((SLIDES, 3), lambda r, *_: (0, 0)),
+                whole(1, D2),
+                whole(3, D2),
+                whole(SLIDES, 3),
                 per_region(HEADS * PATCH, PATCH),
                 per_region(PATCH, D2),
                 per_region(PATCH, D2),
                 per_region(PATCH, D2),
                 per_region(PATCH, D2),
                 per_region(PATCH, D2),
-                row8(D2),
-                row8(PATCH),
-                row8(D2),
-                row8(D2),
-                row8(128),
+                whole(8, D2),
+                whole(8, PATCH),
+                whole(8, D2),
+                whole(8, D2),
+                whole(8, 128),
             ],
             out_specs=[
-                pl.BlockSpec((GRP, 1, PATCH // GRP, D2), lambda r, *_: (0, r, 0, 0)),
-                pl.BlockSpec((2, REST_ROWS, 128), lambda r, *_: (0, 0, 0)),
-                pl.BlockSpec((SLIDES, 3), lambda r, *_: (0, 0)),
-                pl.BlockSpec((3, D2), lambda r, *_: (0, 0)),
+                pl.BlockSpec((GRP, 2, PATCH // GRP, PATCH), lambda r, *_: (0, r, 0, 0)),
+                pl.BlockSpec((1, 3, 2, D2, D2), lambda r, *_: (r, 0, 0, 0, 0)),
+                whole(72, D2),
             ],
             scratch_shapes=[
-                pltpu.VMEM((8, D2), F32),
-                pltpu.VMEM((8, D2), F32),
+                pltpu.VMEM((16, D2), F32),
                 pltpu.VMEM((D2, PATCH), BF),
-                pltpu.VMEM((D2, PATCH), F32),
-                pltpu.VMEM((D2, D2), F32),
-                pltpu.VMEM((D2, D2), F32),
-                pltpu.VMEM((D2, D2), F32),
+                pltpu.VMEM((2, D2, PATCH), F32),
             ] + weight_scratch(),
         ),
         out_shape=[
-            jax.ShapeDtypeStruct((GRP, OWN, PATCH // GRP, D2), BF),
-            jax.ShapeDtypeStruct((2, REST_ROWS, 128), BF),
-            jax.ShapeDtypeStruct((SLIDES, 3), F32),
-            jax.ShapeDtypeStruct((3, D2), F32),
+            jax.ShapeDtypeStruct((GRP, BLOCKS, PATCH // GRP, PATCH), BF),
+            jax.ShapeDtypeStruct((OWN, 3, 2, D2, D2), F32),
+            jax.ShapeDtypeStruct((72, D2), F32),
         ],
         compiler_params=params(60),
+        cost_estimate=pl.CostEstimate(
+            flops=4_000_000_000, bytes_accessed=20_000_000, transcendentals=0
+        ),
         name="region_backward",
-    )(idx, slide, z, tissue, *weights, *kept)
+    )(idx, slide, tissue, *weights, *kept)
+
+
+def split_three(x):
+    parts = []
+    for _ in range(3):
+        top = x.astype(BF).astype(F32)
+        parts.append(top)
+        x = x - top
+    return parts
+
+
+def join_sums_kernel(z_ref, rows_ref, df_ref, out_ref, ext, wide, sem):
+    z = jnp.sum(z_ref[...], axis=0)
+    z = jnp.concatenate([z[0:SLIDES], z[SLIDES:]], axis=1)
+    lane = lax.broadcasted_iota(jnp.int32, (1, PATCH), 1) // 64
+    scalars = jnp.zeros((1, PATCH), F32)
+    for i in range(OWN):
+        scalars = jnp.where(lane == 2 * i, rows_ref[56 + i : 57 + i, 0:1], scalars)
+        scalars = jnp.where(lane == 2 * i + 1, rows_ref[64 + i : 65 + i, 0:1], scalars)
+    ext[...] = jnp.zeros_like(ext)
+    for i, (part, tops) in enumerate(zip(split_three(z), split_three(scalars))):
+        ext[pl.ds(4 * i, 4), :] = part
+        ext[pl.ds(12 + i, 1), :] = tops
+    wide[...] = jnp.broadcast_to(ext[...].astype(BF)[None], wide.shape)
+    copy = pltpu.make_async_copy(wide, out_ref.at[:, BLOCKS - 1], sem)
+    copy.start()
+    copy.wait()
+
+
+def join_sums(z, rows, df):
+    return pl.pallas_call(
+        join_sums_kernel,
+        in_specs=[
+            pl.BlockSpec(memory_space=pltpu.VMEM),
+            pl.BlockSpec(memory_space=pltpu.VMEM),
+            pl.BlockSpec(memory_space=pl.ANY),
+        ],
+        out_specs=pl.BlockSpec(memory_space=pl.ANY),
+        out_shape=jax.ShapeDtypeStruct(df.shape, df.dtype),
+        scratch_shapes=[
+            pltpu.VMEM((16, PATCH), F32),
+            pltpu.VMEM((GRP, 16, PATCH), BF),
+            pltpu.SemaphoreType.DMA,
+        ],
+        input_output_aliases={2: 0},
+        compiler_params=params(16),
+        name="join_sums",
+    )(z, rows, df)
 
 
 STEPS4 = 4
 FB4 = F1 // STEPS4
 
 
+def put_rest(pack, slot, grad, fill=None):
+    at = REST_AT + 192 * slot
+    if not isinstance(slot, int):
+        at = pl.multiple_of(at, 64)
+    for half in range(2):
+        rows = grad[96 * half : 96 * half + 96]
+        pack[half, pl.ds(at, 96), :] = rows[:, :128].astype(BF)
+        tail = jnp.zeros((96, 64), F32) if fill is None else fill
+        high = jnp.concatenate([rows[:, 128:], tail], axis=1)
+        pack[half, pl.ds(at + 96, 96), :] = high.astype(BF)
+
+
+def finish_slides(
+    idx_ref, slide_ref, back_ref, rows_ref, wc_ref, gl_ref, logits_ref, gc_ref, df_s, pq_s, pack
+):
+    ext = back_ref[:, BLOCKS - 1].astype(F32)
+    sums = jnp.sum(ext, axis=0)
+    sums = sums[0:4] + sums[4:8] + sums[8:12]
+    total = sums[:, D2 : D2 + 1]
+    summary = sums[:, :D2] / total
+    wc = wc_ref[...]
+    gl = gl_ref[...]
+    logits_ref[...] = nt(summary, wc, HIGHEST)
+    gc_ref[...] = tn(gl, summary, HIGHEST)
+    along = jnp.sum(nn(gl, wc, HIGHEST) * summary, axis=1, keepdims=True)
+
+    def of_slide(column, s):
+        out = column[SLIDES - 1 : SLIDES]
+        for i in range(SLIDES - 1):
+            out = jnp.where(s == i, column[i : i + 1], out)
+        return out
+
+    def factors(w, a, s):
+        share = w / of_slide(total, s)
+        return share, share * (a - of_slide(along, s))
+
+    for src in range(GRP):
+        scalars = ext[src, 12:13] + ext[src, 13:14] + ext[src, 14:15]
+        for i in range(OWN):
+            w = scalars[:, 128 * i : 128 * i + 1]
+            a = scalars[:, 128 * i + 64 : 128 * i + 65]
+            p, q = factors(w, a, slide_ref[idx_ref[5] + OWN * src + i])
+            f = [back_ref[src, 2 * i + j].astype(F32)[:, :D2] for j in range(2)]
+            df_s[pl.ds(32 * src + 16 * i, 16), :] = (p * f[0] + q * f[1]).astype(BF)
+
+    kept = [rows_ref[pl.ds(8 * i, 8), :] for i in range(9)]
+    region, asum, gated, pre_v, pre_u, dm0, dm1, w_own, a_own = kept
+    row = lax.broadcasted_iota(jnp.int32, (8, 1), 0)
+    p_own = jnp.zeros((8, 1), F32)
+    q_own = jnp.zeros((8, 1), F32)
+    for i in range(OWN):
+        p, q = factors(w_own[i : i + 1, 0:1], a_own[i : i + 1, 0:1], slide_ref[idx_ref[0] + i])
+        p_own = jnp.where(row == i, p, p_own)
+        q_own = jnp.where(row == i, q, q_own)
+    pq_s[0] = jnp.broadcast_to(p_own, (8, 128))
+    pq_s[1] = jnp.broadcast_to(q_own, (8, 128))
+    put_rest(pack, 3, tn(asum, p_own * dm0 + q_own * dm1, HIGHEST))
+    put_rest(pack, 4, tn(region, q_own * pre_v, HIGHEST))
+    g_aw = tn(gated, jnp.broadcast_to(q_own, (8, 64)), HIGHEST)
+    lane = lax.broadcasted_iota(jnp.int32, (96, 64), 1)
+    put_rest(
+        pack, 5, tn(region, q_own * pre_u, HIGHEST), jnp.where(lane == 0, g_aw[:96], g_aw[96:])
+    )
+
+
 def patch_backward_kernel(
-    idx_ref, df_ref, x_ref, mid_ref, hid_ref, gp_ref, we_ref, wd_ref, rest_ref,
-    mine_ref, other_ref,
-    pack, dmid_s, sems,
+    idx_ref, slide_ref, back_ref, x_ref, mid_ref, hid_ref, gp_ref, we_ref, wd_ref, grad_ref,
+    rows_ref, wc_ref, gl_ref,
+    mine_ref, other_ref, logits_ref, gc_ref,
+    pack, dmid_s, df_s, pq_s, sems,
 ):
     step = pl.program_id(0)
     core = idx_ref[3]
@@ -456,17 +543,26 @@
 
     @pl.when(step == 0)
     def _():
-        df = df_ref[...]
+        finish_slides(
+            idx_ref, slide_ref, back_ref, rows_ref, wc_ref, gl_ref, logits_ref, gc_ref,
+            df_s, pq_s, pack,
+        )
+        df = df_s[...]
         dmid_s[...] = nn(df, we_ref[...]).astype(BF)
         g_embed = tn(df, mid_ref[...]).astype(BF)
         for half in range(2):
-            pack[half, pl.ds(REST_AT, REST_ROWS), :] = rest_ref[half]
             for l in range(3):
                 block = g_embed[96 * half : 96 * half + 96, 128 * l : 128 * l + 128]
                 pack[half, pl.ds(EMBED_AT + 96 * l, 96), :] = block
             pack[half, pl.ds(PAD_AT, 96), :] = jnp.zeros((96, 128), BF)
-        for copy in rest_copies():
-            copy.start()
+
+    @pl.when(step > 0)
+    def _():
+        grad = jnp.zeros((D2, D2), F32)
+        for i in range(OWN):
+            for j in range(2):
+                grad = grad + pq_s[j, i : i + 1, 0:1] * grad_ref[i, 0, j]
+        put_rest(pack, step - 1, grad)
 
     dmid = dmid_s[...]
     d_pre = (nt(dmid, wd_ref[...]) * gp_ref[...].astype(F32)).astype(BF)
@@ -475,14 +571,15 @@
         for l in range(3):
             block = g_up[192 * half : 192 * half + 192, 128 * l : 128 * l + 128]
             pack[half, pl.ds(pl.multiple_of(576 * step + 192 * l, 64), 192), :] = block
-    for copy in up_copies(step):
-        copy.start()
     g_down = tn(hid_ref[...], dmid).astype(BF)
     at = DOWN_AT + 1152 * lax.rem(step, 2)
     for l in range(3):
         rows = pl.ds(pl.multiple_of(at + 384 * l, 128), 384)
         pack[step // 2, rows, :] = g_down[:, 128 * l : 128 * l + 128]
 
+    for copy in up_copies(step):
+        copy.start()
+
     @pl.when(step // 2 == core)
     def _():
         down_copy(step, mine_ref).start()
@@ -493,6 +590,8 @@
 
     @pl.when(step == pl.num_programs(0) - 1)
     def _():
+        for copy in rest_copies():
+            copy.start()
         for copy in rest_copies():
             copy.wait()
         for i in range(STEPS4):
@@ -501,41 +600,57 @@
             down_copy(i, mine_ref).wait()
 
 
-def patch_backward(idx, df, tokens, mid, hid, gp, w_embed, w_down, rest):
+def patch_backward(
+    idx, slide, back, tokens, mid, hid, gp, w_embed, w_down, grad, kept_rows, w_class, g_logits
+):
     rows = tokens.shape[0]
     whole = lambda i, *_: (0, 0)
     return pl.pallas_call(
         patch_backward_kernel,
         grid_spec=pltpu.PrefetchScalarGridSpec(
-            num_scalar_prefetch=1,
+            num_scalar_prefetch=2,
             grid=(STEPS4,),
             in_specs=[
-                pl.BlockSpec((rows, D2), whole),
+                pl.BlockSpec(back.shape, lambda i, *_: (0, 0, 0, 0)),
                 pl.BlockSpec((rows, D1), whole),
                 pl.BlockSpec((rows, D1), whole),
                 pl.BlockSpec((rows, FB4), lambda i, *_: (0, i)),
                 pl.BlockSpec((rows, FB4), lambda i, *_: (0, i)),
                 pl.BlockSpec((D2, D1), whole),
                 pl.BlockSpec((FB4, D1), lambda i, *_: (i, 0)),
-                pl.BlockSpec((2, REST_ROWS, 128), lambda i, *_: (0, 0, 0)),
+                pl.BlockSpec(
+                    (OWN, 1, 2, D2, D2), lambda i, *_: (0, jnp.maximum(i - 1, 0), 0, 0, 0)
+                ),
+                pl.BlockSpec((72, D2), whole),
+                pl.BlockSpec((3, D2), whole),
+                pl.BlockSpec((SLIDES, 3), whole),
             ],
             out_specs=[
                 pl.BlockSpec(memory_space=pl.ANY),
                 pl.BlockSpec(memory_space=pl.ANY),
+                pl.BlockSpec((SLIDES, 3), whole),
+                pl.BlockSpec((3, D2), whole),
             ],
             scratch_shapes=[
                 pltpu.VMEM((2, HALF_ROWS, 128), BF),
                 pltpu.VMEM((rows, D1), BF),
+                pltpu.VMEM((rows, D2), BF),
+                pltpu.VMEM((2, 8, 128), F32),
                 pltpu.SemaphoreType.DMA((14,)),
             ],
         ),
         out_shape=[
             jax.ShapeDtypeStruct((HALF_ROWS, 128), BF),
             jax.ShapeDtypeStruct((HALF_ROWS, 128), BF),
-        ],
-        compiler_params=params(58),
+            jax.ShapeDtypeStruct((SLIDES, 3), F32),
+            jax.ShapeDtypeStruct((3, D2), F32),
+        ],
+        compiler_params=params(44),
         name="patch_backward",
-    )(idx, df, tokens, mid, hid, gp, w_embed, w_down, rest)
+    )(
+        idx, slide, back, tokens, mid, hid, gp, w_embed, w_down, grad, kept_rows, w_class,
+        g_logits,
+    )
 
 
 def unpack_kernel(idx_ref, src_ref, *refs):
@@ -591,8 +706,6 @@
 GRP_AXES = ("zl", "x", "c")
 DEV_AXES = ("zh", "y")
 ZLXY = ("y", "zl", "x")
-XYC = ("y", "x", "c")
-Z = ("zh", "zl")
 
 
 def exchange(x, axes):
@@ -629,7 +742,7 @@
     dev = lax.axis_index(DEV_AXES)
     core = lax.axis_index("c")
     first = (dev * GRP + grp) * OWN
-    idx = jnp.stack([first, first % 8, first // 8, core, 1 - core]).astype(jnp.int32)
+    idx = jnp.stack([first, first % 8, first // 8, core, 1 - core, dev * GRP * OWN]).astype(jnp.int32)
     tokens = patches.reshape(-1, D1)
     att_row = att_w.reshape(1, D2)
     feat, hid, gp, mid = patch_forward(tokens, w_up, w_down, w_embed.T)
@@ -638,14 +751,18 @@
     *kept, part = region_forward(
         idx, region_slide, got, tissue, w_query, w_key, w_value, w_out, att_v, att_u, att_row
     )
-    z = add_up(exchange(part, XYC))
-    z = exchange(spread(z, 8), Z)
-    df, rest, logits, g_class = region_backward(
-        idx, region_slide, z, tissue,
-        (w_query, w_key, w_value, w_out, att_v, att_u, att_row, w_class.T, g_logits), kept,
-    )
-    back = exchange(df.reshape(GRP, -1, D2), GRP_AXES).reshape(-1, D2)
-    mine, other = patch_backward(idx, back, tokens, mid, hid, gp, w_embed.T, w_down, rest)
+    z = exchange(part, DEV_AXES)
+    class_rows = w_class.T
+    df, grad, rows = region_backward(
+        idx, region_slide, tissue,
+        (w_query, w_key, w_value, w_out, att_v, att_u, att_row, class_rows, g_logits), kept,
+    )
+    df = join_sums(z, rows, df)
+    back = exchange(df.reshape(GRP, -1, PATCH), GRP_AXES).reshape(df.shape)
+    mine, other, logits, g_class = patch_backward(
+        idx, region_slide, back, tokens, mid, hid, gp, w_embed.T, w_down, grad, rows, class_rows,
+        g_logits,
+    )
     half = add_pair(mine, swap_cores(other))
     chunk = add_up(exchange(half.reshape(PEERS, -1, 128), ZLXY))
     chunk = add_over_zh(chunk)

time: 166 us -> 158 us (0.952)
  blocking collectives: 89.1 us -> 66.2 us
  starting transfers between devices: 13.5 us -> 27.8 us
  waiting for transfers between devices: 19.7 us -> 15 us
  local copies, waits for them, and re-layouts: 1.72 us -> 5.6 us
  Pallas kernels: 38.3 us -> 40.9 us
    all_to_all x5 -> x3, blocking collectives: 89.1 us -> 66.2 us  [exchange(): return lax.all_to_all(x, axes, split_axis=0, concat_axis=0, tiled=True)]
    all_to_all x1 -> x2, starting transfers between devices: 7.19 us -> 17.2 us  [exchange(): return lax.all_to_all(x, axes, split_axis=0, concat_axis=0, tiled=True)]
    ppermute x2, starting transfers between devices: 0.32 us -> 5.01 us  [add_over_zh(): x = add_pair(x, lax.ppermute(x, 'zh', [(i, i ^ flip) for i in range(4)]))]
    ppermute x2, waiting for transfers between devices: 9.26 us -> 4.63 us  [add_over_zh(): x = add_pair(x, lax.ppermute(x, 'zh', [(i, i ^ flip) for i in range(4)]))]
    unnamed x4 -> x28, local copies, waits for them, and re-layouts: 0.71 us -> 4.68 us
    pallas_call x1, Pallas kernels: 8.09 us -> 10.5 us  [patch_backward(): pl.pallas_call(patch_backward_kernel, grid_spec=pltpu.PrefetchScalarGridS...]
    all_to_all x1 -> x2, waiting for transfers between devices: 6.51 us -> 6.61 us  [exchange(): return lax.all_to_all(x, axes, split_axis=0, concat_axis=0, tiled=True)]
  transfers between devices with their start and end apart: 5 -> 6, of which waited for: 5 -> 5; matrix products, arithmetic and copies ran while one was open for 0% -> 0% of each run, Pallas kernels for 1% -> 9%
where the time goes in v3:
time: 158 us; the launch traced here: 157 us
  blocking collectives  66.2 us (42%)
  Pallas kernels  40.9 us (26%)
  starting transfers between devices  27.8 us (18%)
  waiting for transfers between devices  15 us (9%)
  local copies, waits for them, and re-layouts  5.6 us (4%)
    all_to_all x3, blocking collectives, exchange(): return lax.all_to_all(x, axes, split_axis=0, concat_axis=0, tiled=True)  66.2 us
    all_to_all x2, starting transfers between devices, exchange(): return lax.all_to_all(x, axes, split_axis=0, concat_axis=0, tiled=True)  17.2 us
    pallas_call x1, Pallas kernels, region_backward(): pl.pallas_call(region_backward_kernel, grid_spec=pltpu.PrefetchScalarGrid...  11.3 us
    pallas_call x1, Pallas kernels, patch_backward(): pl.pallas_call(patch_backward_kernel, grid_spec=pltpu.PrefetchScalarGridS...  10.5 us
    pallas_call x1, Pallas kernels, region_forward(): pl.pallas_call(region_forward_kernel, grid_spec=pltpu.PrefetchScalarGridS...  7.64 us
    pallas_call x1, Pallas kernels, patch_forward(): pl.pallas_call(patch_forward_kernel, grid=(steps,), in_specs=[pl.BlockSpe...  6.76 us
    all_to_all x2, waiting for transfers between devices, exchange(): return lax.all_to_all(x, axes, split_axis=0, concat_axis=0, tiled=True)  6.61 us
    ppermute x2, starting transfers between devices, swap_cores(): return lax.ppermute(x, 'c', [(0, 1), (1, 0)])  5.62 us
  transfers between devices with their start and end apart: 6, of which 5 were waited for; matrix products, arithmetic and copies ran while one was open for 0% of the time, Pallas kernels for 9%

profile of v3, /device:TPU:1, one launch (start us, length us, event | category | flops | bytes accessed | tf_op | source)
XLA Modules:
  0.0 157.1 jit_solution(15882057980243089129)
XLA Ops:
  0.6 6.8 %patch_forward.1 = (bf16[512,192]{1,0:T(8,128)(2,1)}, bf16[512,1536]{1,0:T(8,128)(2,1)}, bf16[512,1536]{1,0:T(8,128)(2,1)}, bf16[512,384]{1,0:T(8,128)(2,1)}) custom-call(bf16[512,384]{1,0:T(8,128)(2,1)} %bitcast.23, bf16[384,1536]{1,0:T(8,128)(2,1)} %wu_ref.1, bf16[1536,384]{1,0:T(8,128)(2,1)} %wd_ref.3, bf16[192,384]{1,0:T(8,128)(2,1)} %bitcast.25), custom_call_target="tpu_custom_call" | custom-call | tf_op jit(solution)/shard_map/patch_forward/pallas_call | solution.py:106
  7.4 7.2 %all-to-all-start = ((bf16[16,32,192]{2,1,0:T(8,128)(2,1)}), bf16[16,32,192]{2,1,0:T(8,128)(2,1)S(1)}, u32[]{:S(2)}, u32[]{:S(2)}) async-start(bf16[16,32,192]{2,1,0:T(8,128)(2,1)} %bitcast.32), calls=%async_computation | async-start | bytes 524288 | tf_op jit(solution)/shard_map/all_to_all | solution.py:712
  14.6 0.6 stack.27.idx_ref
  15.1 6.6 %all-to-all-done = bf16[16,32,192]{2,1,0:T(8,128)(2,1)S(1)} async-done(((bf16[16,32,192]{2,1,0:T(8,128)(2,1)}), bf16[16,32,192]{2,1,0:T(8,128)(2,1)S(1)}, u32[]{:S(2)}, u32[]{:S(2)}) %all-to-all-start) | async-done | bytes 196640 | tf_op jit(solution)/shard_map/all_to_all | solution.py:712
  21.8 0.7 copy-done.13
  22.5 7.6 %region_forward.1 = (bf16[2,1536,256]{2,1,0:T(8,128)(2,1)}, bf16[2,256,192]{2,1,0:T(8,128)(2,1)}, bf16[2,256,192]{2,1,0:T(8,128)(2,1)}, bf16[2,256,192]{2,1,0:T(...) custom-call(s32[6]{0:T(128)} %stack.27.idx_ref, ...), custom_call_target="tpu_custom_call" | custom-call | tf_op jit(solution)/shard_map/region_forward/pallas_call | solution.py:221
  30.1 10.0 %all-to-all-start.1 = ((f32[16,8,128]{2,1,0:T(8,128)}), f32[16,8,128]{2,1,0:T(8,128)S(1)}, u32[]{:S(2)}, u32[]{:S(2)}) async-start(f32[16,8,128]{2,1,0:T(8,128)} %get-tuple-element.56), calls=%async_computation.1 | async-start | bytes 131072 | tf_op jit(solution)/shard_map/all_to_all | solution.py:712
  40.1 0.0 copy-start.2
  40.2 0.0 copy-start.3
  40.2 0.0 copy-start.5
  40.2 0.0 copy-start.9
  40.2 0.0 copy-start.10
  40.2 0.0 copy-start.11
  40.2 0.0 copy-start.12
  40.2 11.3 %region_backward.1 = (bf16[16,5,16,256]{3,2,1,0:T(8,128)(2,1)}, f32[2,3,2,192,192]{4,3,2,1,0:T(8,128)}, f32[72,192]{1,0:T(8,128)}) custom-call(s32[6]{0:T(128)} %stack.27.idx_ref, s32[512]{0:T(512)} %slide_ref.5, s32[512,256]{1,0:T(8,128)} %tis_ref.3, bf16[192,192]{1,0:T(8,128)(2,1)} %wq_in.3, bf16[192,192]{1,0:T(8,128)(2,1)} %wk_in.3, ...), custom_call_target="tpu_custom_call" | custom-call | flops 4000000000 | bytes 20000000 | tf_op jit(solution)/shard_map/region_backward/pallas_call | solution.py:353
  51.5 0.0 copy-start
  51.5 0.0 all-to-all-done.1.z_ref
  51.5 0.0 copy-start.1
  51.5 1.2 copy-done.1
  52.7 0.9 copy-done.7
  53.6 0.1 join_sums.1
  53.7 15.6 %all_to_all.25 = bf16[16,80,256]{2,1,0:T(8,128)(2,1)S(1)} all-to-all(bf16[16,80,256]{2,1,0:T(8,128)(2,1)S(1)} %bitcast.22), channel_id=1, replica_groups=mesh['zl'=2,'x'=4,'c'=2,'zh'=4,'y'=4] {'zl','x','c'}, dimensions={0} | all-to-all | bytes 1310720 | tf_op jit(solution)/shard_map/all_to_all | solution.py:712
  69.4 0.0 copy-done.2
  69.4 0.0 copy-done.9
  69.4 0.0 copy-done.10
  69.4 0.0 copy-done.11
  69.4 0.0 copy-done.12
  69.4 0.0 copy-done
  69.4 0.0 copy-done.4
  69.4 0.0 copy-start.6
  69.4 1.0 copy-done.6
  70.4 0.9 copy-done.8
  71.3 10.5 %patch_backward.1 = (bf16[6144,128]{1,0:T(8,128)(2,1)S(1)}, bf16[6144,128]{1,0:T(8,128)(2,1)S(1)}, f32[4,3]{1,0:T(4,128)}, f32[3,192]{1,0:T(4,128)}) custom-call(s32[6]{0:T(128)S(1)} %copy-done.9, s32[512]{0:T(512)S(1)} %copy-done.10, bf16[16,5,16,256]{3,2,1,0:T(8,128)(2,1)S(1)} %bitcast.21, bf16[512,384]{1,0:T(8,128)(2,1)S(1)} %bitcast.24, ...), custom_call_target="tpu_custom_call" | custom-call | tf_op jit(solution)/shard_map/patch_backward/pallas_call | solution.py:608
  81.9 0.8 collective-permute-start
  82.6 3.0 %collective-permute-done = bf16[6144,128]{1,0:T(8,128)(2,1)S(1)} collective-permute-done((bf16[6144,128]{1,0:T(8,128)(2,1)S(1)}, bf16[6144,128]{1,0:T(8,128)(2,1)S(1)}, u32[]{:S(2)}, u32[]{:S(2)}) %collective-permute-start) | collective-permute-done | bytes 1572896 | tf_op jit(solution)/shard_map/ppermute | solution.py:716
  85.7 0.4 add_convert_fusion
  86.1 26.7 %all_to_all.26 = bf16[32,192,128]{2,1,0:T(8,128)(2,1)S(1)} all-to-all(bf16[32,192,128]{2,1,0:T(8,128)(2,1)S(1)} %bitcast.29), channel_id=1, replica_groups=mesh['zl'=2,'x'=4,'c'=2,'zh'=4,'y'=4] {'y','zl','x'}, dimensions={0} | all-to-all | bytes 3145728 | tf_op jit(solution)/shard_map/all_to_all | solution.py:712
  112.8 0.2 reduce_sum.12
  113.0 2.2 %collective-permute-start.1 = (bf16[192,128]{1,0:T(8,128)(2,1)S(1)}, bf16[192,128]{1,0:T(8,128)(2,1)S(1)}, u32[]{:S(2)}, u32[]{:S(2)}) collective-permute-start(bf16[192,128]{1,0:T(8,128)(2,1)S(1)} %reduce_sum.12), channel_id=1, source_target_pairs={{0,4},{4,0},{8,12},{12,8},{1,5},{5,1},{9,13},{13,9},{2,6},{6,2},{1... | collective-permute-start | bytes 147464 | tf_op jit(solution)/shard_map/ppermute | solution.py:729
  115.2 2.3 %collective-permute-done.1 = bf16[192,128]{1,0:T(8,128)(2,1)S(1)} collective-permute-done((bf16[192,128]{1,0:T(8,128)(2,1)S(1)}, bf16[192,128]{1,0:T(8,128)(2,1)S(1)}, u32[]{:S(2)}, u32[]{:S(2)}) %collective-permute-start.1) | collective-permute-done | bytes 49184 | tf_op jit(solution)/shard_map/ppermute | solution.py:729
  117.5 2.9 %collective-permute-start.2 = (bf16[192,128]{1,0:T(8,128)(2,1)S(1)}, bf16[192,128]{1,0:T(8,128)(2,1)S(1)}, u32[]{:S(2)}, u32[]{:S(2)}) collective-permute-start(bf16[192,128]{1,0:T(8,128)(2,1)S(1)} %add_convert_fusion.2), channel_id=1, source_target_pairs={{0,12},{4,8},{8,4},{12,0},{1,13},{5,9},{9,5},{13,1},{2,14},{6,10},... | collective-permute-start | bytes 147464 | tf_op jit(solution)/shard_map/ppermute | solution.py:729
  120.3 2.3 %collective-permute-done.2 = bf16[192,128]{1,0:T(8,128)(2,1)S(1)} collective-permute-done((bf16[192,128]{1,0:T(8,128)(2,1)S(1)}, bf16[192,128]{1,0:T(8,128)(2,1)S(1)}, u32[]{:S(2)}, u32[]{:S(2)}) %collective-permute-start.2) | collective-permute-done | bytes 49184 | tf_op jit(solution)/shard_map/ppermute | solution.py:729
  122.7 0.3 broadcast_in_dim.2
  123.0 23.9 %all_to_all.27 = bf16[32,192,128]{2,1,0:T(8,128)(2,1)S(1)} all-to-all(bf16[32,192,128]{2,1,0:T(8,128)(2,1)S(1)} %broadcast_in_dim.2), channel_id=1, replica_groups=mesh['zl'=2,'x'=4,'c'=2,'zh'=4,'y'=4] {'y','zl','x'}, dimensions={0} | all-to-all | bytes 3145728 | tf_op jit(solution)/shard_map/all_to_all | solution.py:712
  146.9 4.8 %collective-permute-start.3 = (bf16[6144,128]{1,0:T(8,128)(2,1)S(1)}, bf16[6144,128]{1,0:T(8,128)(2,1)S(1)}, u32[]{:S(2)}, u32[]{:S(2)}) collective-permute-start(bf16[6144,128]{1,0:T(8,128)(2,1)S(1)} %bitcast.19), channel_id=1, source_target_pairs={{0,16},{16,0},{1,17},{17,1},{2,18},{18,2},{3,19},{19,3},{4,20},{20... | collective-permute-start | bytes 4718600 | tf_op jit(solution)/shard_map/ppermute | solution.py:716
  151.7 2.3 %unpack.2 = (f32[384,1536]{1,0:T(8,128)}, f32[1536,384]{1,0:T(8,128)}, f32[192,384]{1,0:T(8,128)}, f32[192,192]{1,0:T(8,128)}, f32[192,192]{1,0:T(8,128)}, /*ind...) custom-call(s32[6]{0:T(128)S(1)} %copy-done.9, ...), custom_call_target="tpu_custom_call" | custom-call | tf_op jit(solution)/shard_map/unpack/pallas_call | solution.py:679
  154.0 0.7 collective-permute-done.3.src_ref
  154.8 2.3 %unpack.3 = (f32[384,1536]{1,0:T(8,128)}, f32[1536,384]{1,0:T(8,128)}, f32[192,384]{1,0:T(8,128)}, f32[192,192]{1,0:T(8,128)}, f32[192,192]{1,0:T(8,128)}, /*ind...) custom-call(s32[6]{0:T(128)S(1)} %copy-done.9, ...), custom_call_target="tpu_custom_call", output_to_operand_aliasing={{0}: (2, {}), {1}: (3, {}), {2}: (4, {}), {3}: (5, {}), {4}... | custom-call | tf_op jit(solution)/shard_map/unpack/pallas_call | solution.py:679
  (8 shorter events, 0.0 us)
Async XLA Ops:
  7.4 14.3 %all-to-all-start = ((bf16[16,32,192]{2,1,0:T(8,128)(2,1)}), bf16[16,32,192]{2,1,0:T(8,128)(2,1)S(1)}, u32[]{:S(2)}, u32[]{:S(2)}) async-start(bf16[16,32,192]{2,1,0:T(8,128)(2,1)} %bitcast.32), calls=%async_computation | async-start | bytes 524288 | tf_op jit(solution)/shard_map/all_to_all | solution.py:712
  21.8 0.7 copy-start.13
  30.1 21.4 %all-to-all-start.1 = ((f32[16,8,128]{2,1,0:T(8,128)}), f32[16,8,128]{2,1,0:T(8,128)S(1)}, u32[]{:S(2)}, u32[]{:S(2)}) async-start(f32[16,8,128]{2,1,0:T(8,128)} %get-tuple-element.56), calls=%async_computation.1 | async-start | bytes 131072 | tf_op jit(solution)/shard_map/all_to_all | solution.py:712
  40.1 29.2 %copy-start.2 = (bf16[32,16,384]{2,1,0:T(8,128)(2,1)S(1)}, bf16[32,16,384]{2,1,0:T(8,128)(2,1)}, u32[]{:S(2)}) copy-start(bf16[32,16,384]{2,1,0:T(8,128)(2,1)} %param.15) | copy-start | bytes 1179652
  40.2 29.2 %copy-start.3 = (bf16[512,1536]{1,0:T(8,128)(2,1)S(1)}, bf16[512,1536]{1,0:T(8,128)(2,1)}, u32[]{:S(2)}) copy-start(bf16[512,1536]{1,0:T(8,128)(2,1)} %get-tuple-element.71.hid_ref) | copy-start | bytes 4718596
  40.2 29.2 %copy-start.5 = (bf16[384,192]{0,1:T(8,128)(2,1)S(1)}, bf16[384,192]{0,1:T(8,128)(2,1)}, u32[]{:S(2)}) copy-start(bf16[384,192]{0,1:T(8,128)(2,1)} %param.20) | copy-start | bytes 442372
  40.2 29.2 %copy-start.9 = (s32[6]{0:T(128)S(1)}, s32[6]{0:T(128)}, u32[]{:S(2)}) copy-start(s32[6]{0:T(128)} %stack.27.idx_ref) | copy-start | bytes 76
  40.2 29.2 %copy-start.10 = (s32[512]{0:T(512)S(1)}, s32[512]{0:T(512)}, u32[]{:S(2)}) copy-start(s32[512]{0:T(512)} %slide_ref.5) | copy-start | bytes 6148
  40.2 29.2 %copy-start.11 = (f32[192,3]{0,1:T(4,128)S(1)}, f32[192,3]{0,1:T(4,128)}, u32[]{:S(2)}) copy-start(f32[192,3]{0,1:T(4,128)} %param.28) | copy-start | bytes 6916
  40.2 29.2 %copy-start.12 = (f32[4,3]{1,0:T(4,128)S(1)}, f32[4,3]{1,0:T(4,128)}, u32[]{:S(2)}) copy-start(f32[4,3]{1,0:T(4,128)} %gl_ref.3) | copy-start | bytes 148
  51.5 17.9 %copy-start = (bf16[1536,384]{1,0:T(8,128)(2,1)S(1)}, bf16[1536,384]{1,0:T(8,128)(2,1)}, u32[]{:S(2)}) copy-start(bf16[1536,384]{1,0:T(8,128)(2,1)} %wd_ref.3) | copy-start | bytes 3538948
  51.5 1.2 copy-start.1
  52.7 0.9 copy-start.7
  53.6 15.8 %copy-start.4 = (bf16[512,1536]{1,0:T(8,128)(2,1)S(1)}, bf16[512,1536]{1,0:T(8,128)(2,1)}, u32[]{:S(2)}) copy-start(bf16[512,1536]{1,0:T(8,128)(2,1)} %get-tuple-element.72.gp_ref) | copy-start | bytes 4718596
  69.4 1.0 copy-start.6
  70.4 0.9 copy-start.8
  81.9 3.8 %collective-permute-start = (bf16[6144,128]{1,0:T(8,128)(2,1)S(1)}, bf16[6144,128]{1,0:T(8,128)(2,1)S(1)}, u32[]{:S(2)}, u32[]{:S(2)}) collective-permute-start(bf16[6144,128]{1,0:T(8,128)(2,1)S(1)} %get-tuple-element.76), channel_id=1, source_target_pairs={{0,16},{16,0},{1,17},{17,1},{2,18},{18,2},{3,19},{19,3},{4,20},{20... | collective-permute-start | bytes 4718600 | tf_op jit(solution)/shard_map/ppermute | solution.py:716
  113.0 4.4 %collective-permute-start.1 = (bf16[192,128]{1,0:T(8,128)(2,1)S(1)}, bf16[192,128]{1,0:T(8,128)(2,1)S(1)}, u32[]{:S(2)}, u32[]{:S(2)}) collective-permute-start(bf16[192,128]{1,0:T(8,128)(2,1)S(1)} %reduce_sum.12), channel_id=1, source_target_pairs={{0,4},{4,0},{8,12},{12,8},{1,5},{5,1},{9,13},{13,9},{2,6},{6,2},{1... | collective-permute-start | bytes 147464 | tf_op jit(solution)/shard_map/ppermute | solution.py:729
  117.5 5.2 %collective-permute-start.2 = (bf16[192,128]{1,0:T(8,128)(2,1)S(1)}, bf16[192,128]{1,0:T(8,128)(2,1)S(1)}, u32[]{:S(2)}, u32[]{:S(2)}) collective-permute-start(bf16[192,128]{1,0:T(8,128)(2,1)S(1)} %add_convert_fusion.2), channel_id=1, source_target_pairs={{0,12},{4,8},{8,4},{12,0},{1,13},{5,9},{9,5},{13,1},{2,14},{6,10},... | collective-permute-start | bytes 147464 | tf_op jit(solution)/shard_map/ppermute | solution.py:729
  146.9 7.9 %collective-permute-start.3 = (bf16[6144,128]{1,0:T(8,128)(2,1)S(1)}, bf16[6144,128]{1,0:T(8,128)(2,1)S(1)}, u32[]{:S(2)}, u32[]{:S(2)}) collective-permute-start(bf16[6144,128]{1,0:T(8,128)(2,1)S(1)} %bitcast.19), channel_id=1, source_target_pairs={{0,16},{16,0},{1,17},{17,1},{2,18},{18,2},{3,19},{19,3},{4,20},{20... | collective-permute-start | bytes 4718600 | tf_op jit(solution)/shard_map/ppermute | solution.py:716

commit v4 on v3

v4 whole, which is shorter than its diff:
```python
import math

import jax
import jax.numpy as jnp
from jax import lax
from jax.experimental import pallas as pl
from jax.experimental.pallas import tpu as pltpu
from jax.sharding import Mesh, PartitionSpec as P

D1 = 384
F1 = 1536
HEADS = 6
HEAD_DIM = 32
D2 = 192
PATCH = 256
SLIDES = 4
GRP = 16
OWN = 2
SCALE = 1.0 / math.sqrt(HEAD_DIM)
GELU_C = math.sqrt(2.0 / math.pi)
GELU_A = 0.044715

BF = jnp.bfloat16
F32 = jnp.float32
HIGHEST = lax.Precision.HIGHEST
MIB = 1024 * 1024

HALF_ROWS = 6144
DOWN_AT = 2304
REST_AT = 4608
REST_ROWS = 1152
EMBED_AT = REST_AT + REST_ROWS
PAD_AT = EMBED_AT + 288
PEERS = 32


def nn(a, b, precision=None):
    return jnp.dot(a, b, precision=precision, preferred_element_type=F32)


def nt(a, b, precision=None):
    return lax.dot_general(
        a, b, (((1,), (1,)), ((), ())), precision=precision, preferred_element_type=F32
    )


def tn(a, b, precision=None):
    return lax.dot_general(
        a, b, (((0,), (0,)), ((), ())), precision=precision, preferred_element_type=F32
    )


def params(mib=32):
    return pltpu.CompilerParams(vmem_limit_bytes=mib * MIB)


def patch_forward_kernel(x_ref, wu_ref, wd_ref, we_ref, feat_ref, mid_ref, acc):
    step = pl.program_id(0)
    x = x_ref[...]
    pre = nn(x, wu_ref[...])
    sq = pre * pre
    t = jnp.tanh(GELU_C * (pre + GELU_A * (pre * sq)))
    part = nn((pre * (0.5 + 0.5 * t)).astype(BF), wd_ref[...])

    @pl.when(step == 0)
    def _():
        acc[...] = x.astype(F32) + part

    @pl.when(step > 0)
    def _():
        acc[...] += part

    @pl.when(step == pl.num_programs(0) - 1)
    def _():
        mid = acc[...].astype(BF)
        mid_ref[...] = mid
        feat_ref[...] = nt(mid, we_ref[...]).astype(BF)


STEPS1 = 4
FB1 = F1 // STEPS1


def patch_forward(tokens, w_up, w_down, w_embed):
    rows = tokens.shape[0]
    whole = lambda i: (0, 0)
    return pl.pallas_call(
        patch_forward_kernel,
        grid=(STEPS1,),
        in_specs=[
            pl.BlockSpec((rows, D1), whole),
            pl.BlockSpec((D1, FB1), lambda i: (0, i)),
            pl.BlockSpec((FB1, D1), lambda i: (i, 0)),
            pl.BlockSpec((D2, D1), whole),
        ],
        out_specs=[
            pl.BlockSpec((rows, D2), whole),
            pl.BlockSpec((rows, D1), whole),
        ],
        out_shape=[
            jax.ShapeDtypeStruct((rows, D2), BF),
            jax.ShapeDtypeStruct((rows, D1), BF),
        ],
        scratch_shapes=[pltpu.VMEM((rows, D1), F32)],
        compiler_params=params(61),
        name="patch_forward",
    )(tokens, w_up, w_down, w_embed)


def patch_slopes_kernel(after_ref, x_ref, wu_ref, hid_ref, gp_ref, xt_ref):
    x = x_ref[...]

    @pl.when(pl.program_id(0) == 0)
    def _():
        xt_ref[...] = x.T

    pre = nn(x, wu_ref[...])
    sq = pre * pre
    t = jnp.tanh(GELU_C * (pre + GELU_A * (pre * sq)))
    half_up = 0.5 + 0.5 * t
    hid_ref[...] = (pre * half_up).astype(BF).T
    slope = (0.5 * GELU_C) * (1.0 - t * t) * (1.0 + (3.0 * GELU_A) * sq)
    gp_ref[...] = (half_up + pre * slope).astype(BF)


def patch_slopes(after, tokens, w_up):
    rows = tokens.shape[0]
    whole = lambda i: (0, 0)
    return pl.pallas_call(
        patch_slopes_kernel,
        grid=(STEPS1,),
        in_specs=[
            pl.BlockSpec(memory_space=pl.ANY),
            pl.BlockSpec((rows, D1), whole),
            pl.BlockSpec((D1, FB1), lambda i: (0, i)),
        ],
        out_specs=[
            pl.BlockSpec((FB1, rows), lambda i: (i, 0)),
            pl.BlockSpec((rows, FB1), lambda i: (0, i)),
            pl.BlockSpec((D1, rows), whole),
        ],
        out_shape=[
            pltpu.HBM((F1, rows), BF),
            pltpu.HBM((rows, F1), BF),
            pltpu.HBM((D1, rows), BF),
        ],
        compiler_params=params(61),
        cost_estimate=pl.CostEstimate(
            flops=3_000_000_000, bytes_accessed=12_000_000, transcendentals=0
        ),
        name="patch_slopes",
    )(after, tokens, w_up)


def gather_weights_kernel(*refs):
    ins, (wp_ref, ap_ref) = refs[:6], refs[6:]
    for i in range(4):
        wp_ref[i] = ins[i][...]
    for i in range(2):
        ap_ref[i] = ins[4 + i][...]


def gather_weights(weights):
    vm = pl.BlockSpec(memory_space=pltpu.VMEM)
    return pl.pallas_call(
        gather_weights_kernel,
        in_specs=[vm] * 6,
        out_specs=[vm] * 2,
        out_shape=[
            jax.ShapeDtypeStruct((4, D2, D2), BF),
            jax.ShapeDtypeStruct((2, D2, D2), F32),
        ],
        compiler_params=params(24),
        cost_estimate=pl.CostEstimate(
            flops=1_000_000_000, bytes_accessed=4_000_000, transcendentals=0
        ),
        name="gather_weights",
    )(*weights)


def tissue_row(idx_ref, tis_ref, r):
    return tis_ref[pl.ds(idx_ref[1] + r, 1), :].astype(F32)


def column_of(row, width):
    return jnp.broadcast_to(row, (PATCH, row.shape[1])).T[:, :width]


def head_mask(h, shape, dim):
    return (lax.broadcasted_iota(jnp.int32, shape, dim) // HEAD_DIM == h).astype(F32)


def region_forward_kernel(
    idx_ref, slide_ref, f_ref, tis_ref, wp_ref, ap_ref, aw_ref,
    p_ref, x_ref, asum_ref, reg_ref, tanh_ref, gate_ref, w_ref,
    part_ref,
):
    r = pl.program_id(0)
    trow = tissue_row(idx_ref, tis_ref, r)
    tcol = column_of(trow, D2)
    x = (f_ref[...].reshape(PATCH, D2).astype(F32) * tcol).astype(BF)
    q = nn(x, wp_ref[0]).astype(BF)
    k = nn(x, wp_ref[1])
    v = nn(x, wp_ref[2]).astype(BF)
    x_ref[0] = x
    spread = jnp.zeros((PATCH, D2), F32)
    for h in range(HEADS):
        mask = head_mask(h, (1, D2), 1)
        st = nt((k * mask).astype(BF), q) * SCALE
        top = jnp.max(st, axis=0, keepdims=True)
        ex = jnp.exp(st - top)
        total = jnp.sum(ex, axis=0, keepdims=True)
        pb = (ex * (1.0 / total)).astype(BF)
        p_ref[0, pl.ds(h * PATCH, PATCH), :] = pb
        spread = spread + nn(pb, (tcol * mask).astype(BF))
    asum = jnp.sum(spread * v.astype(F32), axis=0, keepdims=True)
    xsum = jnp.sum(x.astype(F32), axis=0, keepdims=True)
    count = jnp.maximum(jnp.sum(trow, axis=1, keepdims=True), 1.0)
    mixed = xsum + nn(jnp.broadcast_to(asum, (8, D2)), wp_ref[3].astype(F32), HIGHEST)[0:1]

    @pl.when(r == 0)
    def _():
        lane = lax.broadcasted_iota(jnp.int32, (8, PATCH), 1)
        reg_ref[...] = jnp.where(lane < D2, 0.0, 1.0)
        asum_ref[...] = jnp.zeros_like(asum_ref)

    asum_ref[pl.ds(r, 1), :] = asum
    reg_ref[pl.ds(r, 1), pl.ds(0, D2)] = mixed / count

    @pl.when(r == OWN - 1)
    def _():
        region = reg_ref[:, pl.ds(0, D2)]
        tanh_part = jnp.tanh(nn(region, ap_ref[0], HIGHEST))
        gate_part = jax.nn.sigmoid(nn(region, ap_ref[1], HIGHEST))
        tanh_ref[...] = tanh_part
        gate_ref[...] = gate_part
        score = jnp.sum(tanh_part * gate_part * aw_ref[...], axis=1, keepdims=True)
        weight = jnp.exp(score)
        w_ref[...] = jnp.broadcast_to(weight, w_ref.shape)
        wide = reg_ref[...] * weight
        slot = lax.broadcasted_iota(jnp.int32, (SLIDES, 1), 0)
        sums = jnp.zeros((SLIDES, PATCH), F32)
        for i in range(OWN):
            own = (slot == slide_ref[idx_ref[0] + i]).astype(F32)
            sums = sums + own * wide[i : i + 1]
        both = jnp.concatenate([sums[:, :128], sums[:, 128:]], axis=0)
        part_ref[...] = jnp.broadcast_to(both[None], part_ref.shape)


def packed_specs():
    return [
        pl.BlockSpec((4, D2, D2), lambda r, *_: (0, 0, 0)),
        pl.BlockSpec((2, D2, D2), lambda r, *_: (0, 0, 0)),
    ]


def region_forward(idx, slide, got, tissue, wp, ap, att_w):
    row8 = lambda width: pl.BlockSpec((8, width), lambda r, *_: (0, 0))
    per_region = lambda rows, width: pl.BlockSpec((1, rows, width), lambda r, *_: (r, 0, 0))
    return pl.pallas_call(
        region_forward_kernel,
        grid_spec=pltpu.PrefetchScalarGridSpec(
            num_scalar_prefetch=2,
            grid=(OWN,),
            in_specs=[
                pl.BlockSpec((GRP, 1, PATCH // GRP, D2), lambda r, *_: (0, r, 0, 0)),
                pl.BlockSpec((8, PATCH), lambda r, idx, _: (idx[2], 0)),
                *packed_specs(),
                pl.BlockSpec((1, D2), lambda r, *_: (0, 0)),
            ],
            out_specs=[
                per_region(HEADS * PATCH, PATCH),
                per_region(PATCH, D2),
                row8(D2),
                row8(PATCH),
                row8(D2),
                row8(D2),
                row8(128),
                pl.BlockSpec((GRP, 8, 128), lambda r, *_: (0, 0, 0)),
            ],
        ),
        out_shape=[
            jax.ShapeDtypeStruct((OWN, HEADS * PATCH, PATCH), BF),
            jax.ShapeDtypeStruct((OWN, PATCH, D2), BF),
            jax.ShapeDtypeStruct((8, D2), F32),
            jax.ShapeDtypeStruct((8, PATCH), F32),
            jax.ShapeDtypeStruct((8, D2), F32),
            jax.ShapeDtypeStruct((8, D2), F32),
            jax.ShapeDtypeStruct((8, 128), F32),
            jax.ShapeDtypeStruct((GRP, 8, 128), F32),
        ],
        compiler_params=params(40),
        name="region_forward",
    )(idx, slide, got, tissue, wp, ap, att_w)


def directions(
    idx_ref, slide_ref, tis_ref, wp_ref, ap_ref, aw_ref, wc_ref, gl_ref,
    asum_ref, reg_ref, tanh_ref, gate_ref, w_ref, rows_ref, cols_ref, scal_ref,
):
    d_summary = nn(gl_ref[...], wc_ref[...], HIGHEST)
    slot = lax.broadcasted_iota(jnp.int32, (SLIDES, 1), 0)
    row = lax.broadcasted_iota(jnp.int32, (8, 1), 0)
    d_own = jnp.zeros((8, D2), F32)
    count = jnp.ones((8, 1), F32)
    for i in range(OWN):
        mine = slot == slide_ref[idx_ref[0] + i]
        d_own = jnp.where(
            row == i, jnp.sum(jnp.where(mine, d_summary, 0.0), axis=0, keepdims=True), d_own
        )
        t_i = tissue_row(idx_ref, tis_ref, i)
        count = jnp.where(row == i, jnp.maximum(jnp.sum(t_i, axis=1, keepdims=True), 1.0), count)
    region = reg_ref[:, pl.ds(0, D2)]
    tanh_part = tanh_ref[...]
    gate_part = gate_ref[...]
    pre_v = aw_ref[...] * gate_part * (1.0 - tanh_part * tanh_part)
    pre_u = aw_ref[...] * tanh_part * gate_part * (1.0 - gate_part)
    second = nt(pre_v, ap_ref[0], HIGHEST) + nt(pre_u, ap_ref[1], HIGHEST)
    own = jnp.sum(d_own * region, axis=1, keepdims=True)
    dm = (d_own / count, second / count)
    kept = (
        pre_v, pre_u, dm[0], dm[1],
        jnp.broadcast_to(w_ref[:, 0:1], (8, D2)), jnp.broadcast_to(own, (8, D2)),
        nt(dm[0].astype(BF), wp_ref[3]), nt(dm[1].astype(BF), wp_ref[3]),
    )
    for i, value in enumerate(kept):
        rows_ref[pl.ds(8 * i, 8), :] = value
    turned = jnp.concatenate(
        [region, asum_ref[...], tanh_part * gate_part, jnp.zeros((104, D2), F32)], axis=0
    )
    cols_ref[...] = turned.T
    lane = lax.broadcasted_iota(jnp.int32, (1, PATCH), 1) // 64
    scalars = jnp.zeros((1, PATCH), F32)
    for i in range(OWN):
        scalars = jnp.where(lane == 2 * i, w_ref[i : i + 1, 0:1], scalars)
        scalars = jnp.where(lane == 2 * i + 1, own[i : i + 1], scalars)
    scal_ref[...] = jnp.broadcast_to(scalars, (8, PATCH))


def pull_back(r, idx_ref, tis_ref, wp_ref, p_ref, x_ref, rows_ref, df_ref, grad_ref, kt_s, dqt_s):
    trow = tissue_row(idx_ref, tis_ref, r)
    tcol = column_of(trow, D2)
    x = x_ref[0]
    q = nn(x, wp_ref[0]).astype(BF).astype(F32)
    v = nn(x, wp_ref[2]).astype(BF)
    kt_s[...] = nn(x, wp_ref[1]).T.astype(BF)
    spread = jnp.zeros((PATCH, D2), F32)
    dm = [rows_ref[pl.ds(8 * (2 + j) + r, 1), :] for j in range(2)]
    da = [rows_ref[pl.ds(8 * (6 + j) + r, 1), :].astype(BF).astype(F32) for j in range(2)]
    da_col = jnp.concatenate([jnp.broadcast_to(d, (128, D2)) for d in da], axis=0).T
    dk = [jnp.zeros((PATCH, D2), F32) for _ in range(2)]
    for h in range(HEADS):
        e = nn(v, (da_col * head_mask(h, (D2, 1), 0)).astype(BF))
        pb = p_ref[0, pl.ds(h * PATCH, PATCH), :]
        pt = pb.astype(F32)
        mask = head_mask(h, (1, D2), 1)
        spread = spread + nn(pb, (tcol * mask).astype(BF))
        q_head = (q * mask).astype(BF)
        k_head = kt_s[pl.ds(h * HEAD_DIM, HEAD_DIM), :]
        for j in range(2):
            e_j = e[:, 128 * j : 128 * j + 128]
            pe = pt * jnp.concatenate([e_j, e_j], axis=1)
            ds = (pe - pt * jnp.sum(pe, axis=0, keepdims=True)).astype(BF)
            dk[j] = dk[j] + nn(ds, q_head)
            dqt_s[j, pl.ds(h * HEAD_DIM, HEAD_DIM), :] = nn(k_head, ds)
    xt = x.astype(F32).T.astype(BF)
    for j in range(2):
        dq = (dqt_s[j] * (trow * SCALE)).T.astype(BF)
        dk_j = (dk[j] * SCALE).astype(BF)
        dv = (spread * da[j]).astype(BF)
        grad_ref[0, 0, j] = nn(xt, dq)
        grad_ref[0, 1, j] = nn(xt, dk_j)
        grad_ref[0, 2, j] = nn(xt, dv)
        d_flat = dm[j] + nt(dq, wp_ref[0]) + nt(dk_j, wp_ref[1]) + nt(dv, wp_ref[2])
        d_flat = (tcol * d_flat).astype(BF).reshape(GRP, PATCH // GRP, D2)
        df_ref[:, j, :, pl.ds(0, D2)] = d_flat
        df_ref[:, j, :, pl.ds(D2, 64)] = jnp.zeros((GRP, PATCH // GRP, 64), BF)


BLOCKS = 2 * OWN + 1


def region_backward_kernel(
    idx_ref, slide_ref, tis_ref, wp_ref, ap_ref, aw_ref, wc_ref, gl_ref,
    p_ref, x_ref, asum_ref, reg_ref, tanh_ref, gate_ref, w_ref,
    df_ref, grad_ref, rows_ref, cols_ref, scal_ref,
    kt_s, dqt_s,
):
    r = pl.program_id(0)

    @pl.when(r == 0)
    def _():
        directions(
            idx_ref, slide_ref, tis_ref, wp_ref, ap_ref, aw_ref, wc_ref, gl_ref,
            asum_ref, reg_ref, tanh_ref, gate_ref, w_ref, rows_ref, cols_ref, scal_ref,
        )

    pull_back(
        r, idx_ref, tis_ref, wp_ref, p_ref, x_ref, rows_ref, df_ref, grad_ref, kt_s, dqt_s
    )


def region_backward(idx, slide, tissue, wp, ap, att_w, w_class, g_logits, kept):
    whole = lambda rows, width: pl.BlockSpec((rows, width), lambda r, *_: (0, 0))
    region = lambda rows, width: pl.BlockSpec((1, rows, width), lambda r, *_: (r, 0, 0))
    return pl.pallas_call(
        region_backward_kernel,
        grid_spec=pltpu.PrefetchScalarGridSpec(
            num_scalar_prefetch=2,
            grid=(OWN,),
            in_specs=[
                pl.BlockSpec((8, PATCH), lambda r, idx, _: (idx[2], 0)),
                *packed_specs(),
                whole(1, D2), whole(3, D2), whole(SLIDES, 3),
                region(HEADS * PATCH, PATCH),
                region(PATCH, D2),
                whole(8, D2), whole(8, PATCH), whole(8, D2), whole(8, D2), whole(8, 128),
            ],
            out_specs=[
                pl.BlockSpec((GRP, 2, PATCH // GRP, PATCH), lambda r, *_: (0, r, 0, 0)),
                pl.BlockSpec((1, 3, 2, D2, D2), lambda r, *_: (r, 0, 0, 0, 0)),
                whole(64, D2),
                whole(D2, 128),
                whole(8, PATCH),
            ],
            scratch_shapes=[pltpu.VMEM((D2, PATCH), BF), pltpu.VMEM((2, D2, PATCH), F32)],
        ),
        out_shape=[
            pltpu.HBM((GRP, BLOCKS, PATCH // GRP, PATCH), BF),
            pltpu.HBM((OWN, 3, 2, D2, D2), F32),
            pltpu.HBM((64, D2), F32),
            pltpu.HBM((D2, 128), F32),
            jax.ShapeDtypeStruct((8, PATCH), F32),
        ],
        compiler_params=params(40),
        cost_estimate=pl.CostEstimate(
            flops=4_000_000_000, bytes_accessed=20_000_000, transcendentals=0
        ),
        name="region_backward",
    )(idx, slide, tissue, wp, ap, att_w, w_class, g_logits, *kept)


def split_three(x):
    parts = []
    for _ in range(3):
        top = x.astype(BF).astype(F32)
        parts.append(top)
        x = x - top
    return parts


def join_sums_kernel(z_ref, scal_ref, df_ref, out_ref, ext, wide, sem):
    z = jnp.sum(z_ref[...], axis=0)
    z = jnp.concatenate([z[0:SLIDES], z[SLIDES:]], axis=1)
    ext[...] = jnp.zeros_like(ext)
    for i, (part, tops) in enumerate(zip(split_three(z), split_three(scal_ref[0:1]))):
        ext[pl.ds(4 * i, 4), :] = part
        ext[pl.ds(12 + i, 1), :] = tops
    wide[...] = jnp.broadcast_to(ext[...].astype(BF)[None], wide.shape)
    copy = pltpu.make_async_copy(wide, out_ref.at[:, BLOCKS - 1], sem)
    copy.start()
    copy.wait()


def join_sums(z, scalars, df):
    return pl.pallas_call(
        join_sums_kernel,
        in_specs=[pl.BlockSpec(memory_space=pltpu.VMEM)] * 2
        + [pl.BlockSpec(memory_space=pl.ANY)],
        out_specs=pl.BlockSpec(memory_space=pl.ANY),
        out_shape=pltpu.HBM(df.shape, df.dtype),
        scratch_shapes=[
            pltpu.VMEM((16, PATCH), F32),
            pltpu.VMEM((GRP, 16, PATCH), BF),
            pltpu.SemaphoreType.DMA,
        ],
        input_output_aliases={2: 0},
        compiler_params=params(24),
        name="join_sums",
    )(z, scalars, df)


STEPS4 = 4
FB4 = F1 // STEPS4


def put_rest(pack, slot, grad, fill=None):
    at = REST_AT + 192 * slot
    if not isinstance(slot, int):
        at = pl.multiple_of(at, 64)
    for half in range(2):
        rows = grad[96 * half : 96 * half + 96]
        pack[half, pl.ds(at, 96), :] = rows[:, :128].astype(BF)
        tail = jnp.zeros((96, 64), F32) if fill is None else fill
        high = jnp.concatenate([rows[:, 128:], tail], axis=1)
        pack[half, pl.ds(at + 96, 96), :] = high.astype(BF)


def finish_slides(
    idx_ref, slide_ref, back_ref, rows_ref, cols_ref, wc_ref, gl_ref, logits_ref, gc_ref,
    df_s, pq_s, pack,
):
    ext = back_ref[:, BLOCKS - 1].astype(F32)
    sums = jnp.sum(ext, axis=0)
    sums = sums[0:4] + sums[4:8] + sums[8:12]
    total = sums[:, D2 : D2 + 1]
    summary = sums[:, :D2] / total
    wc = wc_ref[...]
    gl = gl_ref[...]
    logits_ref[...] = nt(summary, wc, HIGHEST)
    gc_ref[...] = tn(gl, summary, HIGHEST)
    along = jnp.sum(nn(gl, wc, HIGHEST) * summary, axis=1, keepdims=True)

    def of_slide(column, s):
        out = column[SLIDES - 1 : SLIDES]
        for i in range(SLIDES - 1):
            out = jnp.where(s == i, column[i : i + 1], out)
        return out

    def factors(w, a, s):
        share = w / of_slide(total, s)
        return share, share * (a - of_slide(along, s))

    for src in range(GRP):
        scalars = ext[src, 12:13] + ext[src, 13:14] + ext[src, 14:15]
        for i in range(OWN):
            w = scalars[:, 128 * i : 128 * i + 1]
            a = scalars[:, 128 * i + 64 : 128 * i + 65]
            p, q = factors(w, a, slide_ref[idx_ref[5] + OWN * src + i])
            f = [back_ref[src, 2 * i + j].astype(F32)[:, :D2] for j in range(2)]
            df_s[pl.ds(32 * src + 16 * i, 16), :] = (p * f[0] + q * f[1]).astype(BF)

    kept = [rows_ref[pl.ds(8 * i, 8), :] for i in range(6)]
    pre_v, pre_u, dm0, dm1, w_own, a_own = kept
    row = lax.broadcasted_iota(jnp.int32, (8, 1), 0)
    p_own = jnp.zeros((8, 1), F32)
    q_own = jnp.zeros((8, 1), F32)
    for i in range(OWN):
        p, q = factors(w_own[i : i + 1, 0:1], a_own[i : i + 1, 0:1], slide_ref[idx_ref[0] + i])
        p_own = jnp.where(row == i, p, p_own)
        q_own = jnp.where(row == i, q, q_own)
    pq_s[0] = jnp.broadcast_to(p_own, (8, 128))
    pq_s[1] = jnp.broadcast_to(q_own, (8, 128))

    def outer(at, rows):
        out = cols_ref[:, at : at + 1] * rows[0:1]
        return out + cols_ref[:, at + 1 : at + 2] * rows[1:2]

    put_rest(pack, 3, outer(8, p_own * dm0 + q_own * dm1))
    put_rest(pack, 4, outer(0, q_own * pre_v))
    g_aw = outer(16, jnp.broadcast_to(q_own, (8, 64)))
    lane = lax.broadcasted_iota(jnp.int32, (96, 64), 1)
    put_rest(pack, 5, outer(0, q_own * pre_u), jnp.where(lane == 0, g_aw[:96], g_aw[96:]))


def patch_backward_kernel(
    idx_ref, slide_ref, back_ref, xt_ref, mid_ref, hid_ref, gp_ref, we_ref, wd_ref,
    grad_ref, rows_ref, cols_ref, wc_ref, gl_ref,
    mine_ref, other_ref, logits_ref, gc_ref,
    pack, dmid_s, df_s, pq_s, sems,
):
    step = pl.program_id(0)
    core = idx_ref[3]

    def up_copies(i):
        rows = pl.ds(pl.multiple_of(576 * i, 64), 576)
        return (
            pltpu.make_async_copy(pack.at[core, rows], mine_ref.at[rows], sems.at[2 * i]),
            pltpu.make_async_copy(pack.at[1 - core, rows], other_ref.at[rows], sems.at[2 * i + 1]),
        )

    def down_copy(i, dst):
        rows = pl.ds(pl.multiple_of(DOWN_AT + 1152 * lax.rem(i, 2), 128), 1152)
        return pltpu.make_async_copy(pack.at[i // 2, rows], dst.at[rows], sems.at[8 + i])

    def rest_copies():
        rows = pl.ds(REST_AT, HALF_ROWS - REST_AT)
        return (
            pltpu.make_async_copy(pack.at[core, rows], mine_ref.at[rows], sems.at[12]),
            pltpu.make_async_copy(pack.at[1 - core, rows], other_ref.at[rows], sems.at[13]),
        )

    @pl.when(step == 0)
    def _():
        finish_slides(
            idx_ref, slide_ref, back_ref, rows_ref, cols_ref, wc_ref, gl_ref, logits_ref, gc_ref,
            df_s, pq_s, pack,
        )
        df = df_s[...]
        dmid_s[...] = nn(df, we_ref[...]).astype(BF)
        g_embed = tn(df, mid_ref[...]).astype(BF)
        for half in range(2):
            for l in range(3):
                block = g_embed[96 * half : 96 * half + 96, 128 * l : 128 * l + 128]
                pack[half, pl.ds(EMBED_AT + 96 * l, 96), :] = block
            pack[half, pl.ds(PAD_AT, 96), :] = jnp.zeros((96, 128), BF)

    @pl.when(step > 0)
    def _():
        grad = jnp.zeros((D2, D2), F32)
        for i in range(OWN):
            for j in range(2):
                grad = grad + pq_s[j, i : i + 1, 0:1] * grad_ref[i, 0, j]
        put_rest(pack, step - 1, grad)

    dmid = dmid_s[...]
    d_pre = (nt(dmid, wd_ref[...]) * gp_ref[...].astype(F32)).astype(BF)
    g_up = nn(xt_ref[...], d_pre).astype(BF)
    for half in range(2):
        for l in range(3):
            block = g_up[192 * half : 192 * half + 192, 128 * l : 128 * l + 128]
            pack[half, pl.ds(pl.multiple_of(576 * step + 192 * l, 64), 192), :] = block
    g_down = nn(hid_ref[...], dmid).astype(BF)
    at = DOWN_AT + 1152 * lax.rem(step, 2)
    for l in range(3):
        rows = pl.ds(pl.multiple_of(at + 384 * l, 128), 384)
        pack[step // 2, rows, :] = g_down[:, 128 * l : 128 * l + 128]

    for copy in up_copies(step):
        copy.start()

    @pl.when(step // 2 == core)
    def _():
        down_copy(step, mine_ref).start()

    @pl.when(step // 2 != core)
    def _():
        down_copy(step, other_ref).start()

    @pl.when(step == pl.num_programs(0) - 1)
    def _():
        for copy in rest_copies():
            copy.start()
        for copy in rest_copies():
            copy.wait()
        for i in range(STEPS4):
            for copy in up_copies(i):
                copy.wait()
            down_copy(i, mine_ref).wait()


def patch_backward(
    idx, slide, back, turned, mid, hid, gp, w_embed, w_down, grads, rows, cols, w_class, g_logits
):
    tokens = turned.shape[1]
    whole = lambda i, *_: (0, 0)
    grad = pl.BlockSpec(
        (OWN, 1, 2, D2, D2), lambda i, *_: (0, jnp.maximum(i - 1, 0), 0, 0, 0)
    )
    return pl.pallas_call(
        patch_backward_kernel,
        grid_spec=pltpu.PrefetchScalarGridSpec(
            num_scalar_prefetch=2,
            grid=(STEPS4,),
            in_specs=[
                pl.BlockSpec(back.shape, lambda i, *_: (0, 0, 0, 0)),
                pl.BlockSpec((D1, tokens), whole),
                pl.BlockSpec((tokens, D1), whole),
                pl.BlockSpec((FB4, tokens), lambda i, *_: (i, 0)),
                pl.BlockSpec((tokens, FB4), lambda i, *_: (0, i)),
                pl.BlockSpec((D2, D1), whole),
                pl.BlockSpec((FB4, D1), lambda i, *_: (i, 0)),
                grad,
                pl.BlockSpec((64, D2), whole),
                pl.BlockSpec((D2, 128), whole),
                pl.BlockSpec((3, D2), whole),
                pl.BlockSpec((SLIDES, 3), whole),
            ],
            out_specs=[
                pl.BlockSpec(memory_space=pl.ANY),
                pl.BlockSpec(memory_space=pl.ANY),
                pl.BlockSpec((SLIDES, 3), whole),
                pl.BlockSpec((3, D2), whole),
            ],
            scratch_shapes=[
                pltpu.VMEM((2, HALF_ROWS, 128), BF),
                pltpu.VMEM((tokens, D1), BF),
                pltpu.VMEM((tokens, D2), BF),
                pltpu.VMEM((2, 8, 128), F32),
                pltpu.SemaphoreType.DMA((14,)),
            ],
        ),
        out_shape=[
            jax.ShapeDtypeStruct((HALF_ROWS, 128), BF),
            jax.ShapeDtypeStruct((HALF_ROWS, 128), BF),
            jax.ShapeDtypeStruct((SLIDES, 3), F32),
            jax.ShapeDtypeStruct((3, D2), F32),
        ],
        compiler_params=params(61),
        name="patch_backward",
    )(
        idx, slide, back, turned, mid, hid, gp, w_embed, w_down, grads, rows, cols, w_class,
        g_logits,
    )


def unpack_kernel(idx_ref, src_ref, *refs):
    up_ref, down_ref, embed_ref, q_ref, k_ref, v_ref, o_ref, av_ref, au_ref, aw_ref = refs[-10:]
    for l in range(12):
        up_ref[:, pl.ds(128 * l, 128)] = src_ref[pl.ds(192 * l, 192), :].astype(F32)
    for i in range(2):
        for l in range(3):
            rows = src_ref[pl.ds(DOWN_AT + 1152 * i + 384 * l, 384), :]
            down_ref[pl.ds(384 * i, 384), pl.ds(128 * l, 128)] = rows.astype(F32)
    for slot, ref in enumerate((q_ref, k_ref, v_ref, o_ref, av_ref, au_ref)):
        at = REST_AT + 192 * slot
        ref[:, pl.ds(0, 128)] = src_ref[pl.ds(at, 96), :].astype(F32)
        ref[:, pl.ds(128, 64)] = src_ref[pl.ds(at + 96, 96), :][:, :64].astype(F32)
    for l in range(3):
        embed_ref[:, pl.ds(128 * l, 128)] = src_ref[pl.ds(EMBED_AT + 96 * l, 96), :].astype(F32)
    tail = src_ref[pl.ds(EMBED_AT - 96, 96), :].astype(F32).T
    aw_ref[:, pl.ds(0, 96)] = tail[64:65, :]
    aw_ref[:, pl.ds(96, 96)] = tail[65:66, :]


def unpack(idx, src, which, earlier=()):
    square = jax.ShapeDtypeStruct((D2, D2), F32)
    half = lambda rows, width: pl.BlockSpec((rows, width), lambda i, idx: (idx[which], 0))
    hbm = pl.BlockSpec(memory_space=pltpu.HBM)
    return pl.pallas_call(
        unpack_kernel,
        grid_spec=pltpu.PrefetchScalarGridSpec(
            num_scalar_prefetch=1,
            grid=(1,),
            in_specs=[pl.BlockSpec((HALF_ROWS, 128), lambda i, idx: (0, 0))] + [hbm] * len(earlier),
            out_specs=[
                half(D1 // 2, F1),
                half(F1 // 2, D1),
                half(D2 // 2, D1),
            ]
            + [half(D2 // 2, D2)] * 6
            + [pl.BlockSpec((1, D2), lambda i, idx: (0, 0))],
        ),
        out_shape=[
            jax.ShapeDtypeStruct((D1, F1), F32),
            jax.ShapeDtypeStruct((F1, D1), F32),
            jax.ShapeDtypeStruct((D2, D1), F32),
            square, square, square, square, square, square,
            jax.ShapeDtypeStruct((1, D2), F32),
        ],
        input_output_aliases={2 + i: i for i in range(len(earlier))},
        compiler_params=params(),
        name="unpack",
    )(idx, src, *earlier)


GRP_AXES = ("zl", "x", "c")
DEV_AXES = ("zh", "y")
ZLXY = ("y", "zl", "x")


def exchange(x, axes):
    return lax.all_to_all(x, axes, split_axis=0, concat_axis=0, tiled=True)


def swap_cores(x):
    return lax.ppermute(x, "c", [(0, 1), (1, 0)])


def spread(x, n):
    return jnp.broadcast_to(x[None], (n,) + x.shape)


def add_pair(x, y):
    return (x.astype(F32) + y.astype(F32)).astype(x.dtype)


def add_over_zh(x):
    got = [lax.ppermute(x, "zh", [(i, i ^ k) for i in range(4)]) for k in (1, 2, 3)]
    a, b, c, d = [y.astype(F32) for y in (x, *got)]
    return ((a + b) + (c + d)).astype(x.dtype)


def add_up(x):
    return jnp.sum(x.astype(F32), axis=0).astype(x.dtype)


def body(
    patches, tissue, region_slide, w_up, w_down, w_embed, w_query, w_key, w_value, w_out,
    att_v, att_u, att_w, w_class, g_logits,
):
    grp = lax.axis_index(GRP_AXES)
    dev = lax.axis_index(DEV_AXES)
    core = lax.axis_index("c")
    first = (dev * GRP + grp) * OWN
    idx = jnp.stack([first, first % 8, first // 8, core, 1 - core, dev * GRP * OWN]).astype(jnp.int32)
    tokens = patches.reshape(-1, D1)
    att_row = att_w.reshape(1, D2)
    class_rows = w_class.T
    feat, mid = patch_forward(tokens, w_up, w_down, w_embed.T)
    wp, ap = gather_weights((w_query, w_key, w_value, w_out, att_v, att_u))
    got = exchange(feat.reshape(GRP, -1, D2), GRP_AXES)
    got = got.reshape(GRP, OWN, PATCH // GRP, D2)
    *kept, part = region_forward(idx, region_slide, got, tissue, wp, ap, att_row)
    z = exchange(part, DEV_AXES)
    df, grads, rows, cols, scalars = region_backward(
        idx, region_slide, tissue, wp, ap, att_row, class_rows, g_logits, kept
    )
    df = join_sums(z, scalars, df)
    hid, gp, turned = patch_slopes(rows, tokens, w_up)
    back = exchange(df.reshape(GRP, -1, PATCH), GRP_AXES).reshape(df.shape)
    mine, other, logits, g_class = patch_backward(
        idx, region_slide, back, turned, mid, hid, gp, w_embed.T, w_down, grads, rows,
        cols, class_rows, g_logits,
    )
    half = add_pair(mine, swap_cores(other))
    chunk = add_up(exchange(half.reshape(PEERS, -1, 128), ZLXY))
    chunk = add_over_zh(chunk)
    half = exchange(spread(chunk, PEERS), ZLXY).reshape(HALF_ROWS, 128)
    other = swap_cores(half)
    grads = unpack(idx, other, 4, unpack(idx, half, 3))
    up, down, embed, query, key, value, out, gv, gu, gw = grads
    return (
        logits, up, down, embed.T, query, key, value, out, gv, gu, gw.reshape(D2), g_class.T,
    )


def solution(mesh):
    fine = Mesh(mesh.devices.reshape(2, 4, 2, 4, 4), GRP_AXES + DEV_AXES)
    placed = (P(DEV_AXES, GRP_AXES, None),) + (P(),) * 14
    return jax.shard_map(
        body,
        mesh=fine,
        in_specs=placed,
        out_specs=(P(),) * 12,
        check_vma=False,
    )
```

time: 158 us -> 152 us (0.962)
  blocking collectives: 66.2 us -> 49 us
  waiting for transfers between devices: 15 us -> 22.1 us
  starting transfers between devices: 27.8 us -> 34.6 us
  local copies, waits for them, and re-layouts: 5.6 us -> 1.35 us
    all_to_all x3 -> x2, blocking collectives: 66.2 us -> 49 us  [exchange(): return lax.all_to_all(x, axes, split_axis=0, concat_axis=0, tiled=True)]
    all_to_all x2 -> x3, waiting for transfers between devices: 6.61 us -> 13.2 us  [exchange(): return lax.all_to_all(x, axes, split_axis=0, concat_axis=0, tiled=True)]
    all_to_all x2 -> x3, starting transfers between devices: 17.2 us -> 22.9 us  [exchange(): return lax.all_to_all(x, axes, split_axis=0, concat_axis=0, tiled=True)]
    pallas_call x1 -> x3, Pallas kernels: 6.76 us -> 12.2 us  [the longest x1 6.33 us: patch_forward(): pl.pallas_call(patch_forward_kernel, grid=(STEPS1,), in_specs=[pl.BlockSp...]
    unnamed x28, local copies, waits for them, and re-layouts: 4.68 us -> 0.93 us
    pallas_call x1, Pallas kernels: 11.3 us -> 8.27 us  [region_backward(): pl.pallas_call(region_backward_kernel, grid_spec=pltpu.PrefetchScalarGrid...]
    pallas_call x1, Pallas kernels: 7.64 us -> 4.69 us  [region_forward(): pl.pallas_call(region_forward_kernel, grid_spec=pltpu.PrefetchScalarGridS...]
    ppermute x2 -> x3, starting transfers between devices: 5.01 us -> 5.74 us  [add_over_zh(): lax.ppermute(x, 'zh', [(i, i ^ k) for i in range(4)])]
  transfers between devices with their start and end apart: 6 -> 8, of which waited for: 5 -> 6; matrix products, arithmetic and copies ran while one was open for 0% -> 0% of each run, Pallas kernels for 9% -> 11%
where the time goes in v4:
time: 152 us; the launch traced here: 151 us
  blocking collectives  49 us (32%)
  Pallas kernels  41.2 us (27%)
  starting transfers between devices  34.6 us (23%)
  waiting for transfers between devices  22.1 us (15%)
  other arithmetic  2.07 us (1%)
    all_to_all x2, blocking collectives, exchange(): return lax.all_to_all(x, axes, split_axis=0, concat_axis=0, tiled=True)  49 us
    all_to_all x3, starting transfers between devices, exchange(): return lax.all_to_all(x, axes, split_axis=0, concat_axis=0, tiled=True)  22.9 us
    all_to_all x3, waiting for transfers between devices, exchange(): return lax.all_to_all(x, axes, split_axis=0, concat_axis=0, tiled=True)  13.2 us
    pallas_call x1, Pallas kernels, patch_backward(): pl.pallas_call(patch_backward_kernel, grid_spec=pltpu.PrefetchScalarGridS...  10.7 us
    pallas_call x1, Pallas kernels, region_backward(): pl.pallas_call(region_backward_kernel, grid_spec=pltpu.PrefetchScalarGrid...  8.27 us
    pallas_call x1, Pallas kernels, patch_forward(): pl.pallas_call(patch_forward_kernel, grid=(STEPS1,), in_specs=[pl.BlockSp...  6.33 us
    ppermute x2, starting transfers between devices, swap_cores(): return lax.ppermute(x, 'c', [(0, 1), (1, 0)])  5.94 us
    pallas_call x1, Pallas kernels, patch_slopes(): pl.pallas_call(patch_slopes_kernel, grid=(STEPS1,), in_specs=[pl.BlockSpe...  5.8 us
  transfers between devices with their start and end apart: 8, of which 6 were waited for; matrix products, arithmetic and copies ran while one was open for 0% of the time, Pallas kernels for 11%

profile of v4, /device:TPU:1, one launch (start us, length us, event | category | flops | bytes accessed | tf_op | source)
XLA Modules:
  0.0 151.2 jit_solution(5148812751914637238)
XLA Ops:
  0.6 0.0 copy-start.7
  0.7 6.3 %patch_forward.1 = (bf16[512,192]{1,0:T(8,128)(2,1)}, bf16[512,384]{1,0:T(8,128)(2,1)}) custom-call(bf16[512,384]{1,0:T(8,128)(2,1)} %bitcast.31, bf16[384,1536]{1,0:T(8,128)(2,1)} %wu_ref.3, bf16[1536,384]{1,0:T(8,128)(2,1)} %wd_ref.3, bf16[192,384]{1,0:T(8,128)(2,1)} %bitcast.29), custom_call_target="tpu_custom_call" | custom-call | tf_op jit(solution)/shard_map/patch_forward/pallas_call | solution.py:87
  7.0 7.2 %all-to-all-start = ((bf16[16,32,192]{2,1,0:T(8,128)(2,1)}), bf16[16,32,192]{2,1,0:T(8,128)(2,1)S(1)}, u32[]{:S(2)}, u32[]{:S(2)}) async-start(bf16[16,32,192]{2,1,0:T(8,128)(2,1)} %bitcast.34), calls=%async_computation | async-start | bytes 524288 | tf_op jit(solution)/shard_map/all_to_all | solution.py:753
  14.2 0.1 stack.27.idx_ref
  14.3 0.0 copy-done.8
  14.3 0.0 copy-done.10
  14.3 0.0 copy-done.11
  14.3 0.0 copy-done.12
  14.3 0.0 copy-start.1
  14.3 0.0 copy-start
  14.3 0.0 copy-start.3
  14.4 0.0 copy-start.6
  14.4 0.1 gather_weights.1
  14.4 0.0 copy-start.4
  14.4 0.0 copy-start.5
  14.5 6.9 %all-to-all-done = bf16[16,32,192]{2,1,0:T(8,128)(2,1)S(1)} async-done(((bf16[16,32,192]{2,1,0:T(8,128)(2,1)}), bf16[16,32,192]{2,1,0:T(8,128)(2,1)S(1)}, u32[]{:S(2)}, u32[]{:S(2)}) %all-to-all-start) | async-done | bytes 196640 | tf_op jit(solution)/shard_map/all_to_all | solution.py:753
  21.4 0.0 copy-done.3
  21.4 4.7 %region_forward.1 = (bf16[2,1536,256]{2,1,0:T(8,128)(2,1)S(1)}, bf16[2,256,192]{2,1,0:T(8,128)(2,1)S(1)}, f32[8,192]{1,0:T(8,128)S(1)}, f32[8,256]{1,0:T(8,128)S...) custom-call(s32[6]{0:T(128)S(1)} %stack.27.idx_ref, ...), custom_call_target="tpu_custom_call" | custom-call | tf_op jit(solution)/shard_map/region_forward/pallas_call | solution.py:260
  26.1 10.0 %all-to-all-start.1 = ((f32[16,8,128]{2,1,0:T(8,128)}), f32[16,8,128]{2,1,0:T(8,128)S(1)}, u32[]{:S(2)}, u32[]{:S(2)}) async-start(f32[16,8,128]{2,1,0:T(8,128)} %get-tuple-element.59), calls=%async_computation.1 | async-start | bytes 131072 | tf_op jit(solution)/shard_map/all_to_all | solution.py:753
  36.1 0.0 copy-done.1
  36.1 0.0 copy-done.4
  36.1 0.0 copy-done.5
  36.1 8.3 %region_backward.1 = (bf16[16,5,16,256]{3,2,1,0:T(8,128)(2,1)}, f32[2,3,2,192,192]{4,3,2,1,0:T(8,128)}, f32[64,192]{1,0:T(8,128)}, f32[192,128]{1,0:T(8,128)}, f32[8,256]{1,0:T(8,128)S(1)}) custom-call(s32[6]{0:T(128)S(1)} %stack.27.idx_ref, s32[512]{0:T(512)S(1)} %copy-done.3, s32[512,256]{1,0:T(8,128)S(1)} %copy-done, ...), custom_call_target="tpu_custom_call" | custom-call | flops 4000000000 | bytes 20000000 | tf_op jit(solution)/shard_map/region_backward/pallas_call | solution.py:406
  44.4 0.7 all-to-all-done.1.z_ref
  45.1 0.8 join_sums.1
  45.9 5.7 %all-to-all-start.2 = ((bf16[16,80,256]{2,1,0:T(8,128)(2,1)}), bf16[16,80,256]{2,1,0:T(8,128)(2,1)S(1)}, u32[]{:S(2)}, u32[]{:S(2)}) async-start(bf16[16,80,256]{2,1,0:T(8,128)(2,1)} %bitcast.28), calls=%async_computation.2 | async-start | bytes 1310720 | tf_op jit(solution)/shard_map/all_to_all | solution.py:753
  51.6 5.8 %patch_slopes.1 = (bf16[1536,512]{1,0:T(8,128)(2,1)}, bf16[512,1536]{1,0:T(8,128)(2,1)}, bf16[384,512]{1,0:T(8,128)(2,1)}) custom-call(f32[64,192]{1,0:T(8,128)} %get-tuple-element.69.after_ref.rows_ref, bf16[512,384]{1,0:T(8,128)(2,1)} %bitcast.32, bf16[384,1536]{1,0:T(8,128)(2,1)} %wu_ref.3), custom_call_target="tpu_custom_call" | custom-call | flops 3000000000 | bytes 12000000 | tf_op jit(solution)/shard_map/patch_slopes/pallas_call | solution.py:129
  57.4 5.5 %all-to-all-done.2 = bf16[16,80,256]{2,1,0:T(8,128)(2,1)S(1)} async-done(((bf16[16,80,256]{2,1,0:T(8,128)(2,1)}), bf16[16,80,256]{2,1,0:T(8,128)(2,1)S(1)}, u32[]{:S(2)}, u32[]{:S(2)}) %all-to-all-start.2) | async-done | bytes 655392 | tf_op jit(solution)/shard_map/all_to_all | solution.py:753
  62.9 0.9 copy-done.13
  63.8 10.7 %patch_backward.1 = (bf16[6144,128]{1,0:T(8,128)(2,1)}, bf16[6144,128]{1,0:T(8,128)(2,1)}, f32[4,3]{1,0:T(4,128)}, f32[3,192]{1,0:T(4,128)}) custom-call(s32[6]{0:T(128)} %copy-done.1, s32[512]{0:T(512)} %slide_ref.5, bf16[16,5,16,256]{3,2,1,0:T(8,128)(2,1)} %bitcast.27, bf16[384,512]{1,0:T(8,128)(2,1)} %get-tuple-element.70.xt_ref, ...), custom_call_target="tpu_custom_call" | custom-call | tf_op jit(solution)/shard_map/patch_backward/pallas_call | solution.py:650
  74.5 1.2 collective-permute-start
  75.7 3.2 %collective-permute-done = bf16[6144,128]{1,0:T(8,128)(2,1)S(1)} collective-permute-done((bf16[6144,128]{1,0:T(8,128)(2,1)}, bf16[6144,128]{1,0:T(8,128)(2,1)S(1)}, u32[]{:S(2)}, u32[]{:S(2)}) %collective-permute-start) | collective-permute-done | bytes 1572896 | tf_op jit(solution)/shard_map/ppermute | solution.py:757
  78.9 1.8 %add_convert_fusion = bf16[6144,128]{1,0:T(8,128)(2,1)S(1)} fusion(bf16[6144,128]{1,0:T(8,128)(2,1)S(1)} %collective-permute-done, bf16[6144,128]{1,0:T(8,128)(2,1)} %get-tuple-element.77), kind=kLoop, calls=%fused_computation | loop fusion | flops 3145728 | bytes 4718592 | tf_op jit(solution)/shard_map/convert_element_type | solution.py:765
  80.8 25.0 %all_to_all.25 = bf16[32,192,128]{2,1,0:T(8,128)(2,1)S(1)} all-to-all(bf16[32,192,128]{2,1,0:T(8,128)(2,1)S(1)} %bitcast.26), channel_id=1, replica_groups=mesh['zl'=2,'x'=4,'c'=2,'zh'=4,'y'=4] {'y','zl','x'}, dimensions={0} | all-to-all | bytes 3145728 | tf_op jit(solution)/shard_map/all_to_all | solution.py:753
  105.8 0.2 reduce_sum.12
  106.0 3.4 %collective-permute-start.3 = (bf16[192,128]{1,0:T(8,128)(2,1)S(1)}, bf16[192,128]{1,0:T(8,128)(2,1)S(1)}, u32[]{:S(2)}, u32[]{:S(2)}) collective-permute-start(bf16[192,128]{1,0:T(8,128)(2,1)S(1)} %reduce_sum.12), channel_id=1, source_target_pairs={{0,12},{4,8},{8,4},{12,0},{1,13},{5,9},{9,5},{13,1},{2,14},{6,10},... | collective-permute-start | bytes 147464 | tf_op jit(solution)/shard_map/ppermute | solution.py:769
  109.4 2.1 %collective-permute-start.2 = (bf16[192,128]{1,0:T(8,128)(2,1)S(1)}, bf16[192,128]{1,0:T(8,128)(2,1)S(1)}, u32[]{:S(2)}, u32[]{:S(2)}) collective-permute-start(bf16[192,128]{1,0:T(8,128)(2,1)S(1)} %reduce_sum.12), channel_id=1, source_target_pairs={{0,8},{4,12},{8,0},{12,4},{1,9},{5,13},{9,1},{13,5},{2,10},{6,14},... | collective-permute-start | bytes 147464 | tf_op jit(solution)/shard_map/ppermute | solution.py:769
  111.5 0.3 collective-permute-start.1
  111.7 0.0 collective-permute-done.3
  111.8 5.0 %collective-permute-done.2 = bf16[192,128]{1,0:T(8,128)(2,1)S(1)} collective-permute-done((bf16[192,128]{1,0:T(8,128)(2,1)S(1)}, bf16[192,128]{1,0:T(8,128)(2,1)S(1)}, u32[]{:S(2)}, u32[]{:S(2)}) %collective-permute-start.2) | collective-permute-done | bytes 49184 | tf_op jit(solution)/shard_map/ppermute | solution.py:769
  116.8 0.0 collective-permute-done.1
  116.8 0.3 broadcast_in_dim.2
  117.2 0.0 copy-start.2
  117.2 24.0 %all_to_all.26 = bf16[32,192,128]{2,1,0:T(8,128)(2,1)S(1)} all-to-all(bf16[32,192,128]{2,1,0:T(8,128)(2,1)S(1)} %broadcast_in_dim.2), channel_id=1, replica_groups=mesh['zl'=2,'x'=4,'c'=2,'zh'=4,'y'=4] {'y','zl','x'}, dimensions={0} | all-to-all | bytes 3145728 | tf_op jit(solution)/shard_map/all_to_all | solution.py:753
  141.2 4.7 %collective-permute-start.4 = (bf16[6144,128]{1,0:T(8,128)(2,1)S(1)}, bf16[6144,128]{1,0:T(8,128)(2,1)S(1)}, u32[]{:S(2)}, u32[]{:S(2)}) collective-permute-start(bf16[6144,128]{1,0:T(8,128)(2,1)S(1)} %bitcast.19), channel_id=1, source_target_pairs={{0,16},{16,0},{1,17},{17,1},{2,18},{18,2},{3,19},{19,3},{4,20},{20... | collective-permute-start | bytes 4718600 | tf_op jit(solution)/shard_map/ppermute | solution.py:757
  145.9 2.3 %unpack.2 = (f32[384,1536]{1,0:T(8,128)}, f32[1536,384]{1,0:T(8,128)}, f32[192,384]{1,0:T(8,128)}, f32[192,192]{1,0:T(8,128)}, f32[192,192]{1,0:T(8,128)}, /*ind...) custom-call(s32[6]{0:T(128)S(1)} %copy-done.2, ...), custom_call_target="tpu_custom_call" | custom-call | tf_op jit(solution)/shard_map/unpack/pallas_call | solution.py:720
  148.2 0.7 collective-permute-done.4.src_ref
  148.9 2.3 %unpack.3 = (f32[384,1536]{1,0:T(8,128)}, f32[1536,384]{1,0:T(8,128)}, f32[192,384]{1,0:T(8,128)}, f32[192,192]{1,0:T(8,128)}, f32[192,192]{1,0:T(8,128)}, /*ind...) custom-call(s32[6]{0:T(128)S(1)} %copy-done.2, ...), custom_call_target="tpu_custom_call", output_to_operand_aliasing={{0}: (2, {}), {1}: (3, {}), {2}: (4, {}), {3}: (5, {}), {4}... | custom-call | tf_op jit(solution)/shard_map/unpack/pallas_call | solution.py:720
  (12 shorter events, 0.1 us)
Async XLA Ops:
  0.6 13.6 %copy-start.7 = (f32[192,192]{1,0:T(8,128)S(1)}, f32[192,192]{1,0:T(8,128)}, u32[]{:S(2)}) copy-start(f32[192,192]{1,0:T(8,128)} %refs_4_.1) | copy-start | bytes 442372
  0.7 13.6 %copy-start.8 = (f32[192,192]{1,0:T(8,128)S(1)}, f32[192,192]{1,0:T(8,128)}, u32[]{:S(2)}) copy-start(f32[192,192]{1,0:T(8,128)} %refs_5_.1) | copy-start | bytes 442372
  0.7 13.6 %copy-start.9 = (bf16[192,192]{1,0:T(8,128)(2,1)S(1)}, bf16[192,192]{1,0:T(8,128)(2,1)}, u32[]{:S(2)}) copy-start(bf16[192,192]{1,0:T(8,128)(2,1)} %refs_0_.1) | copy-start | bytes 221188
  0.7 13.6 %copy-start.10 = (bf16[192,192]{1,0:T(8,128)(2,1)S(1)}, bf16[192,192]{1,0:T(8,128)(2,1)}, u32[]{:S(2)}) copy-start(bf16[192,192]{1,0:T(8,128)(2,1)} %refs_1_.1) | copy-start | bytes 221188
  0.7 13.6 %copy-start.11 = (bf16[192,192]{1,0:T(8,128)(2,1)S(1)}, bf16[192,192]{1,0:T(8,128)(2,1)}, u32[]{:S(2)}) copy-start(bf16[192,192]{1,0:T(8,128)(2,1)} %refs_2_.1) | copy-start | bytes 221188
  0.7 13.6 %copy-start.12 = (bf16[192,192]{1,0:T(8,128)(2,1)S(1)}, bf16[192,192]{1,0:T(8,128)(2,1)}, u32[]{:S(2)}) copy-start(bf16[192,192]{1,0:T(8,128)(2,1)} %refs_3_.1) | copy-start | bytes 221188
  7.0 14.3 %all-to-all-start = ((bf16[16,32,192]{2,1,0:T(8,128)(2,1)}), bf16[16,32,192]{2,1,0:T(8,128)(2,1)S(1)}, u32[]{:S(2)}, u32[]{:S(2)}) async-start(bf16[16,32,192]{2,1,0:T(8,128)(2,1)} %bitcast.34), calls=%async_computation | async-start | bytes 524288 | tf_op jit(solution)/shard_map/all_to_all | solution.py:753
  14.3 21.8 %copy-start.1 = (s32[6]{0:T(128)}, s32[6]{0:T(128)S(1)}, u32[]{:S(2)}) copy-start(s32[6]{0:T(128)S(1)} %stack.27.idx_ref) | copy-start | bytes 76
  14.3 7.0 %copy-start = (s32[512,256]{1,0:T(8,128)S(1)}, s32[512,256]{1,0:T(8,128)}, u32[]{:S(2)}) copy-start(s32[512,256]{1,0:T(8,128)} %tis_ref.3) | copy-start | bytes 1572868
  14.3 7.0 %copy-start.3 = (s32[512]{0:T(512)S(1)}, s32[512]{0:T(512)}, u32[]{:S(2)}) copy-start(s32[512]{0:T(512)} %slide_ref.5) | copy-start | bytes 6148
  14.4 7.0 %copy-start.6 = (f32[192]{0:T(256)S(1)}, f32[192]{0:T(256)}, u32[]{:S(2)}) copy-start(f32[192]{0:T(256)} %param.27) | copy-start | bytes 2308
  14.4 21.7 %copy-start.4 = (f32[192,3]{0,1:T(4,128)S(1)}, f32[192,3]{0,1:T(4,128)}, u32[]{:S(2)}) copy-start(f32[192,3]{0,1:T(4,128)} %param.28) | copy-start | bytes 6916
  14.4 21.7 %copy-start.5 = (f32[4,3]{1,0:T(4,128)S(1)}, f32[4,3]{1,0:T(4,128)}, u32[]{:S(2)}) copy-start(f32[4,3]{1,0:T(4,128)} %gl_ref.3) | copy-start | bytes 148
  26.1 19.1 %all-to-all-start.1 = ((f32[16,8,128]{2,1,0:T(8,128)}), f32[16,8,128]{2,1,0:T(8,128)S(1)}, u32[]{:S(2)}, u32[]{:S(2)}) async-start(f32[16,8,128]{2,1,0:T(8,128)} %get-tuple-element.59), calls=%async_computation.1 | async-start | bytes 131072 | tf_op jit(solution)/shard_map/all_to_all | solution.py:753
  45.9 17.0 %all-to-all-start.2 = ((bf16[16,80,256]{2,1,0:T(8,128)(2,1)}), bf16[16,80,256]{2,1,0:T(8,128)(2,1)S(1)}, u32[]{:S(2)}, u32[]{:S(2)}) async-start(bf16[16,80,256]{2,1,0:T(8,128)(2,1)} %bitcast.28), calls=%async_computation.2 | async-start | bytes 1310720 | tf_op jit(solution)/shard_map/all_to_all | solution.py:753
  62.9 0.9 copy-start.13
  74.5 4.5 %collective-permute-start = (bf16[6144,128]{1,0:T(8,128)(2,1)}, bf16[6144,128]{1,0:T(8,128)(2,1)S(1)}, u32[]{:S(2)}, u32[]{:S(2)}) collective-permute-start(bf16[6144,128]{1,0:T(8,128)(2,1)} %get-tuple-element.78), channel_id=1, source_target_pairs={{0,16},{16,0},{1,17},{17,1},{2,18},{18,2},{3,19},{19,3},{4,20},{20... | collective-permute-start | bytes 4718600 | tf_op jit(solution)/shard_map/ppermute | solution.py:757
  106.0 5.7 %collective-permute-start.3 = (bf16[192,128]{1,0:T(8,128)(2,1)S(1)}, bf16[192,128]{1,0:T(8,128)(2,1)S(1)}, u32[]{:S(2)}, u32[]{:S(2)}) collective-permute-start(bf16[192,128]{1,0:T(8,128)(2,1)S(1)} %reduce_sum.12), channel_id=1, source_target_pairs={{0,12},{4,8},{8,4},{12,0},{1,13},{5,9},{9,5},{13,1},{2,14},{6,10},... | collective-permute-start | bytes 147464 | tf_op jit(solution)/shard_map/ppermute | solution.py:769
  109.4 7.4 %collective-permute-start.2 = (bf16[192,128]{1,0:T(8,128)(2,1)S(1)}, bf16[192,128]{1,0:T(8,128)(2,1)S(1)}, u32[]{:S(2)}, u32[]{:S(2)}) collective-permute-start(bf16[192,128]{1,0:T(8,128)(2,1)S(1)} %reduce_sum.12), channel_id=1, source_target_pairs={{0,8},{4,12},{8,0},{12,4},{1,9},{5,13},{9,1},{13,5},{2,10},{6,14},... | collective-permute-start | bytes 147464 | tf_op jit(solution)/shard_map/ppermute | solution.py:769
  111.5 5.3 %collective-permute-start.1 = (bf16[192,128]{1,0:T(8,128)(2,1)S(1)}, bf16[192,128]{1,0:T(8,128)(2,1)S(1)}, u32[]{:S(2)}, u32[]{:S(2)}) collective-permute-start(bf16[192,128]{1,0:T(8,128)(2,1)S(1)} %reduce_sum.12), channel_id=1, source_target_pairs={{0,4},{4,0},{8,12},{12,8},{1,5},{5,1},{9,13},{13,9},{2,6},{6,2},{1... | collective-permute-start | bytes 147464 | tf_op jit(solution)/shard_map/ppermute | solution.py:769
  117.2 28.7 %copy-start.2 = (s32[6]{0:T(128)S(1)}, s32[6]{0:T(128)}, u32[]{:S(2)}) copy-start(s32[6]{0:T(128)} %copy-done.1) | copy-start | bytes 76
  141.2 7.8 %collective-permute-start.4 = (bf16[6144,128]{1,0:T(8,128)(2,1)S(1)}, bf16[6144,128]{1,0:T(8,128)(2,1)S(1)}, u32[]{:S(2)}, u32[]{:S(2)}) collective-permute-start(bf16[6144,128]{1,0:T(8,128)(2,1)S(1)} %bitcast.19), channel_id=1, source_target_pairs={{0,16},{16,0},{1,17},{17,1},{2,18},{18,2},{3,19},{19,3},{4,20},{20... | collective-permute-start | bytes 4718600 | tf_op jit(solution)/shard_map/ppermute | solution.py:757

commit v5 on v4

--- a/solution.py
+++ b/solution.py
@@ -54,54 +54,37 @@
     return pltpu.CompilerParams(vmem_limit_bytes=mib * MIB)
 
 
-def patch_forward_kernel(x_ref, wu_ref, wd_ref, we_ref, feat_ref, mid_ref, acc):
-    step = pl.program_id(0)
+STEPS1 = 4
+FB1 = F1 // STEPS1
+
+
+def begin(copies):
+    for copy in copies:
+        copy.start()
+    return copies
+
+
+def patch_forward_kernel(x_ref, wu_ref, wd_ref, we_ref, feat_ref, mid_ref):
     x = x_ref[...]
     pre = nn(x, wu_ref[...])
-    sq = pre * pre
-    t = jnp.tanh(GELU_C * (pre + GELU_A * (pre * sq)))
-    part = nn((pre * (0.5 + 0.5 * t)).astype(BF), wd_ref[...])
-
-    @pl.when(step == 0)
-    def _():
-        acc[...] = x.astype(F32) + part
-
-    @pl.when(step > 0)
-    def _():
-        acc[...] += part
-
-    @pl.when(step == pl.num_programs(0) - 1)
-    def _():
-        mid = acc[...].astype(BF)
-        mid_ref[...] = mid
-        feat_ref[...] = nt(mid, we_ref[...]).astype(BF)
-
-
-STEPS1 = 4
-FB1 = F1 // STEPS1
+    t = jnp.tanh(GELU_C * (pre + GELU_A * (pre * (pre * pre))))
+    hid = (pre * (0.5 + 0.5 * t)).astype(BF)
+    mid = (x.astype(F32) + nn(hid, wd_ref[...])).astype(BF)
+    mid_ref[...] = mid
+    feat_ref[...] = nt(mid, we_ref[...]).astype(BF)
 
 
 def patch_forward(tokens, w_up, w_down, w_embed):
     rows = tokens.shape[0]
-    whole = lambda i: (0, 0)
+    vmem = pl.BlockSpec(memory_space=pltpu.VMEM)
     return pl.pallas_call(
         patch_forward_kernel,
-        grid=(STEPS1,),
-        in_specs=[
-            pl.BlockSpec((rows, D1), whole),
-            pl.BlockSpec((D1, FB1), lambda i: (0, i)),
-            pl.BlockSpec((FB1, D1), lambda i: (i, 0)),
-            pl.BlockSpec((D2, D1), whole),
-        ],
-        out_specs=[
-            pl.BlockSpec((rows, D2), whole),
-            pl.BlockSpec((rows, D1), whole),
-        ],
+        in_specs=[vmem] * 4,
+        out_specs=[vmem] * 2,
         out_shape=[
             jax.ShapeDtypeStruct((rows, D2), BF),
             jax.ShapeDtypeStruct((rows, D1), BF),
         ],
-        scratch_shapes=[pltpu.VMEM((rows, D1), F32)],
         compiler_params=params(61),
         name="patch_forward",
     )(tokens, w_up, w_down, w_embed)
@@ -195,56 +178,50 @@
     p_ref, x_ref, asum_ref, reg_ref, tanh_ref, gate_ref, w_ref,
     part_ref,
 ):
-    r = pl.program_id(0)
-    trow = tissue_row(idx_ref, tis_ref, r)
-    tcol = column_of(trow, D2)
-    x = (f_ref[...].reshape(PATCH, D2).astype(F32) * tcol).astype(BF)
-    q = nn(x, wp_ref[0]).astype(BF)
-    k = nn(x, wp_ref[1])
-    v = nn(x, wp_ref[2]).astype(BF)
-    x_ref[0] = x
-    spread = jnp.zeros((PATCH, D2), F32)
-    for h in range(HEADS):
-        mask = head_mask(h, (1, D2), 1)
-        st = nt((k * mask).astype(BF), q) * SCALE
-        top = jnp.max(st, axis=0, keepdims=True)
-        ex = jnp.exp(st - top)
-        total = jnp.sum(ex, axis=0, keepdims=True)
-        pb = (ex * (1.0 / total)).astype(BF)
-        p_ref[0, pl.ds(h * PATCH, PATCH), :] = pb
-        spread = spread + nn(pb, (tcol * mask).astype(BF))
-    asum = jnp.sum(spread * v.astype(F32), axis=0, keepdims=True)
-    xsum = jnp.sum(x.astype(F32), axis=0, keepdims=True)
-    count = jnp.maximum(jnp.sum(trow, axis=1, keepdims=True), 1.0)
-    mixed = xsum + nn(jnp.broadcast_to(asum, (8, D2)), wp_ref[3].astype(F32), HIGHEST)[0:1]
-
-    @pl.when(r == 0)
-    def _():
-        lane = lax.broadcasted_iota(jnp.int32, (8, PATCH), 1)
-        reg_ref[...] = jnp.where(lane < D2, 0.0, 1.0)
-        asum_ref[...] = jnp.zeros_like(asum_ref)
-
-    asum_ref[pl.ds(r, 1), :] = asum
-    reg_ref[pl.ds(r, 1), pl.ds(0, D2)] = mixed / count
-
-    @pl.when(r == OWN - 1)
-    def _():
-        region = reg_ref[:, pl.ds(0, D2)]
-        tanh_part = jnp.tanh(nn(region, ap_ref[0], HIGHEST))
-        gate_part = jax.nn.sigmoid(nn(region, ap_ref[1], HIGHEST))
-        tanh_ref[...] = tanh_part
-        gate_ref[...] = gate_part
-        score = jnp.sum(tanh_part * gate_part * aw_ref[...], axis=1, keepdims=True)
-        weight = jnp.exp(score)
-        w_ref[...] = jnp.broadcast_to(weight, w_ref.shape)
-        wide = reg_ref[...] * weight
-        slot = lax.broadcasted_iota(jnp.int32, (SLIDES, 1), 0)
-        sums = jnp.zeros((SLIDES, PATCH), F32)
-        for i in range(OWN):
-            own = (slot == slide_ref[idx_ref[0] + i]).astype(F32)
-            sums = sums + own * wide[i : i + 1]
-        both = jnp.concatenate([sums[:, :128], sums[:, 128:]], axis=0)
-        part_ref[...] = jnp.broadcast_to(both[None], part_ref.shape)
+    lane = lax.broadcasted_iota(jnp.int32, (8, PATCH), 1)
+    reg_ref[...] = jnp.where(lane < D2, 0.0, 1.0)
+    asum_ref[...] = jnp.zeros_like(asum_ref)
+    for r in range(OWN):
+        trow = tissue_row(idx_ref, tis_ref, r)
+        tcol = column_of(trow, D2)
+        x = (f_ref[:, r].reshape(PATCH, D2).astype(F32) * tcol).astype(BF)
+        q = nn(x, wp_ref[0]).astype(BF)
+        k = nn(x, wp_ref[1])
+        v = nn(x, wp_ref[2]).astype(BF)
+        x_ref[r] = x
+        spread = jnp.zeros((PATCH, D2), F32)
+        for h in range(HEADS):
+            mask = head_mask(h, (1, D2), 1)
+            st = nt((k * mask).astype(BF), q) * SCALE
+            top = jnp.max(st, axis=0, keepdims=True)
+            ex = jnp.exp(st - top)
+            total = jnp.sum(ex, axis=0, keepdims=True)
+            pb = (ex * (1.0 / total)).astype(BF)
+            p_ref[r, pl.ds(h * PATCH, PATCH), :] = pb
+            spread = spread + nn(pb, (tcol * mask).astype(BF))
+        asum = jnp.sum(spread * v.astype(F32), axis=0, keepdims=True)
+        xsum = jnp.sum(x.astype(F32), axis=0, keepdims=True)
+        count = jnp.maximum(jnp.sum(trow, axis=1, keepdims=True), 1.0)
+        mixed = xsum + nn(jnp.broadcast_to(asum, (8, D2)), wp_ref[3].astype(F32), HIGHEST)[0:1]
+        asum_ref[pl.ds(r, 1), :] = asum
+        reg_ref[pl.ds(r, 1), pl.ds(0, D2)] = mixed / count
+
+    region = reg_ref[:, pl.ds(0, D2)]
+    tanh_part = jnp.tanh(nn(region, ap_ref[0], HIGHEST))
+    gate_part = jax.nn.sigmoid(nn(region, ap_ref[1], HIGHEST))
+    tanh_ref[...] = tanh_part
+    gate_ref[...] = gate_part
+    score = jnp.sum(tanh_part * gate_part * aw_ref[...], axis=1, keepdims=True)
+    weight = jnp.exp(score)
+    w_ref[...] = jnp.broadcast_to(weight, w_ref.shape)
+    wide = reg_ref[...] * weight
+    slot = lax.broadcasted_iota(jnp.int32, (SLIDES, 1), 0)
+    sums = jnp.zeros((SLIDES, PATCH), F32)
+    for i in range(OWN):
+        own = (slot == slide_ref[idx_ref[0] + i]).astype(F32)
+        sums = sums + own * wide[i : i + 1]
+    both = jnp.concatenate([sums[:, :128], sums[:, 128:]], axis=0)
+    part_ref[...] = jnp.broadcast_to(both[None], part_ref.shape)
 
 
 def packed_specs():
@@ -256,14 +233,14 @@
 
 def region_forward(idx, slide, got, tissue, wp, ap, att_w):
     row8 = lambda width: pl.BlockSpec((8, width), lambda r, *_: (0, 0))
-    per_region = lambda rows, width: pl.BlockSpec((1, rows, width), lambda r, *_: (r, 0, 0))
+    per_region = lambda rows, width: pl.BlockSpec((OWN, rows, width), lambda r, *_: (0, 0, 0))
     return pl.pallas_call(
         region_forward_kernel,
         grid_spec=pltpu.PrefetchScalarGridSpec(
             num_scalar_prefetch=2,
-            grid=(OWN,),
+            grid=(1,),
             in_specs=[
-                pl.BlockSpec((GRP, 1, PATCH // GRP, D2), lambda r, *_: (0, r, 0, 0)),
+                pl.BlockSpec((GRP, OWN, PATCH // GRP, D2), lambda r, *_: (0, 0, 0, 0)),
                 pl.BlockSpec((8, PATCH), lambda r, idx, _: (idx[2], 0)),
                 *packed_specs(),
                 pl.BlockSpec((1, D2), lambda r, *_: (0, 0)),
@@ -340,10 +317,10 @@
 def pull_back(r, idx_ref, tis_ref, wp_ref, p_ref, x_ref, rows_ref, df_ref, grad_ref, kt_s, dqt_s):
     trow = tissue_row(idx_ref, tis_ref, r)
     tcol = column_of(trow, D2)
-    x = x_ref[0]
+    x = x_ref[r]
     q = nn(x, wp_ref[0]).astype(BF).astype(F32)
     v = nn(x, wp_ref[2]).astype(BF)
-    kt_s[...] = nn(x, wp_ref[1]).T.astype(BF)
+    kt_s[r] = nn(x, wp_ref[1]).T.astype(BF)
     spread = jnp.zeros((PATCH, D2), F32)
     dm = [rows_ref[pl.ds(8 * (2 + j) + r, 1), :] for j in range(2)]
     da = [rows_ref[pl.ds(8 * (6 + j) + r, 1), :].astype(BF).astype(F32) for j in range(2)]
@@ -351,30 +328,30 @@
     dk = [jnp.zeros((PATCH, D2), F32) for _ in range(2)]
     for h in range(HEADS):
         e = nn(v, (da_col * head_mask(h, (D2, 1), 0)).astype(BF))
-        pb = p_ref[0, pl.ds(h * PATCH, PATCH), :]
+        pb = p_ref[r, pl.ds(h * PATCH, PATCH), :]
         pt = pb.astype(F32)
         mask = head_mask(h, (1, D2), 1)
         spread = spread + nn(pb, (tcol * mask).astype(BF))
         q_head = (q * mask).astype(BF)
-        k_head = kt_s[pl.ds(h * HEAD_DIM, HEAD_DIM), :]
+        k_head = kt_s[r, pl.ds(h * HEAD_DIM, HEAD_DIM), :]
         for j in range(2):
             e_j = e[:, 128 * j : 128 * j + 128]
             pe = pt * jnp.concatenate([e_j, e_j], axis=1)
             ds = (pe - pt * jnp.sum(pe, axis=0, keepdims=True)).astype(BF)
             dk[j] = dk[j] + nn(ds, q_head)
-            dqt_s[j, pl.ds(h * HEAD_DIM, HEAD_DIM), :] = nn(k_head, ds)
+            dqt_s[r, j, pl.ds(h * HEAD_DIM, HEAD_DIM), :] = nn(k_head, ds)
     xt = x.astype(F32).T.astype(BF)
     for j in range(2):
-        dq = (dqt_s[j] * (trow * SCALE)).T.astype(BF)
+        dq = (dqt_s[r, j] * (trow * SCALE)).T.astype(BF)
         dk_j = (dk[j] * SCALE).astype(BF)
         dv = (spread * da[j]).astype(BF)
-        grad_ref[0, 0, j] = nn(xt, dq)
-        grad_ref[0, 1, j] = nn(xt, dk_j)
-        grad_ref[0, 2, j] = nn(xt, dv)
+        grad_ref[r, 0, j] = nn(xt, dq)
+        grad_ref[r, 1, j] = nn(xt, dk_j)
+        grad_ref[r, 2, j] = nn(xt, dv)
         d_flat = dm[j] + nt(dq, wp_ref[0]) + nt(dk_j, wp_ref[1]) + nt(dv, wp_ref[2])
         d_flat = (tcol * d_flat).astype(BF).reshape(GRP, PATCH // GRP, D2)
-        df_ref[:, j, :, pl.ds(0, D2)] = d_flat
-        df_ref[:, j, :, pl.ds(D2, 64)] = jnp.zeros((GRP, PATCH // GRP, 64), BF)
+        df_ref[:, 2 * r + j, :, pl.ds(0, D2)] = d_flat
+        df_ref[:, 2 * r + j, :, pl.ds(D2, 64)] = jnp.zeros((GRP, PATCH // GRP, 64), BF)
 
 
 BLOCKS = 2 * OWN + 1
@@ -386,28 +363,24 @@
     df_ref, grad_ref, rows_ref, cols_ref, scal_ref,
     kt_s, dqt_s,
 ):
-    r = pl.program_id(0)
-
-    @pl.when(r == 0)
-    def _():
-        directions(
-            idx_ref, slide_ref, tis_ref, wp_ref, ap_ref, aw_ref, wc_ref, gl_ref,
-            asum_ref, reg_ref, tanh_ref, gate_ref, w_ref, rows_ref, cols_ref, scal_ref,
+    directions(
+        idx_ref, slide_ref, tis_ref, wp_ref, ap_ref, aw_ref, wc_ref, gl_ref,
+        asum_ref, reg_ref, tanh_ref, gate_ref, w_ref, rows_ref, cols_ref, scal_ref,
+    )
+    for r in range(OWN):
+        pull_back(
+            r, idx_ref, tis_ref, wp_ref, p_ref, x_ref, rows_ref, df_ref, grad_ref, kt_s, dqt_s
         )
-
-    pull_back(
-        r, idx_ref, tis_ref, wp_ref, p_ref, x_ref, rows_ref, df_ref, grad_ref, kt_s, dqt_s
-    )
 
 
 def region_backward(idx, slide, tissue, wp, ap, att_w, w_class, g_logits, kept):
     whole = lambda rows, width: pl.BlockSpec((rows, width), lambda r, *_: (0, 0))
-    region = lambda rows, width: pl.BlockSpec((1, rows, width), lambda r, *_: (r, 0, 0))
+    region = lambda rows, width: pl.BlockSpec((OWN, rows, width), lambda r, *_: (0, 0, 0))
     return pl.pallas_call(
         region_backward_kernel,
         grid_spec=pltpu.PrefetchScalarGridSpec(
             num_scalar_prefetch=2,
-            grid=(OWN,),
+            grid=(1,),
             in_specs=[
                 pl.BlockSpec((8, PATCH), lambda r, idx, _: (idx[2], 0)),
                 *packed_specs(),
@@ -417,13 +390,16 @@
                 whole(8, D2), whole(8, PATCH), whole(8, D2), whole(8, D2), whole(8, 128),
             ],
             out_specs=[
-                pl.BlockSpec((GRP, 2, PATCH // GRP, PATCH), lambda r, *_: (0, r, 0, 0)),
-                pl.BlockSpec((1, 3, 2, D2, D2), lambda r, *_: (r, 0, 0, 0, 0)),
+                pl.BlockSpec((GRP, 2 * OWN, PATCH // GRP, PATCH), lambda r, *_: (0, 0, 0, 0)),
+                pl.BlockSpec((OWN, 3, 2, D2, D2), lambda r, *_: (0, 0, 0, 0, 0)),
                 whole(64, D2),
                 whole(D2, 128),
                 whole(8, PATCH),
             ],
-            scratch_shapes=[pltpu.VMEM((D2, PATCH), BF), pltpu.VMEM((2, D2, PATCH), F32)],
+            scratch_shapes=[
+                pltpu.VMEM((OWN, D2, PATCH), BF),
+                pltpu.VMEM((OWN, 2, D2, PATCH), F32),
+            ],
         ),
         out_shape=[
             pltpu.HBM((GRP, BLOCKS, PATCH // GRP, PATCH), BF),
@@ -478,10 +454,6 @@
         compiler_params=params(24),
         name="join_sums",
     )(z, scalars, df)
-
-
-STEPS4 = 4
-FB4 = F1 // STEPS4
 
 
 def put_rest(pack, slot, grad, fill=None):
@@ -554,154 +526,118 @@
 
 
 def patch_backward_kernel(
-    idx_ref, slide_ref, back_ref, xt_ref, mid_ref, hid_ref, gp_ref, we_ref, wd_ref,
-    grad_ref, rows_ref, cols_ref, wc_ref, gl_ref,
+    idx_ref, slide_ref, back_in, xt_in, mid_in, hid_in, gp_in, we_in, wd_in, grad_in,
+    rows_ref, cols_ref, wc_ref, gl_ref,
     mine_ref, other_ref, logits_ref, gc_ref,
-    pack, dmid_s, df_s, pq_s, sems,
+    back_ref, xt_ref, mid_ref, hid_ref, gp_ref, we_ref, wd_ref, grad_ref,
+    pack, df_s, pq_s, in_sems, sems,
 ):
-    step = pl.program_id(0)
     core = idx_ref[3]
-
-    def up_copies(i):
-        rows = pl.ds(pl.multiple_of(576 * i, 64), 576)
-        return (
-            pltpu.make_async_copy(pack.at[core, rows], mine_ref.at[rows], sems.at[2 * i]),
-            pltpu.make_async_copy(pack.at[1 - core, rows], other_ref.at[rows], sems.at[2 * i + 1]),
+    pairs = (
+        (back_in, back_ref), (we_in, we_ref), (wd_in, wd_ref), (gp_in, gp_ref), (xt_in, xt_ref),
+        (hid_in, hid_ref), (mid_in, mid_ref), (grad_in, grad_ref),
+    )
+    fetch = begin(
+        [pltpu.make_async_copy(a, b, in_sems.at[i]) for i, (a, b) in enumerate(pairs)]
+    )
+    sent = []
+
+    def send(low, size):
+        rows = pl.ds(low, size)
+        at = len(sent)
+        sent.extend(
+            begin(
+                [
+                    pltpu.make_async_copy(
+                        pack.at[core, rows], mine_ref.at[rows], sems.at[at]
+                    ),
+                    pltpu.make_async_copy(
+                        pack.at[1 - core, rows], other_ref.at[rows], sems.at[at + 1]
+                    ),
+                ]
+            )
         )
 
-    def down_copy(i, dst):
-        rows = pl.ds(pl.multiple_of(DOWN_AT + 1152 * lax.rem(i, 2), 128), 1152)
-        return pltpu.make_async_copy(pack.at[i // 2, rows], dst.at[rows], sems.at[8 + i])
-
-    def rest_copies():
-        rows = pl.ds(REST_AT, HALF_ROWS - REST_AT)
-        return (
-            pltpu.make_async_copy(pack.at[core, rows], mine_ref.at[rows], sems.at[12]),
-            pltpu.make_async_copy(pack.at[1 - core, rows], other_ref.at[rows], sems.at[13]),
-        )
-
-    @pl.when(step == 0)
-    def _():
-        finish_slides(
-            idx_ref, slide_ref, back_ref, rows_ref, cols_ref, wc_ref, gl_ref, logits_ref, gc_ref,
-            df_s, pq_s, pack,
-        )
-        df = df_s[...]
-        dmid_s[...] = nn(df, we_ref[...]).astype(BF)
-        g_embed = tn(df, mid_ref[...]).astype(BF)
+    fetch[0].wait()
+    finish_slides(
+        idx_ref, slide_ref, back_ref, rows_ref, cols_ref, wc_ref, gl_ref, logits_ref, gc_ref,
+        df_s, pq_s, pack,
+    )
+    df = df_s[...]
+    fetch[1].wait()
+    dmid = nn(df, we_ref[...]).astype(BF)
+    for i in range(2, 5):
+        fetch[i].wait()
+    d_pre = (nt(dmid, wd_ref[...]) * gp_ref[...].astype(F32)).astype(BF)
+    g_up = nn(xt_ref[...], d_pre).astype(BF)
+    for l in range(F1 // 128):
         for half in range(2):
-            for l in range(3):
-                block = g_embed[96 * half : 96 * half + 96, 128 * l : 128 * l + 128]
-                pack[half, pl.ds(EMBED_AT + 96 * l, 96), :] = block
-            pack[half, pl.ds(PAD_AT, 96), :] = jnp.zeros((96, 128), BF)
-
-    @pl.when(step > 0)
-    def _():
+            block = g_up[192 * half : 192 * half + 192, 128 * l : 128 * l + 128]
+            pack[half, pl.ds(192 * l, 192), :] = block
+    send(0, DOWN_AT)
+    fetch[5].wait()
+    g_down = nn(hid_ref[...], dmid).astype(BF)
+    for half in range(2):
+        for l in range(3):
+            block = g_down[768 * half : 768 * half + 768, 128 * l : 128 * l + 128]
+            pack[half, pl.ds(DOWN_AT + 768 * l, 768), :] = block
+    send(DOWN_AT, REST_AT - DOWN_AT)
+    fetch[6].wait()
+    g_embed = tn(df, mid_ref[...]).astype(BF)
+    for half in range(2):
+        for l in range(3):
+            block = g_embed[96 * half : 96 * half + 96, 128 * l : 128 * l + 128]
+            pack[half, pl.ds(EMBED_AT + 96 * l, 96), :] = block
+        pack[half, pl.ds(PAD_AT, 96), :] = jnp.zeros((96, 128), BF)
+    fetch[7].wait()
+    for slot in range(3):
         grad = jnp.zeros((D2, D2), F32)
         for i in range(OWN):
             for j in range(2):
-                grad = grad + pq_s[j, i : i + 1, 0:1] * grad_ref[i, 0, j]
-        put_rest(pack, step - 1, grad)
-
-    dmid = dmid_s[...]
-    d_pre = (nt(dmid, wd_ref[...]) * gp_ref[...].astype(F32)).astype(BF)
-    g_up = nn(xt_ref[...], d_pre).astype(BF)
-    for half in range(2):
-        for l in range(3):
-            block = g_up[192 * half : 192 * half + 192, 128 * l : 128 * l + 128]
-            pack[half, pl.ds(pl.multiple_of(576 * step + 192 * l, 64), 192), :] = block
-    g_down = nn(hid_ref[...], dmid).astype(BF)
-    at = DOWN_AT + 1152 * lax.rem(step, 2)
-    for l in range(3):
-        rows = pl.ds(pl.multiple_of(at + 384 * l, 128), 384)
-        pack[step // 2, rows, :] = g_down[:, 128 * l : 128 * l + 128]
-
-    for copy in up_copies(step):
-        copy.start()
-
-    @pl.when(step // 2 == core)
-    def _():
-        down_copy(step, mine_ref).start()
-
-    @pl.when(step // 2 != core)
-    def _():
-        down_copy(step, other_ref).start()
-
-    @pl.when(step == pl.num_programs(0) - 1)
-    def _():
-        for copy in rest_copies():
-            copy.start()
-        for copy in rest_copies():
-            copy.wait()
-        for i in range(STEPS4):
-            for copy in up_copies(i):
-                copy.wait()
-            down_copy(i, mine_ref).wait()
+                grad = grad + pq_s[j, i : i + 1, 0:1] * grad_ref[i, slot, j]
+        put_rest(pack, slot, grad)
+    send(REST_AT, HALF_ROWS - REST_AT)
+    for copy in sent:
+        copy.wait()
 
 
 def patch_backward(
     idx, slide, back, turned, mid, hid, gp, w_embed, w_down, grads, rows, cols, w_class, g_logits
 ):
-    tokens = turned.shape[1]
-    whole = lambda i, *_: (0, 0)
-    grad = pl.BlockSpec(
-        (OWN, 1, 2, D2, D2), lambda i, *_: (0, jnp.maximum(i - 1, 0), 0, 0, 0)
-    )
+    hbm = pl.BlockSpec(memory_space=pl.ANY)
+    vmem = pl.BlockSpec(memory_space=pltpu.VMEM)
+    smem = pl.BlockSpec(memory_space=pltpu.SMEM)
+    big = (back, turned, mid, hid, gp, w_embed, w_down, grads)
     return pl.pallas_call(
         patch_backward_kernel,
-        grid_spec=pltpu.PrefetchScalarGridSpec(
-            num_scalar_prefetch=2,
-            grid=(STEPS4,),
-            in_specs=[
-                pl.BlockSpec(back.shape, lambda i, *_: (0, 0, 0, 0)),
-                pl.BlockSpec((D1, tokens), whole),
-                pl.BlockSpec((tokens, D1), whole),
-                pl.BlockSpec((FB4, tokens), lambda i, *_: (i, 0)),
-                pl.BlockSpec((tokens, FB4), lambda i, *_: (0, i)),
-                pl.BlockSpec((D2, D1), whole),
-                pl.BlockSpec((FB4, D1), lambda i, *_: (i, 0)),
-                grad,
-                pl.BlockSpec((64, D2), whole),
-                pl.BlockSpec((D2, 128), whole),
-                pl.BlockSpec((3, D2), whole),
-                pl.BlockSpec((SLIDES, 3), whole),
-            ],
-            out_specs=[
-                pl.BlockSpec(memory_space=pl.ANY),
-                pl.BlockSpec(memory_space=pl.ANY),
-                pl.BlockSpec((SLIDES, 3), whole),
-                pl.BlockSpec((3, D2), whole),
-            ],
-            scratch_shapes=[
-                pltpu.VMEM((2, HALF_ROWS, 128), BF),
-                pltpu.VMEM((tokens, D1), BF),
-                pltpu.VMEM((tokens, D2), BF),
-                pltpu.VMEM((2, 8, 128), F32),
-                pltpu.SemaphoreType.DMA((14,)),
-            ],
-        ),
+        in_specs=[smem] * 2 + [hbm] * 8 + [vmem] * 4,
+        out_specs=[hbm] * 2 + [vmem] * 2,
         out_shape=[
             jax.ShapeDtypeStruct((HALF_ROWS, 128), BF),
             jax.ShapeDtypeStruct((HALF_ROWS, 128), BF),
             jax.ShapeDtypeStruct((SLIDES, 3), F32),
             jax.ShapeDtypeStruct((3, D2), F32),
         ],
+        scratch_shapes=[pltpu.VMEM(a.shape, a.dtype) for a in big]
+        + [
+            pltpu.VMEM((2, HALF_ROWS, 128), BF),
+            pltpu.VMEM((turned.shape[1], D2), BF),
+            pltpu.VMEM((2, 8, 128), F32),
+            pltpu.SemaphoreType.DMA((8,)),
+            pltpu.SemaphoreType.DMA((6,)),
+        ],
         compiler_params=params(61),
         name="patch_backward",
-    )(
-        idx, slide, back, turned, mid, hid, gp, w_embed, w_down, grads, rows, cols, w_class,
-        g_logits,
-    )
+    )(idx, slide, *big, rows, cols, w_class, g_logits)
 
 
 def unpack_kernel(idx_ref, src_ref, *refs):
     up_ref, down_ref, embed_ref, q_ref, k_ref, v_ref, o_ref, av_ref, au_ref, aw_ref = refs[-10:]
     for l in range(12):
         up_ref[:, pl.ds(128 * l, 128)] = src_ref[pl.ds(192 * l, 192), :].astype(F32)
-    for i in range(2):
-        for l in range(3):
-            rows = src_ref[pl.ds(DOWN_AT + 1152 * i + 384 * l, 384), :]
-            down_ref[pl.ds(384 * i, 384), pl.ds(128 * l, 128)] = rows.astype(F32)
+    for l in range(3):
+        rows = src_ref[pl.ds(DOWN_AT + 768 * l, 768), :]
+        down_ref[:, pl.ds(128 * l, 128)] = rows.astype(F32)
     for slot, ref in enumerate((q_ref, k_ref, v_ref, o_ref, av_ref, au_ref)):
         at = REST_AT + 192 * slot
         ref[:, pl.ds(0, 128)] = src_ref[pl.ds(at, 96), :].astype(F32)

time: 152 us -> 147 us (0.967)
  Pallas kernels: 41.2 us -> 36.2 us
    pallas_call x2, Pallas kernels: 17 us -> 12.5 us  [the longest x1 7.92 us: patch_backward(): pl.pallas_call(patch_backward_kernel, in_specs=[smem] * 2 + [hbm] * 8 + [...]
where the time goes in v5:
time: 147 us; the launch traced here: 146 us
  blocking collectives  48.9 us (33%)
  Pallas kernels  36.2 us (25%)
  starting transfers between devices  34.6 us (24%)
  waiting for transfers between devices  22.2 us (15%)
  other arithmetic  2.07 us (1%)
    all_to_all x2, blocking collectives, exchange(): return lax.all_to_all(x, axes, split_axis=0, concat_axis=0, tiled=True)  48.9 us
    all_to_all x3, starting transfers between devices, exchange(): return lax.all_to_all(x, axes, split_axis=0, concat_axis=0, tiled=True)  22.9 us
    all_to_all x3, waiting for transfers between devices, exchange(): return lax.all_to_all(x, axes, split_axis=0, concat_axis=0, tiled=True)  13.3 us
    pallas_call x1, Pallas kernels, region_backward(): pl.pallas_call(region_backward_kernel, grid_spec=pltpu.PrefetchScalarGrid...  8.17 us
    pallas_call x1, Pallas kernels, patch_backward(): pl.pallas_call(patch_backward_kernel, in_specs=[smem] * 2 + [hbm] * 8 + [...  7.92 us
    ppermute x2, starting transfers between devices, swap_cores(): return lax.ppermute(x, 'c', [(0, 1), (1, 0)])  5.98 us
    pallas_call x1, Pallas kernels, patch_slopes(): pl.pallas_call(patch_slopes_kernel, grid=(STEPS1,), in_specs=[pl.BlockSpe...  5.8 us
    ppermute x3, starting transfers between devices, add_over_zh(): lax.ppermute(x, 'zh', [(i, i ^ k) for i in range(4)])  5.74 us
  transfers between devices with their start and end apart: 8, of which 6 were waited for; matrix products, arithmetic and copies ran while one was open for 0% of the time, Pallas kernels for 11%

profile of v5, /device:TPU:1, one launch (start us, length us, event | category | flops | bytes accessed | tf_op | source)
XLA Modules:
  0.0 146.3 jit_solution(13816549199675163132)
XLA Ops:
  0.6 0.0 copy-start.7
  0.7 0.0 copy-start.8
  0.7 0.0 copy-start.9
  0.7 0.0 copy-start.10
  0.7 4.6 %patch_forward.1 = (bf16[512,192]{1,0:T(8,128)(2,1)}, bf16[512,384]{1,0:T(8,128)(2,1)}) custom-call(bf16[512,384]{1,0:T(8,128)(2,1)} %bitcast.31, bf16[384,1536]{1,0:T(8,128)(2,1)} %wu_ref.3, bf16[1536,384]{1,0:T(8,128)(2,1)} %wd_in.1, bf16[192,384]{1,0:T(8,128)(2,1)} %bitcast.29), custom_call_target="tpu_custom_call" | custom-call | tf_op jit(solution)/shard_map/patch_forward/pallas_call | solution.py:80
  5.3 7.2 %all-to-all-start = ((bf16[16,32,192]{2,1,0:T(8,128)(2,1)}), bf16[16,32,192]{2,1,0:T(8,128)(2,1)S(1)}, u32[]{:S(2)}, u32[]{:S(2)}) async-start(bf16[16,32,192]{2,1,0:T(8,128)(2,1)} %bitcast.34), calls=%async_computation | async-start | bytes 524288 | tf_op jit(solution)/shard_map/all_to_all | solution.py:689
  12.5 0.1 stack.27.idx_ref
  12.6 0.0 copy-done.7
  12.6 0.0 copy-done.9
  12.6 0.0 copy-start.1
  12.6 0.0 copy-start
  12.6 0.0 copy-start.3
  12.7 0.0 copy-start.6
  12.7 0.1 gather_weights.1
  12.7 0.0 copy-start.4
  12.7 0.0 copy-start.5
  12.8 6.9 %all-to-all-done = bf16[16,32,192]{2,1,0:T(8,128)(2,1)S(1)} async-done(((bf16[16,32,192]{2,1,0:T(8,128)(2,1)}), bf16[16,32,192]{2,1,0:T(8,128)(2,1)S(1)}, u32[]{:S(2)}, u32[]{:S(2)}) %all-to-all-start) | async-done | bytes 196640 | tf_op jit(solution)/shard_map/all_to_all | solution.py:689
  19.7 0.0 copy-done
  19.7 0.0 copy-done.6
  19.7 4.3 %region_forward.1 = (bf16[2,1536,256]{2,1,0:T(8,128)(2,1)S(1)}, bf16[2,256,192]{2,1,0:T(8,128)(2,1)S(1)}, f32[8,192]{1,0:T(8,128)S(1)}, f32[8,256]{1,0:T(8,128)S...) custom-call(s32[6]{0:T(128)S(1)} %stack.27.idx_ref, ...), custom_call_target="tpu_custom_call" | custom-call | tf_op jit(solution)/shard_map/region_forward/pallas_call | solution.py:237
  24.0 10.0 %all-to-all-start.1 = ((f32[16,8,128]{2,1,0:T(8,128)}), f32[16,8,128]{2,1,0:T(8,128)S(1)}, u32[]{:S(2)}, u32[]{:S(2)}) async-start(f32[16,8,128]{2,1,0:T(8,128)} %get-tuple-element.59), calls=%async_computation.1 | async-start | bytes 131072 | tf_op jit(solution)/shard_map/all_to_all | solution.py:689
  34.0 8.2 %region_backward.1 = (bf16[16,5,16,256]{3,2,1,0:T(8,128)(2,1)}, f32[2,3,2,192,192]{4,3,2,1,0:T(8,128)}, f32[64,192]{1,0:T(8,128)}, f32[192,128]{1,0:T(8,128)}, f32[8,256]{1,0:T(8,128)S(1)}) custom-call(s32[6]{0:T(128)S(1)} %stack.27.idx_ref, s32[512]{0:T(512)S(1)} %copy-done.3, s32[512,256]{1,0:T(8,128)S(1)} %copy-done, ...), custom_call_target="tpu_custom_call" | custom-call | flops 4000000000 | bytes 20000000 | tf_op jit(solution)/shard_map/region_backward/pallas_call | solution.py:379
  42.2 0.8 all-to-all-done.1.z_ref
  43.0 0.8 join_sums.1
  43.8 5.7 %all-to-all-start.2 = ((bf16[16,80,256]{2,1,0:T(8,128)(2,1)}), bf16[16,80,256]{2,1,0:T(8,128)(2,1)S(1)}, u32[]{:S(2)}, u32[]{:S(2)}) async-start(bf16[16,80,256]{2,1,0:T(8,128)(2,1)} %bitcast.28), calls=%async_computation.2 | async-start | bytes 1310720 | tf_op jit(solution)/shard_map/all_to_all | solution.py:689
  49.5 5.8 %patch_slopes.1 = (bf16[1536,512]{1,0:T(8,128)(2,1)}, bf16[512,1536]{1,0:T(8,128)(2,1)}, bf16[384,512]{1,0:T(8,128)(2,1)}) custom-call(f32[64,192]{1,0:T(8,128)} %get-tuple-element.69.after_ref.rows_ref, bf16[512,384]{1,0:T(8,128)(2,1)} %bitcast.32, bf16[384,1536]{1,0:T(8,128)(2,1)} %wu_ref.3), custom_call_target="tpu_custom_call" | custom-call | flops 3000000000 | bytes 12000000 | tf_op jit(solution)/shard_map/patch_slopes/pallas_call | solution.py:112
  55.3 5.5 %all-to-all-done.2 = bf16[16,80,256]{2,1,0:T(8,128)(2,1)S(1)} async-done(((bf16[16,80,256]{2,1,0:T(8,128)(2,1)}), bf16[16,80,256]{2,1,0:T(8,128)(2,1)S(1)}, u32[]{:S(2)}, u32[]{:S(2)}) %all-to-all-start.2) | async-done | bytes 655392 | tf_op jit(solution)/shard_map/all_to_all | solution.py:689
  60.8 0.9 copy-done.13
  61.7 7.9 %patch_backward.1 = (bf16[6144,128]{1,0:T(8,128)(2,1)}, bf16[6144,128]{1,0:T(8,128)(2,1)}, f32[4,3]{1,0:T(4,128)}, f32[3,192]{1,0:T(4,128)}) custom-call(s32[6]{0:T(128)} %copy-done.1, s32[512]{0:T(512)} %slide_ref.5, bf16[16,5,16,256]{3,2,1,0:T(8,128)(2,1)} %bitcast.27, bf16[384,512]{1,0:T(8,128)(2,1)} %get-tuple-element.70.xt_in, ...), custom_call_target="tpu_custom_call" | custom-call | tf_op jit(solution)/shard_map/patch_backward/pallas_call | solution.py:611
  69.6 1.3 collective-permute-start
  70.9 3.2 %collective-permute-done = bf16[6144,128]{1,0:T(8,128)(2,1)S(1)} collective-permute-done((bf16[6144,128]{1,0:T(8,128)(2,1)}, bf16[6144,128]{1,0:T(8,128)(2,1)S(1)}, u32[]{:S(2)}, u32[]{:S(2)}) %collective-permute-start) | collective-permute-done | bytes 1572896 | tf_op jit(solution)/shard_map/ppermute | solution.py:693
  74.1 1.8 %add_convert_fusion = bf16[6144,128]{1,0:T(8,128)(2,1)S(1)} fusion(bf16[6144,128]{1,0:T(8,128)(2,1)S(1)} %collective-permute-done, bf16[6144,128]{1,0:T(8,128)(2,1)} %get-tuple-element.77), kind=kLoop, calls=%fused_computation | loop fusion | flops 3145728 | bytes 4718592 | tf_op jit(solution)/shard_map/convert_element_type | solution.py:701
  75.9 24.9 %all_to_all.25 = bf16[32,192,128]{2,1,0:T(8,128)(2,1)S(1)} all-to-all(bf16[32,192,128]{2,1,0:T(8,128)(2,1)S(1)} %bitcast.26), channel_id=1, replica_groups=mesh['zl'=2,'x'=4,'c'=2,'zh'=4,'y'=4] {'y','zl','x'}, dimensions={0} | all-to-all | bytes 3145728 | tf_op jit(solution)/shard_map/all_to_all | solution.py:689
  100.8 0.2 reduce_sum.12
  101.0 3.4 %collective-permute-start.3 = (bf16[192,128]{1,0:T(8,128)(2,1)S(1)}, bf16[192,128]{1,0:T(8,128)(2,1)S(1)}, u32[]{:S(2)}, u32[]{:S(2)}) collective-permute-start(bf16[192,128]{1,0:T(8,128)(2,1)S(1)} %reduce_sum.12), channel_id=1, source_target_pairs={{0,12},{4,8},{8,4},{12,0},{1,13},{5,9},{9,5},{13,1},{2,14},{6,10},... | collective-permute-start | bytes 147464 | tf_op jit(solution)/shard_map/ppermute | solution.py:705
  104.4 2.1 %collective-permute-start.2 = (bf16[192,128]{1,0:T(8,128)(2,1)S(1)}, bf16[192,128]{1,0:T(8,128)(2,1)S(1)}, u32[]{:S(2)}, u32[]{:S(2)}) collective-permute-start(bf16[192,128]{1,0:T(8,128)(2,1)S(1)} %reduce_sum.12), channel_id=1, source_target_pairs={{0,8},{4,12},{8,0},{12,4},{1,9},{5,13},{9,1},{13,5},{2,10},{6,14},... | collective-permute-start | bytes 147464 | tf_op jit(solution)/shard_map/ppermute | solution.py:705
  106.5 0.3 collective-permute-start.1
  106.8 0.0 collective-permute-done.3
  106.8 5.0 %collective-permute-done.2 = bf16[192,128]{1,0:T(8,128)(2,1)S(1)} collective-permute-done((bf16[192,128]{1,0:T(8,128)(2,1)S(1)}, bf16[192,128]{1,0:T(8,128)(2,1)S(1)}, u32[]{:S(2)}, u32[]{:S(2)}) %collective-permute-start.2) | collective-permute-done | bytes 49184 | tf_op jit(solution)/shard_map/ppermute | solution.py:705
  111.8 0.0 collective-permute-done.1
  111.8 0.3 broadcast_in_dim.2
  112.2 0.0 copy-start.2
  112.2 24.0 %all_to_all.26 = bf16[32,192,128]{2,1,0:T(8,128)(2,1)S(1)} all-to-all(bf16[32,192,128]{2,1,0:T(8,128)(2,1)S(1)} %broadcast_in_dim.2), channel_id=1, replica_groups=mesh['zl'=2,'x'=4,'c'=2,'zh'=4,'y'=4] {'y','zl','x'}, dimensions={0} | all-to-all | bytes 3145728 | tf_op jit(solution)/shard_map/all_to_all | solution.py:689
  136.2 4.7 %collective-permute-start.4 = (bf16[6144,128]{1,0:T(8,128)(2,1)S(1)}, bf16[6144,128]{1,0:T(8,128)(2,1)S(1)}, u32[]{:S(2)}, u32[]{:S(2)}) collective-permute-start(bf16[6144,128]{1,0:T(8,128)(2,1)S(1)} %bitcast.19), channel_id=1, source_target_pairs={{0,16},{16,0},{1,17},{17,1},{2,18},{18,2},{3,19},{19,3},{4,20},{20... | collective-permute-start | bytes 4718600 | tf_op jit(solution)/shard_map/ppermute | solution.py:693
  140.9 0.0 copy-done.2
  140.9 2.3 %unpack.2 = (f32[384,1536]{1,0:T(8,128)}, f32[1536,384]{1,0:T(8,128)}, f32[192,384]{1,0:T(8,128)}, f32[192,192]{1,0:T(8,128)}, f32[192,192]{1,0:T(8,128)}, /*ind...) custom-call(s32[6]{0:T(128)S(1)} %copy-done.2, ...), custom_call_target="tpu_custom_call" | custom-call | tf_op jit(solution)/shard_map/unpack/pallas_call | solution.py:656
  143.2 0.7 collective-permute-done.4.src_ref
  144.0 2.3 %unpack.3 = (f32[384,1536]{1,0:T(8,128)}, f32[1536,384]{1,0:T(8,128)}, f32[192,384]{1,0:T(8,128)}, f32[192,192]{1,0:T(8,128)}, f32[192,192]{1,0:T(8,128)}, /*ind...) custom-call(s32[6]{0:T(128)S(1)} %copy-done.2, ...), custom_call_target="tpu_custom_call", output_to_operand_aliasing={{0}: (2, {}), {1}: (3, {}), {2}: (4, {}), {3}: (5, {}), {4}... | custom-call | tf_op jit(solution)/shard_map/unpack/pallas_call | solution.py:656
  (12 shorter events, 0.1 us)
Async XLA Ops:
  0.6 11.9 %copy-start.7 = (f32[192,192]{1,0:T(8,128)S(1)}, f32[192,192]{1,0:T(8,128)}, u32[]{:S(2)}) copy-start(f32[192,192]{1,0:T(8,128)} %refs_4_.1) | copy-start | bytes 442372
  0.7 11.9 %copy-start.8 = (f32[192,192]{1,0:T(8,128)S(1)}, f32[192,192]{1,0:T(8,128)}, u32[]{:S(2)}) copy-start(f32[192,192]{1,0:T(8,128)} %refs_5_.1) | copy-start | bytes 442372
  0.7 11.9 %copy-start.9 = (bf16[192,192]{1,0:T(8,128)(2,1)S(1)}, bf16[192,192]{1,0:T(8,128)(2,1)}, u32[]{:S(2)}) copy-start(bf16[192,192]{1,0:T(8,128)(2,1)} %refs_0_.1) | copy-start | bytes 221188
  0.7 11.9 %copy-start.10 = (bf16[192,192]{1,0:T(8,128)(2,1)S(1)}, bf16[192,192]{1,0:T(8,128)(2,1)}, u32[]{:S(2)}) copy-start(bf16[192,192]{1,0:T(8,128)(2,1)} %refs_1_.1) | copy-start | bytes 221188
  0.7 11.9 %copy-start.11 = (bf16[192,192]{1,0:T(8,128)(2,1)S(1)}, bf16[192,192]{1,0:T(8,128)(2,1)}, u32[]{:S(2)}) copy-start(bf16[192,192]{1,0:T(8,128)(2,1)} %refs_2_.1) | copy-start | bytes 221188
  0.7 11.9 %copy-start.12 = (bf16[192,192]{1,0:T(8,128)(2,1)S(1)}, bf16[192,192]{1,0:T(8,128)(2,1)}, u32[]{:S(2)}) copy-start(bf16[192,192]{1,0:T(8,128)(2,1)} %refs_3_.1) | copy-start | bytes 221188
  5.3 14.3 %all-to-all-start = ((bf16[16,32,192]{2,1,0:T(8,128)(2,1)}), bf16[16,32,192]{2,1,0:T(8,128)(2,1)S(1)}, u32[]{:S(2)}, u32[]{:S(2)}) async-start(bf16[16,32,192]{2,1,0:T(8,128)(2,1)} %bitcast.34), calls=%async_computation | async-start | bytes 524288 | tf_op jit(solution)/shard_map/all_to_all | solution.py:689
  12.6 21.4 %copy-start.1 = (s32[6]{0:T(128)}, s32[6]{0:T(128)S(1)}, u32[]{:S(2)}) copy-start(s32[6]{0:T(128)S(1)} %stack.27.idx_ref) | copy-start | bytes 76
  12.6 7.0 %copy-start = (s32[512,256]{1,0:T(8,128)S(1)}, s32[512,256]{1,0:T(8,128)}, u32[]{:S(2)}) copy-start(s32[512,256]{1,0:T(8,128)} %tis_ref.3) | copy-start | bytes 1572868
  12.6 7.0 %copy-start.3 = (s32[512]{0:T(512)S(1)}, s32[512]{0:T(512)}, u32[]{:S(2)}) copy-start(s32[512]{0:T(512)} %slide_ref.5) | copy-start | bytes 6148
  12.7 7.0 %copy-start.6 = (f32[192]{0:T(256)S(1)}, f32[192]{0:T(256)}, u32[]{:S(2)}) copy-start(f32[192]{0:T(256)} %param.27) | copy-start | bytes 2308
  12.7 21.3 %copy-start.4 = (f32[192,3]{0,1:T(4,128)S(1)}, f32[192,3]{0,1:T(4,128)}, u32[]{:S(2)}) copy-start(f32[192,3]{0,1:T(4,128)} %param.28) | copy-start | bytes 6916
  12.7 21.3 %copy-start.5 = (f32[4,3]{1,0:T(4,128)S(1)}, f32[4,3]{1,0:T(4,128)}, u32[]{:S(2)}) copy-start(f32[4,3]{1,0:T(4,128)} %gl_ref.3) | copy-start | bytes 148
  24.0 19.1 %all-to-all-start.1 = ((f32[16,8,128]{2,1,0:T(8,128)}), f32[16,8,128]{2,1,0:T(8,128)S(1)}, u32[]{:S(2)}, u32[]{:S(2)}) async-start(f32[16,8,128]{2,1,0:T(8,128)} %get-tuple-element.59), calls=%async_computation.1 | async-start | bytes 131072 | tf_op jit(solution)/shard_map/all_to_all | solution.py:689
  43.8 17.0 %all-to-all-start.2 = ((bf16[16,80,256]{2,1,0:T(8,128)(2,1)}), bf16[16,80,256]{2,1,0:T(8,128)(2,1)S(1)}, u32[]{:S(2)}, u32[]{:S(2)}) async-start(bf16[16,80,256]{2,1,0:T(8,128)(2,1)} %bitcast.28), calls=%async_computation.2 | async-start | bytes 1310720 | tf_op jit(solution)/shard_map/all_to_all | solution.py:689
  60.8 0.9 copy-start.13
  69.6 4.5 %collective-permute-start = (bf16[6144,128]{1,0:T(8,128)(2,1)}, bf16[6144,128]{1,0:T(8,128)(2,1)S(1)}, u32[]{:S(2)}, u32[]{:S(2)}) collective-permute-start(bf16[6144,128]{1,0:T(8,128)(2,1)} %get-tuple-element.78), channel_id=1, source_target_pairs={{0,16},{16,0},{1,17},{17,1},{2,18},{18,2},{3,19},{19,3},{4,20},{20... | collective-permute-start | bytes 4718600 | tf_op jit(solution)/shard_map/ppermute | solution.py:693
  101.0 5.7 %collective-permute-start.3 = (bf16[192,128]{1,0:T(8,128)(2,1)S(1)}, bf16[192,128]{1,0:T(8,128)(2,1)S(1)}, u32[]{:S(2)}, u32[]{:S(2)}) collective-permute-start(bf16[192,128]{1,0:T(8,128)(2,1)S(1)} %reduce_sum.12), channel_id=1, source_target_pairs={{0,12},{4,8},{8,4},{12,0},{1,13},{5,9},{9,5},{13,1},{2,14},{6,10},... | collective-permute-start | bytes 147464 | tf_op jit(solution)/shard_map/ppermute | solution.py:705
  104.4 7.4 %collective-permute-start.2 = (bf16[192,128]{1,0:T(8,128)(2,1)S(1)}, bf16[192,128]{1,0:T(8,128)(2,1)S(1)}, u32[]{:S(2)}, u32[]{:S(2)}) collective-permute-start(bf16[192,128]{1,0:T(8,128)(2,1)S(1)} %reduce_sum.12), channel_id=1, source_target_pairs={{0,8},{4,12},{8,0},{12,4},{1,9},{5,13},{9,1},{13,5},{2,10},{6,14},... | collective-permute-start | bytes 147464 | tf_op jit(solution)/shard_map/ppermute | solution.py:705
  106.5 5.3 %collective-permute-start.1 = (bf16[192,128]{1,0:T(8,128)(2,1)S(1)}, bf16[192,128]{1,0:T(8,128)(2,1)S(1)}, u32[]{:S(2)}, u32[]{:S(2)}) collective-permute-start(bf16[192,128]{1,0:T(8,128)(2,1)S(1)} %reduce_sum.12), channel_id=1, source_target_pairs={{0,4},{4,0},{8,12},{12,8},{1,5},{5,1},{9,13},{13,9},{2,6},{6,2},{1... | collective-permute-start | bytes 147464 | tf_op jit(solution)/shard_map/ppermute | solution.py:705
  112.2 28.8 %copy-start.2 = (s32[6]{0:T(128)S(1)}, s32[6]{0:T(128)}, u32[]{:S(2)}) copy-start(s32[6]{0:T(128)} %copy-done.1) | copy-start | bytes 76
  136.2 7.8 %collective-permute-start.4 = (bf16[6144,128]{1,0:T(8,128)(2,1)S(1)}, bf16[6144,128]{1,0:T(8,128)(2,1)S(1)}, u32[]{:S(2)}, u32[]{:S(2)}) collective-permute-start(bf16[6144,128]{1,0:T(8,128)(2,1)S(1)} %bitcast.19), channel_id=1, source_target_pairs={{0,16},{16,0},{1,17},{17,1},{2,18},{18,2},{3,19},{19,3},{4,20},{20... | collective-permute-start | bytes 4718600 | tf_op jit(solution)/shard_map/ppermute | solution.py:693

commit v6 on v5

--- a/solution.py
+++ b/solution.py
@@ -165,8 +165,13 @@
     return tis_ref[pl.ds(idx_ref[1] + r, 1), :].astype(F32)
 
 
+def turned_row(row, width):
+    return jnp.broadcast_to(row, (PATCH, row.shape[1])).T[:, :width]
+
+
 def column_of(row, width):
-    return jnp.broadcast_to(row, (PATCH, row.shape[1])).T[:, :width]
+    first = lax.broadcasted_iota(jnp.int32, (16, row.shape[1]), 0) == 0
+    return tn(jnp.where(first, row, 0.0).astype(BF), jnp.ones((16, width), BF))
 
 
 def head_mask(h, shape, dim):
@@ -183,7 +188,7 @@
     asum_ref[...] = jnp.zeros_like(asum_ref)
     for r in range(OWN):
         trow = tissue_row(idx_ref, tis_ref, r)
-        tcol = column_of(trow, D2)
+        tcol = turned_row(trow, D2)
         x = (f_ref[:, r].reshape(PATCH, D2).astype(F32) * tcol).astype(BF)
         q = nn(x, wp_ref[0]).astype(BF)
         k = nn(x, wp_ref[1])
@@ -314,47 +319,61 @@
     scal_ref[...] = jnp.broadcast_to(scalars, (8, PATCH))
 
 
-def pull_back(r, idx_ref, tis_ref, wp_ref, p_ref, x_ref, rows_ref, df_ref, grad_ref, kt_s, dqt_s):
-    trow = tissue_row(idx_ref, tis_ref, r)
-    tcol = column_of(trow, D2)
-    x = x_ref[r]
-    q = nn(x, wp_ref[0]).astype(BF).astype(F32)
-    v = nn(x, wp_ref[2]).astype(BF)
-    kt_s[r] = nn(x, wp_ref[1]).T.astype(BF)
-    spread = jnp.zeros((PATCH, D2), F32)
-    dm = [rows_ref[pl.ds(8 * (2 + j) + r, 1), :] for j in range(2)]
-    da = [rows_ref[pl.ds(8 * (6 + j) + r, 1), :].astype(BF).astype(F32) for j in range(2)]
-    da_col = jnp.concatenate([jnp.broadcast_to(d, (128, D2)) for d in da], axis=0).T
-    dk = [jnp.zeros((PATCH, D2), F32) for _ in range(2)]
+def pull_back(idx_ref, tis_ref, wp_ref, p_ref, x_ref, rows_ref, df_ref, grad_ref, kt_s, dqt_s):
+    regions = range(OWN)
+    pairs = [(r, j) for r in regions for j in range(2)]
+    trow = [tissue_row(idx_ref, tis_ref, r) for r in regions]
+    tcol = [column_of(row, D2) for row in trow]
+    x = [x_ref[r] for r in regions]
+    q = [nn(x[r], wp_ref[0]).astype(BF).astype(F32) for r in regions]
+    v = [nn(x[r], wp_ref[2]).astype(BF) for r in regions]
+    for r in regions:
+        kt_s[r] = lax.dot_general(
+            wp_ref[1], x[r], (((0,), (1,)), ((), ())), preferred_element_type=F32
+        ).astype(BF)
+    dm = {(r, j): rows_ref[pl.ds(8 * (2 + j) + r, 1), :] for r, j in pairs}
+    da = {
+        (r, j): rows_ref[pl.ds(8 * (6 + j) + r, 1), :].astype(BF).astype(F32) for r, j in pairs
+    }
+    row = lax.broadcasted_iota(jnp.int32, (16, D2), 0)
+    head = lax.broadcasted_iota(jnp.int32, (16, D2), 1) // HEAD_DIM
+    e = []
+    for r in regions:
+        by_head = jnp.where(row // 2 == head, jnp.where(row % 2 == 0, da[r, 0], da[r, 1]), 0.0)
+        e.append(nt(by_head.astype(BF), v[r]).T)
+    spread = [jnp.zeros((PATCH, D2), F32) for _ in regions]
+    dk = {pair: jnp.zeros((PATCH, D2), F32) for pair in pairs}
     for h in range(HEADS):
-        e = nn(v, (da_col * head_mask(h, (D2, 1), 0)).astype(BF))
-        pb = p_ref[r, pl.ds(h * PATCH, PATCH), :]
-        pt = pb.astype(F32)
         mask = head_mask(h, (1, D2), 1)
-        spread = spread + nn(pb, (tcol * mask).astype(BF))
-        q_head = (q * mask).astype(BF)
-        k_head = kt_s[r, pl.ds(h * HEAD_DIM, HEAD_DIM), :]
-        for j in range(2):
-            e_j = e[:, 128 * j : 128 * j + 128]
-            pe = pt * jnp.concatenate([e_j, e_j], axis=1)
-            ds = (pe - pt * jnp.sum(pe, axis=0, keepdims=True)).astype(BF)
-            dk[j] = dk[j] + nn(ds, q_head)
-            dqt_s[r, j, pl.ds(h * HEAD_DIM, HEAD_DIM), :] = nn(k_head, ds)
-    xt = x.astype(F32).T.astype(BF)
-    for j in range(2):
-        dq = (dqt_s[r, j] * (trow * SCALE)).T.astype(BF)
-        dk_j = (dk[j] * SCALE).astype(BF)
-        dv = (spread * da[j]).astype(BF)
-        grad_ref[r, 0, j] = nn(xt, dq)
-        grad_ref[r, 1, j] = nn(xt, dk_j)
-        grad_ref[r, 2, j] = nn(xt, dv)
-        d_flat = dm[j] + nt(dq, wp_ref[0]) + nt(dk_j, wp_ref[1]) + nt(dv, wp_ref[2])
-        d_flat = (tcol * d_flat).astype(BF).reshape(GRP, PATCH // GRP, D2)
-        df_ref[:, 2 * r + j, :, pl.ds(0, D2)] = d_flat
-        df_ref[:, 2 * r + j, :, pl.ds(D2, 64)] = jnp.zeros((GRP, PATCH // GRP, 64), BF)
-
-
-BLOCKS = 2 * OWN + 1
+        rows = pl.ds(h * HEAD_DIM, HEAD_DIM)
+        for r in regions:
+            pb = p_ref[r, pl.ds(h * PATCH, PATCH), :]
+            pt = pb.astype(F32)
+            spread[r] = spread[r] + nn(pb, (tcol[r] * mask).astype(BF))
+            q_head = (q[r] * mask).astype(BF)
+            k_head = kt_s[r, rows, :]
+            for j in range(2):
+                pe = pt * e[r][:, 2 * h + j : 2 * h + j + 1]
+                ds = (pe - pt * jnp.sum(pe, axis=0, keepdims=True)).astype(BF)
+                dk[r, j] = dk[r, j] + nn(ds, q_head)
+                dqt_s[r, j, rows, :] = nn(k_head, ds)
+    xt = [x[r].T for r in regions]
+    flat = {}
+    for r, j in pairs:
+        dq = (dqt_s[r, j] * (trow[r] * SCALE)).astype(BF).T
+        dk_j = (dk[r, j] * SCALE).astype(BF)
+        dv = (spread[r] * da[r, j]).astype(BF)
+        grad_ref[r, 0, j] = nn(xt[r], dq)
+        grad_ref[r, 1, j] = nn(xt[r], dk_j)
+        grad_ref[r, 2, j] = nn(xt[r], dv)
+        d_flat = dm[r, j] + nt(dq, wp_ref[0]) + nt(dk_j, wp_ref[1]) + nt(dv, wp_ref[2])
+        flat[r, j] = tcol[r] * d_flat
+    for r in regions:
+        both = jnp.concatenate([flat[r, 0], flat[r, 1]], axis=1).astype(BF)
+        df_ref[:, r] = both.reshape(GRP, PATCH // GRP, 2 * D2)
+
+
+WIDE = 2 * D2 + 128
 
 
 def region_backward_kernel(
@@ -367,10 +386,7 @@
         idx_ref, slide_ref, tis_ref, wp_ref, ap_ref, aw_ref, wc_ref, gl_ref,
         asum_ref, reg_ref, tanh_ref, gate_ref, w_ref, rows_ref, cols_ref, scal_ref,
     )
-    for r in range(OWN):
-        pull_back(
-            r, idx_ref, tis_ref, wp_ref, p_ref, x_ref, rows_ref, df_ref, grad_ref, kt_s, dqt_s
-        )
+    pull_back(idx_ref, tis_ref, wp_ref, p_ref, x_ref, rows_ref, df_ref, grad_ref, kt_s, dqt_s)
 
 
 def region_backward(idx, slide, tissue, wp, ap, att_w, w_class, g_logits, kept):
@@ -390,7 +406,7 @@
                 whole(8, D2), whole(8, PATCH), whole(8, D2), whole(8, D2), whole(8, 128),
             ],
             out_specs=[
-                pl.BlockSpec((GRP, 2 * OWN, PATCH // GRP, PATCH), lambda r, *_: (0, 0, 0, 0)),
+                pl.BlockSpec((GRP, OWN, PATCH // GRP, 2 * D2), lambda r, *_: (0, 0, 0, 0)),
                 pl.BlockSpec((OWN, 3, 2, D2, D2), lambda r, *_: (0, 0, 0, 0, 0)),
                 whole(64, D2),
                 whole(D2, 128),
@@ -402,7 +418,7 @@
             ],
         ),
         out_shape=[
-            pltpu.HBM((GRP, BLOCKS, PATCH // GRP, PATCH), BF),
+            pltpu.HBM((GRP, OWN, PATCH // GRP, WIDE), BF),
             pltpu.HBM((OWN, 3, 2, D2, D2), F32),
             pltpu.HBM((64, D2), F32),
             pltpu.HBM((D2, 128), F32),
@@ -432,8 +448,10 @@
     for i, (part, tops) in enumerate(zip(split_three(z), split_three(scal_ref[0:1]))):
         ext[pl.ds(4 * i, 4), :] = part
         ext[pl.ds(12 + i, 1), :] = tops
-    wide[...] = jnp.broadcast_to(ext[...].astype(BF)[None], wide.shape)
-    copy = pltpu.make_async_copy(wide, out_ref.at[:, BLOCKS - 1], sem)
+    for i in range(OWN):
+        block = ext[:, pl.ds(128 * i, 128)].astype(BF)
+        wide[:, i] = jnp.broadcast_to(block[None], (GRP, 16, 128))
+    copy = pltpu.make_async_copy(wide, out_ref.at[:, :, :, pl.ds(2 * D2, 128)], sem)
     copy.start()
     copy.wait()
 
@@ -447,7 +465,7 @@
         out_shape=pltpu.HBM(df.shape, df.dtype),
         scratch_shapes=[
             pltpu.VMEM((16, PATCH), F32),
-            pltpu.VMEM((GRP, 16, PATCH), BF),
+            pltpu.VMEM((GRP, OWN, 16, 128), BF),
             pltpu.SemaphoreType.DMA,
         ],
         input_output_aliases={2: 0},
@@ -472,7 +490,8 @@
     idx_ref, slide_ref, back_ref, rows_ref, cols_ref, wc_ref, gl_ref, logits_ref, gc_ref,
     df_s, pq_s, pack,
 ):
-    ext = back_ref[:, BLOCKS - 1].astype(F32)
+    ext = [back_ref[:, i, :, pl.ds(2 * D2, 128)].astype(F32) for i in range(OWN)]
+    ext = jnp.concatenate(ext, axis=2)
     sums = jnp.sum(ext, axis=0)
     sums = sums[0:4] + sums[4:8] + sums[8:12]
     total = sums[:, D2 : D2 + 1]
@@ -499,8 +518,9 @@
             w = scalars[:, 128 * i : 128 * i + 1]
             a = scalars[:, 128 * i + 64 : 128 * i + 65]
             p, q = factors(w, a, slide_ref[idx_ref[5] + OWN * src + i])
-            f = [back_ref[src, 2 * i + j].astype(F32)[:, :D2] for j in range(2)]
-            df_s[pl.ds(32 * src + 16 * i, 16), :] = (p * f[0] + q * f[1]).astype(BF)
+            f = back_ref[src, i].astype(F32)
+            rows = p * f[:, :D2] + q * f[:, D2 : 2 * D2]
+            df_s[pl.ds(32 * src + 16 * i, 16), :] = rows.astype(BF)
 
     kept = [rows_ref[pl.ds(8 * i, 8), :] for i in range(6)]
     pre_v, pre_u, dm0, dm1, w_own, a_own = kept
@@ -537,9 +557,8 @@
         (back_in, back_ref), (we_in, we_ref), (wd_in, wd_ref), (gp_in, gp_ref), (xt_in, xt_ref),
         (hid_in, hid_ref), (mid_in, mid_ref), (grad_in, grad_ref),
     )
-    fetch = begin(
-        [pltpu.make_async_copy(a, b, in_sems.at[i]) for i, (a, b) in enumerate(pairs)]
-    )
+    fetch = [pltpu.make_async_copy(a, b, in_sems.at[i]) for i, (a, b) in enumerate(pairs)]
+    begin(fetch)
     sent = []
 
     def send(low, size):
@@ -734,7 +753,7 @@
     )
     df = join_sums(z, scalars, df)
     hid, gp, turned = patch_slopes(rows, tokens, w_up)
-    back = exchange(df.reshape(GRP, -1, PATCH), GRP_AXES).reshape(df.shape)
+    back = exchange(df.reshape(GRP, -1, WIDE), GRP_AXES).reshape(df.shape)
     mine, other, logits, g_class = patch_backward(
         idx, region_slide, back, turned, mid, hid, gp, w_embed.T, w_down, grads, rows,
         cols, class_rows, g_logits,

time: 147 us -> 145 us (0.986)
  waiting for transfers between devices: 22.2 us -> 20.4 us
where the time goes in v6:
time: 145 us; the launch traced here: 144 us
  blocking collectives  49.7 us (34%)
  Pallas kernels  35.5 us (24%)
  starting transfers between devices  34.3 us (24%)
  waiting for transfers between devices  20.4 us (14%)
  other arithmetic  2.07 us (1%)
    all_to_all x2, blocking collectives, exchange(): return lax.all_to_all(x, axes, split_axis=0, concat_axis=0, tiled=True)  49.7 us
    all_to_all x3, starting transfers between devices, exchange(): return lax.all_to_all(x, axes, split_axis=0, concat_axis=0, tiled=True)  22.9 us
    all_to_all x3, waiting for transfers between devices, exchange(): return lax.all_to_all(x, axes, split_axis=0, concat_axis=0, tiled=True)  12.6 us
    pallas_call x1, Pallas kernels, patch_backward(): pl.pallas_call(patch_backward_kernel, in_specs=[smem] * 2 + [hbm] * 8 + [...  8.01 us
    pallas_call x1, Pallas kernels, region_backward(): pl.pallas_call(region_backward_kernel, grid_spec=pltpu.PrefetchScalarGrid...  7.36 us
    pallas_call x1, Pallas kernels, patch_slopes(): pl.pallas_call(patch_slopes_kernel, grid=(STEPS1,), in_specs=[pl.BlockSpe...  5.8 us
    ppermute x3, starting transfers between devices, add_over_zh(): lax.ppermute(x, 'zh', [(i, i ^ k) for i in range(4)])  5.74 us
    ppermute x2, starting transfers between devices, swap_cores(): return lax.ppermute(x, 'c', [(0, 1), (1, 0)])  5.65 us
  transfers between devices with their start and end apart: 8, of which 6 were waited for; matrix products, arithmetic and copies ran while one was open for 0% of the time, Pallas kernels for 11%

profile of v6, /device:TPU:1, one launch (start us, length us, event | category | flops | bytes accessed | tf_op | source)
XLA Modules:
  0.0 144.2 jit_solution(2801268723369526021)
XLA Ops:
  0.6 0.0 copy-start.7
  0.7 0.0 copy-start.8
  0.7 0.0 copy-start.9
  0.7 0.0 copy-start.10
  0.7 0.0 copy-start.11
  0.7 0.0 copy-start.12
  0.7 4.6 %patch_forward.1 = (bf16[512,192]{1,0:T(8,128)(2,1)}, bf16[512,384]{1,0:T(8,128)(2,1)}) custom-call(bf16[512,384]{1,0:T(8,128)(2,1)} %bitcast.31, bf16[384,1536]{1,0:T(8,128)(2,1)} %wu_ref.3, bf16[1536,384]{1,0:T(8,128)(2,1)} %wd_in.1, bf16[192,384]{1,0:T(8,128)(2,1)} %bitcast.29), custom_call_target="tpu_custom_call" | custom-call | tf_op jit(solution)/shard_map/patch_forward/pallas_call | solution.py:80
  5.3 7.2 %all-to-all-start = ((bf16[16,32,192]{2,1,0:T(8,128)(2,1)}), bf16[16,32,192]{2,1,0:T(8,128)(2,1)S(1)}, u32[]{:S(2)}, u32[]{:S(2)}) async-start(bf16[16,32,192]{2,1,0:T(8,128)(2,1)} %bitcast.34), calls=%async_computation | async-start | bytes 524288 | tf_op jit(solution)/shard_map/all_to_all | solution.py:708
  12.5 0.1 stack.27.idx_ref
  12.6 0.0 copy-done.9
  12.6 0.0 copy-start.1
  12.6 0.0 copy-start
  12.6 0.0 copy-start.3
  12.7 0.0 copy-start.6
  12.7 0.1 gather_weights.1
  12.7 0.0 copy-start.4
  12.7 0.0 copy-start.5
  12.8 6.9 %all-to-all-done = bf16[16,32,192]{2,1,0:T(8,128)(2,1)S(1)} async-done(((bf16[16,32,192]{2,1,0:T(8,128)(2,1)}), bf16[16,32,192]{2,1,0:T(8,128)(2,1)S(1)}, u32[]{:S(2)}, u32[]{:S(2)}) %all-to-all-start) | async-done | bytes 196640 | tf_op jit(solution)/shard_map/all_to_all | solution.py:708
  19.7 0.0 copy-done
  19.7 0.0 copy-done.6
  19.7 4.3 %region_forward.1 = (bf16[2,1536,256]{2,1,0:T(8,128)(2,1)S(1)}, bf16[2,256,192]{2,1,0:T(8,128)(2,1)S(1)}, f32[8,192]{1,0:T(8,128)S(1)}, f32[8,256]{1,0:T(8,128)S...) custom-call(s32[6]{0:T(128)S(1)} %stack.27.idx_ref, ...), custom_call_target="tpu_custom_call" | custom-call | tf_op jit(solution)/shard_map/region_forward/pallas_call | solution.py:242
  24.0 10.0 %all-to-all-start.1 = ((f32[16,8,128]{2,1,0:T(8,128)}), f32[16,8,128]{2,1,0:T(8,128)S(1)}, u32[]{:S(2)}, u32[]{:S(2)}) async-start(f32[16,8,128]{2,1,0:T(8,128)} %get-tuple-element.59), calls=%async_computation.1 | async-start | bytes 131072 | tf_op jit(solution)/shard_map/all_to_all | solution.py:708
  34.0 7.4 %region_backward.1 = (bf16[16,2,16,512]{3,2,1,0:T(8,128)(2,1)}, f32[2,3,2,192,192]{4,3,2,1,0:T(8,128)}, f32[64,192]{1,0:T(8,128)}, f32[192,128]{1,0:T(8,128)}, f32[8,256]{1,0:T(8,128)S(1)}) custom-call(s32[6]{0:T(128)S(1)} %stack.27.idx_ref, s32[512]{0:T(512)S(1)} %copy-done.3, s32[512,256]{1,0:T(8,128)S(1)} %copy-done, ...), custom_call_target="tpu_custom_call" | custom-call | flops 4000000000 | bytes 20000000 | tf_op jit(solution)/shard_map/region_backward/pallas_call | solution.py:395
  41.4 1.6 %all-to-all-done.1.z_ref = f32[16,8,128]{2,1,0:T(8,128)S(1)} async-done(((f32[16,8,128]{2,1,0:T(8,128)}), f32[16,8,128]{2,1,0:T(8,128)S(1)}, u32[]{:S(2)}, u32[]{:S(2)}) %all-to-all-start.1) | async-done | bytes 65568 | tf_op jit(solution)/shard_map/all_to_all | solution.py:708
  43.0 0.7 join_sums.1
  43.8 5.7 %all-to-all-start.2 = ((bf16[16,32,512]{2,1,0:T(8,128)(2,1)}), bf16[16,32,512]{2,1,0:T(8,128)(2,1)S(1)}, u32[]{:S(2)}, u32[]{:S(2)}) async-start(bf16[16,32,512]{2,1,0:T(8,128)(2,1)} %bitcast.28), calls=%async_computation.2 | async-start | bytes 1048576 | tf_op jit(solution)/shard_map/all_to_all | solution.py:708
  49.5 5.8 %patch_slopes.1 = (bf16[1536,512]{1,0:T(8,128)(2,1)}, bf16[512,1536]{1,0:T(8,128)(2,1)}, bf16[384,512]{1,0:T(8,128)(2,1)}) custom-call(f32[64,192]{1,0:T(8,128)} %get-tuple-element.69.after_ref.rows_ref, bf16[512,384]{1,0:T(8,128)(2,1)} %bitcast.32, bf16[384,1536]{1,0:T(8,128)(2,1)} %wu_ref.3), custom_call_target="tpu_custom_call" | custom-call | flops 3000000000 | bytes 12000000 | tf_op jit(solution)/shard_map/patch_slopes/pallas_call | solution.py:112
  55.3 4.1 %all-to-all-done.2 = bf16[16,32,512]{2,1,0:T(8,128)(2,1)S(1)} async-done(((bf16[16,32,512]{2,1,0:T(8,128)(2,1)}), bf16[16,32,512]{2,1,0:T(8,128)(2,1)S(1)}, u32[]{:S(2)}, u32[]{:S(2)}) %all-to-all-start.2) | async-done | bytes 524320 | tf_op jit(solution)/shard_map/all_to_all | solution.py:708
  59.3 0.8 copy-done.13
  60.2 8.0 %patch_backward.1 = (bf16[6144,128]{1,0:T(8,128)(2,1)}, bf16[6144,128]{1,0:T(8,128)(2,1)}, f32[4,3]{1,0:T(4,128)}, f32[3,192]{1,0:T(4,128)}) custom-call(s32[6]{0:T(128)} %copy-done.1, s32[512]{0:T(512)} %slide_ref.5, bf16[16,2,16,512]{3,2,1,0:T(8,128)(2,1)} %bitcast.27, bf16[384,512]{1,0:T(8,128)(2,1)} %get-tuple-element.70.xt_in, ...), custom_call_target="tpu_custom_call" | custom-call | tf_op jit(solution)/shard_map/patch_backward/pallas_call | solution.py:630
  68.2 1.2 collective-permute-start
  69.4 3.2 %collective-permute-done = bf16[6144,128]{1,0:T(8,128)(2,1)S(1)} collective-permute-done((bf16[6144,128]{1,0:T(8,128)(2,1)}, bf16[6144,128]{1,0:T(8,128)(2,1)S(1)}, u32[]{:S(2)}, u32[]{:S(2)}) %collective-permute-start) | collective-permute-done | bytes 1572896 | tf_op jit(solution)/shard_map/ppermute | solution.py:712
  72.7 1.8 %add_convert_fusion = bf16[6144,128]{1,0:T(8,128)(2,1)S(1)} fusion(bf16[6144,128]{1,0:T(8,128)(2,1)S(1)} %collective-permute-done, bf16[6144,128]{1,0:T(8,128)(2,1)} %get-tuple-element.77), kind=kLoop, calls=%fused_computation | loop fusion | flops 3145728 | bytes 4718592 | tf_op jit(solution)/shard_map/convert_element_type | solution.py:720
  74.5 24.8 %all_to_all.25 = bf16[32,192,128]{2,1,0:T(8,128)(2,1)S(1)} all-to-all(bf16[32,192,128]{2,1,0:T(8,128)(2,1)S(1)} %bitcast.26), channel_id=1, replica_groups=mesh['zl'=2,'x'=4,'c'=2,'zh'=4,'y'=4] {'y','zl','x'}, dimensions={0} | all-to-all | bytes 3145728 | tf_op jit(solution)/shard_map/all_to_all | solution.py:708
  99.3 0.2 reduce_sum.12
  99.5 2.6 %collective-permute-start.3 = (bf16[192,128]{1,0:T(8,128)(2,1)S(1)}, bf16[192,128]{1,0:T(8,128)(2,1)S(1)}, u32[]{:S(2)}, u32[]{:S(2)}) collective-permute-start(bf16[192,128]{1,0:T(8,128)(2,1)S(1)} %reduce_sum.12), channel_id=1, source_target_pairs={{0,12},{4,8},{8,4},{12,0},{1,13},{5,9},{9,5},{13,1},{2,14},{6,10},... | collective-permute-start | bytes 147464 | tf_op jit(solution)/shard_map/ppermute | solution.py:724
  102.2 2.1 %collective-permute-start.2 = (bf16[192,128]{1,0:T(8,128)(2,1)S(1)}, bf16[192,128]{1,0:T(8,128)(2,1)S(1)}, u32[]{:S(2)}, u32[]{:S(2)}) collective-permute-start(bf16[192,128]{1,0:T(8,128)(2,1)S(1)} %reduce_sum.12), channel_id=1, source_target_pairs={{0,8},{4,12},{8,0},{12,4},{1,9},{5,13},{9,1},{13,5},{2,10},{6,14},... | collective-permute-start | bytes 147464 | tf_op jit(solution)/shard_map/ppermute | solution.py:724
  104.3 1.0 collective-permute-start.1
  105.3 0.0 collective-permute-done.3
  105.3 3.8 %collective-permute-done.2 = bf16[192,128]{1,0:T(8,128)(2,1)S(1)} collective-permute-done((bf16[192,128]{1,0:T(8,128)(2,1)S(1)}, bf16[192,128]{1,0:T(8,128)(2,1)S(1)}, u32[]{:S(2)}, u32[]{:S(2)}) %collective-permute-start.2) | collective-permute-done | bytes 49184 | tf_op jit(solution)/shard_map/ppermute | solution.py:724
  109.1 0.0 collective-permute-done.1
  109.1 0.3 broadcast_in_dim.2
  109.5 0.0 copy-start.2
  109.5 24.9 %all_to_all.26 = bf16[32,192,128]{2,1,0:T(8,128)(2,1)S(1)} all-to-all(bf16[32,192,128]{2,1,0:T(8,128)(2,1)S(1)} %broadcast_in_dim.2), channel_id=1, replica_groups=mesh['zl'=2,'x'=4,'c'=2,'zh'=4,'y'=4] {'y','zl','x'}, dimensions={0} | all-to-all | bytes 3145728 | tf_op jit(solution)/shard_map/all_to_all | solution.py:708
  134.4 4.4 %collective-permute-start.4 = (bf16[6144,128]{1,0:T(8,128)(2,1)S(1)}, bf16[6144,128]{1,0:T(8,128)(2,1)S(1)}, u32[]{:S(2)}, u32[]{:S(2)}) collective-permute-start(bf16[6144,128]{1,0:T(8,128)(2,1)S(1)} %bitcast.19), channel_id=1, source_target_pairs={{0,16},{16,0},{1,17},{17,1},{2,18},{18,2},{3,19},{19,3},{4,20},{20... | collective-permute-start | bytes 4718600 | tf_op jit(solution)/shard_map/ppermute | solution.py:712
  138.8 2.3 %unpack.2 = (f32[384,1536]{1,0:T(8,128)}, f32[1536,384]{1,0:T(8,128)}, f32[192,384]{1,0:T(8,128)}, f32[192,192]{1,0:T(8,128)}, f32[192,192]{1,0:T(8,128)}, /*ind...) custom-call(s32[6]{0:T(128)S(1)} %copy-done.2, ...), custom_call_target="tpu_custom_call" | custom-call | tf_op jit(solution)/shard_map/unpack/pallas_call | solution.py:675
  141.1 0.7 collective-permute-done.4.src_ref
  141.8 2.3 %unpack.3 = (f32[384,1536]{1,0:T(8,128)}, f32[1536,384]{1,0:T(8,128)}, f32[192,384]{1,0:T(8,128)}, f32[192,192]{1,0:T(8,128)}, f32[192,192]{1,0:T(8,128)}, /*ind...) custom-call(s32[6]{0:T(128)S(1)} %copy-done.2, ...), custom_call_target="tpu_custom_call", output_to_operand_aliasing={{0}: (2, {}), {1}: (3, {}), {2}: (4, {}), {3}: (5, {}), {4}... | custom-call | tf_op jit(solution)/shard_map/unpack/pallas_call | solution.py:675
  (12 shorter events, 0.1 us)
Async XLA Ops:
  0.6 11.9 %copy-start.7 = (f32[192,192]{1,0:T(8,128)S(1)}, f32[192,192]{1,0:T(8,128)}, u32[]{:S(2)}) copy-start(f32[192,192]{1,0:T(8,128)} %refs_4_.1) | copy-start | bytes 442372
  0.7 11.9 %copy-start.8 = (f32[192,192]{1,0:T(8,128)S(1)}, f32[192,192]{1,0:T(8,128)}, u32[]{:S(2)}) copy-start(f32[192,192]{1,0:T(8,128)} %refs_5_.1) | copy-start | bytes 442372
  0.7 11.9 %copy-start.9 = (bf16[192,192]{1,0:T(8,128)(2,1)S(1)}, bf16[192,192]{1,0:T(8,128)(2,1)}, u32[]{:S(2)}) copy-start(bf16[192,192]{1,0:T(8,128)(2,1)} %refs_0_.1) | copy-start | bytes 221188
  0.7 11.9 %copy-start.10 = (bf16[192,192]{1,0:T(8,128)(2,1)S(1)}, bf16[192,192]{1,0:T(8,128)(2,1)}, u32[]{:S(2)}) copy-start(bf16[192,192]{1,0:T(8,128)(2,1)} %refs_1_.1) | copy-start | bytes 221188
  0.7 11.9 %copy-start.11 = (bf16[192,192]{1,0:T(8,128)(2,1)S(1)}, bf16[192,192]{1,0:T(8,128)(2,1)}, u32[]{:S(2)}) copy-start(bf16[192,192]{1,0:T(8,128)(2,1)} %refs_2_.1) | copy-start | bytes 221188
  0.7 11.9 %copy-start.12 = (bf16[192,192]{1,0:T(8,128)(2,1)S(1)}, bf16[192,192]{1,0:T(8,128)(2,1)}, u32[]{:S(2)}) copy-start(bf16[192,192]{1,0:T(8,128)(2,1)} %refs_3_.1) | copy-start | bytes 221188
  5.3 14.3 %all-to-all-start = ((bf16[16,32,192]{2,1,0:T(8,128)(2,1)}), bf16[16,32,192]{2,1,0:T(8,128)(2,1)S(1)}, u32[]{:S(2)}, u32[]{:S(2)}) async-start(bf16[16,32,192]{2,1,0:T(8,128)(2,1)} %bitcast.34), calls=%async_computation | async-start | bytes 524288 | tf_op jit(solution)/shard_map/all_to_all | solution.py:708
  12.6 21.4 %copy-start.1 = (s32[6]{0:T(128)}, s32[6]{0:T(128)S(1)}, u32[]{:S(2)}) copy-start(s32[6]{0:T(128)S(1)} %stack.27.idx_ref) | copy-start | bytes 76
  12.6 7.0 %copy-start = (s32[512,256]{1,0:T(8,128)S(1)}, s32[512,256]{1,0:T(8,128)}, u32[]{:S(2)}) copy-start(s32[512,256]{1,0:T(8,128)} %tis_ref.3) | copy-start | bytes 1572868
  12.6 7.0 %copy-start.3 = (s32[512]{0:T(512)S(1)}, s32[512]{0:T(512)}, u32[]{:S(2)}) copy-start(s32[512]{0:T(512)} %slide_ref.5) | copy-start | bytes 6148
  12.7 7.0 %copy-start.6 = (f32[192]{0:T(256)S(1)}, f32[192]{0:T(256)}, u32[]{:S(2)}) copy-start(f32[192]{0:T(256)} %param.27) | copy-start | bytes 2308
  12.7 21.3 %copy-start.4 = (f32[192,3]{0,1:T(4,128)S(1)}, f32[192,3]{0,1:T(4,128)}, u32[]{:S(2)}) copy-start(f32[192,3]{0,1:T(4,128)} %param.28) | copy-start | bytes 6916
  12.7 21.3 %copy-start.5 = (f32[4,3]{1,0:T(4,128)S(1)}, f32[4,3]{1,0:T(4,128)}, u32[]{:S(2)}) copy-start(f32[4,3]{1,0:T(4,128)} %gl_ref.3) | copy-start | bytes 148
  24.0 19.1 %all-to-all-start.1 = ((f32[16,8,128]{2,1,0:T(8,128)}), f32[16,8,128]{2,1,0:T(8,128)S(1)}, u32[]{:S(2)}, u32[]{:S(2)}) async-start(f32[16,8,128]{2,1,0:T(8,128)} %get-tuple-element.59), calls=%async_computation.1 | async-start | bytes 131072 | tf_op jit(solution)/shard_map/all_to_all | solution.py:708
  43.8 15.6 %all-to-all-start.2 = ((bf16[16,32,512]{2,1,0:T(8,128)(2,1)}), bf16[16,32,512]{2,1,0:T(8,128)(2,1)S(1)}, u32[]{:S(2)}, u32[]{:S(2)}) async-start(bf16[16,32,512]{2,1,0:T(8,128)(2,1)} %bitcast.28), calls=%async_computation.2 | async-start | bytes 1048576 | tf_op jit(solution)/shard_map/all_to_all | solution.py:708
  59.3 0.8 copy-start.13
  68.2 4.5 %collective-permute-start = (bf16[6144,128]{1,0:T(8,128)(2,1)}, bf16[6144,128]{1,0:T(8,128)(2,1)S(1)}, u32[]{:S(2)}, u32[]{:S(2)}) collective-permute-start(bf16[6144,128]{1,0:T(8,128)(2,1)} %get-tuple-element.78), channel_id=1, source_target_pairs={{0,16},{16,0},{1,17},{17,1},{2,18},{18,2},{3,19},{19,3},{4,20},{20... | collective-permute-start | bytes 4718600 | tf_op jit(solution)/shard_map/ppermute | solution.py:712
  99.5 5.7 %collective-permute-start.3 = (bf16[192,128]{1,0:T(8,128)(2,1)S(1)}, bf16[192,128]{1,0:T(8,128)(2,1)S(1)}, u32[]{:S(2)}, u32[]{:S(2)}) collective-permute-start(bf16[192,128]{1,0:T(8,128)(2,1)S(1)} %reduce_sum.12), channel_id=1, source_target_pairs={{0,12},{4,8},{8,4},{12,0},{1,13},{5,9},{9,5},{13,1},{2,14},{6,10},... | collective-permute-start | bytes 147464 | tf_op jit(solution)/shard_map/ppermute | solution.py:724
  102.2 6.9 %collective-permute-start.2 = (bf16[192,128]{1,0:T(8,128)(2,1)S(1)}, bf16[192,128]{1,0:T(8,128)(2,1)S(1)}, u32[]{:S(2)}, u32[]{:S(2)}) collective-permute-start(bf16[192,128]{1,0:T(8,128)(2,1)S(1)} %reduce_sum.12), channel_id=1, source_target_pairs={{0,8},{4,12},{8,0},{12,4},{1,9},{5,13},{9,1},{13,5},{2,10},{6,14},... | collective-permute-start | bytes 147464 | tf_op jit(solution)/shard_map/ppermute | solution.py:724
  104.3 4.8 %collective-permute-start.1 = (bf16[192,128]{1,0:T(8,128)(2,1)S(1)}, bf16[192,128]{1,0:T(8,128)(2,1)S(1)}, u32[]{:S(2)}, u32[]{:S(2)}) collective-permute-start(bf16[192,128]{1,0:T(8,128)(2,1)S(1)} %reduce_sum.12), channel_id=1, source_target_pairs={{0,4},{4,0},{8,12},{12,8},{1,5},{5,1},{9,13},{13,9},{2,6},{6,2},{1... | collective-permute-start | bytes 147464 | tf_op jit(solution)/shard_map/ppermute | solution.py:724
  109.5 29.3 %copy-start.2 = (s32[6]{0:T(128)S(1)}, s32[6]{0:T(128)}, u32[]{:S(2)}) copy-start(s32[6]{0:T(128)} %copy-done.1) | copy-start | bytes 76
  134.4 7.4 %collective-permute-start.4 = (bf16[6144,128]{1,0:T(8,128)(2,1)S(1)}, bf16[6144,128]{1,0:T(8,128)(2,1)S(1)}, u32[]{:S(2)}, u32[]{:S(2)}) collective-permute-start(bf16[6144,128]{1,0:T(8,128)(2,1)S(1)} %bitcast.19), channel_id=1, source_target_pairs={{0,16},{16,0},{1,17},{17,1},{2,18},{18,2},{3,19},{19,3},{4,20},{20... | collective-permute-start | bytes 4718600 | tf_op jit(solution)/shard_map/ppermute | solution.py:712

commit v7 on v6

--- a/solution.py
+++ b/solution.py
@@ -650,6 +650,25 @@
     )(idx, slide, *big, rows, cols, w_class, g_logits)
 
 
+def bring_in_kernel(src_ref, out_ref, sem):
+    copy = pltpu.make_async_copy(src_ref, out_ref, sem)
+    copy.start()
+    copy.wait()
+
+
+def bring_in(x):
+    return pl.pallas_call(
+        bring_in_kernel,
+        in_specs=[pl.BlockSpec(memory_space=pl.ANY)],
+        out_specs=pl.BlockSpec(memory_space=pltpu.VMEM),
+        out_shape=jax.ShapeDtypeStruct(x.shape, x.dtype),
+        scratch_shapes=[pltpu.SemaphoreType.DMA],
+        compiler_params=params(16),
+        cost_estimate=pl.CostEstimate(flops=0, bytes_accessed=6_000_000, transcendentals=0),
+        name="bring_in",
+    )(x)
+
+
 def unpack_kernel(idx_ref, src_ref, *refs):
     up_ref, down_ref, embed_ref, q_ref, k_ref, v_ref, o_ref, av_ref, au_ref, aw_ref = refs[-10:]
     for l in range(12):
@@ -758,7 +777,7 @@
         idx, region_slide, back, turned, mid, hid, gp, w_embed.T, w_down, grads, rows,
         cols, class_rows, g_logits,
     )
-    half = add_pair(mine, swap_cores(other))
+    half = add_pair(bring_in(mine), swap_cores(other))
     chunk = add_up(exchange(half.reshape(PEERS, -1, 128), ZLXY))
     chunk = add_over_zh(chunk)
     half = exchange(spread(chunk, PEERS), ZLXY).reshape(HALF_ROWS, 128)

time: 145 us -> 143 us (0.986)
  waiting for transfers between devices: 20.4 us -> 18.9 us
    ppermute x2, waiting for transfers between devices: 3.98 us -> 2.45 us  [swap_cores(): return lax.ppermute(x, 'c', [(0, 1), (1, 0)])]
where the time goes in v7:
time: 143 us
  blocking collectives  49.7 us (35%)
  Pallas kernels  35.6 us (25%)
  starting transfers between devices  34.3 us (24%)
  waiting for transfers between devices  18.9 us (13%)
  local copies, waits for them, and re-layouts  2.71 us (2%)
    all_to_all x2, blocking collectives, exchange(): return lax.all_to_all(x, axes, split_axis=0, concat_axis=0, tiled=True)  49.7 us
    all_to_all x3, starting transfers between devices, exchange(): return lax.all_to_all(x, axes, split_axis=0, concat_axis=0, tiled=True)  22.9 us
    all_to_all x3, waiting for transfers between devices, exchange(): return lax.all_to_all(x, axes, split_axis=0, concat_axis=0, tiled=True)  12.6 us
    pallas_call x1, Pallas kernels, patch_backward(): pl.pallas_call(patch_backward_kernel, in_specs=[smem] * 2 + [hbm] * 8 + [...  8.01 us
    pallas_call x1, Pallas kernels, region_backward(): pl.pallas_call(region_backward_kernel, grid_spec=pltpu.PrefetchScalarGrid...  7.36 us
    pallas_call x1, Pallas kernels, patch_slopes(): pl.pallas_call(patch_slopes_kernel, grid=(STEPS1,), in_specs=[pl.BlockSpe...  5.8 us
    ppermute x3, starting transfers between devices, add_over_zh(): lax.ppermute(x, 'zh', [(i, i ^ k) for i in range(4)])  5.74 us
    ppermute x2, starting transfers between devices, swap_cores(): return lax.ppermute(x, 'c', [(0, 1), (1, 0)])  5.66 us
  transfers between devices with their start and end apart: 8, of which 6 were waited for; matrix products, arithmetic and copies ran while one was open for 0% of the time, Pallas kernels for 11%

profile of v7, /device:TPU:1, one launch (start us, length us, event | category | flops | bytes accessed | tf_op | source)
XLA Modules:
  0.0 142.7 jit_solution(16875442433850195267)
XLA Ops:
  0.6 0.0 copy-start.8
  0.7 0.0 copy-start.9
  0.7 0.0 copy-start.10
  0.7 0.0 copy-start.11
  0.7 0.0 copy-start.12
  0.7 4.6 %patch_forward.1 = (bf16[512,192]{1,0:T(8,128)(2,1)}, bf16[512,384]{1,0:T(8,128)(2,1)}) custom-call(bf16[512,384]{1,0:T(8,128)(2,1)} %bitcast.31, bf16[384,1536]{1,0:T(8,128)(2,1)} %wu_ref.3, bf16[1536,384]{1,0:T(8,128)(2,1)} %wd_in.1, bf16[192,384]{1,0:T(8,128)(2,1)} %bitcast.29), custom_call_target="tpu_custom_call" | custom-call | tf_op jit(solution)/shard_map/patch_forward/pallas_call | solution.py:80
  5.3 7.2 %all-to-all-start = ((bf16[16,32,192]{2,1,0:T(8,128)(2,1)}), bf16[16,32,192]{2,1,0:T(8,128)(2,1)S(1)}, u32[]{:S(2)}, u32[]{:S(2)}) async-start(bf16[16,32,192]{2,1,0:T(8,128)(2,1)} %bitcast.34), calls=%async_computation | async-start | bytes 524288 | tf_op jit(solution)/shard_map/all_to_all | solution.py:727
  12.5 0.1 stack.27.idx_ref
  12.6 0.0 copy-done.10
  12.6 0.0 copy-start.2
  12.6 0.0 copy-start.1
  12.6 0.0 copy-start.4
  12.7 0.0 copy-start.7
  12.7 0.1 gather_weights.1
  12.7 0.0 copy-start.5
  12.7 0.0 copy-start.6
  12.8 6.9 %all-to-all-done = bf16[16,32,192]{2,1,0:T(8,128)(2,1)S(1)} async-done(((bf16[16,32,192]{2,1,0:T(8,128)(2,1)}), bf16[16,32,192]{2,1,0:T(8,128)(2,1)S(1)}, u32[]{:S(2)}, u32[]{:S(2)}) %all-to-all-start) | async-done | bytes 196640 | tf_op jit(solution)/shard_map/all_to_all | solution.py:727
  19.7 0.0 copy-done.7
  19.7 4.3 %region_forward.1 = (bf16[2,1536,256]{2,1,0:T(8,128)(2,1)S(1)}, bf16[2,256,192]{2,1,0:T(8,128)(2,1)S(1)}, f32[8,192]{1,0:T(8,128)S(1)}, f32[8,256]{1,0:T(8,128)S...) custom-call(s32[6]{0:T(128)S(1)} %stack.27.idx_ref, ...), custom_call_target="tpu_custom_call" | custom-call | tf_op jit(solution)/shard_map/region_forward/pallas_call | solution.py:242
  24.0 10.0 %all-to-all-start.1 = ((f32[16,8,128]{2,1,0:T(8,128)}), f32[16,8,128]{2,1,0:T(8,128)S(1)}, u32[]{:S(2)}, u32[]{:S(2)}) async-start(f32[16,8,128]{2,1,0:T(8,128)} %get-tuple-element.59), calls=%async_computation.1 | async-start | bytes 131072 | tf_op jit(solution)/shard_map/all_to_all | solution.py:727
  34.0 7.4 %region_backward.1 = (bf16[16,2,16,512]{3,2,1,0:T(8,128)(2,1)}, f32[2,3,2,192,192]{4,3,2,1,0:T(8,128)}, f32[64,192]{1,0:T(8,128)}, f32[192,128]{1,0:T(8,128)}, f32[8,256]{1,0:T(8,128)S(1)}) custom-call(s32[6]{0:T(128)S(1)} %stack.27.idx_ref, s32[512]{0:T(512)S(1)} %copy-done.4, s32[512,256]{1,0:T(8,128)S(1)} %copy-done.1, ...), custom_call_target="tpu_custom_call" | custom-call | flops 4000000000 | bytes 20000000 | tf_op jit(solution)/shard_map/region_backward/pallas_call | solution.py:395
  41.4 1.6 %all-to-all-done.1.z_ref = f32[16,8,128]{2,1,0:T(8,128)S(1)} async-done(((f32[16,8,128]{2,1,0:T(8,128)}), f32[16,8,128]{2,1,0:T(8,128)S(1)}, u32[]{:S(2)}, u32[]{:S(2)}) %all-to-all-start.1) | async-done | bytes 65568 | tf_op jit(solution)/shard_map/all_to_all | solution.py:727
  43.0 0.7 join_sums.1
  43.8 5.7 %all-to-all-start.2 = ((bf16[16,32,512]{2,1,0:T(8,128)(2,1)}), bf16[16,32,512]{2,1,0:T(8,128)(2,1)S(1)}, u32[]{:S(2)}, u32[]{:S(2)}) async-start(bf16[16,32,512]{2,1,0:T(8,128)(2,1)} %bitcast.28), calls=%async_computation.2 | async-start | bytes 1048576 | tf_op jit(solution)/shard_map/all_to_all | solution.py:727
  49.5 5.8 %patch_slopes.1 = (bf16[1536,512]{1,0:T(8,128)(2,1)}, bf16[512,1536]{1,0:T(8,128)(2,1)}, bf16[384,512]{1,0:T(8,128)(2,1)}) custom-call(f32[64,192]{1,0:T(8,128)} %get-tuple-element.69.after_ref.rows_ref, bf16[512,384]{1,0:T(8,128)(2,1)} %bitcast.32, bf16[384,1536]{1,0:T(8,128)(2,1)} %wu_ref.3), custom_call_target="tpu_custom_call" | custom-call | flops 3000000000 | bytes 12000000 | tf_op jit(solution)/shard_map/patch_slopes/pallas_call | solution.py:112
  55.3 4.1 %all-to-all-done.2 = bf16[16,32,512]{2,1,0:T(8,128)(2,1)S(1)} async-done(((bf16[16,32,512]{2,1,0:T(8,128)(2,1)}), bf16[16,32,512]{2,1,0:T(8,128)(2,1)S(1)}, u32[]{:S(2)}, u32[]{:S(2)}) %all-to-all-start.2) | async-done | bytes 524320 | tf_op jit(solution)/shard_map/all_to_all | solution.py:727
  59.3 0.8 copy-done.14
  60.1 8.0 %patch_backward.1 = (bf16[6144,128]{1,0:T(8,128)(2,1)}, bf16[6144,128]{1,0:T(8,128)(2,1)}, f32[4,3]{1,0:T(4,128)}, f32[3,192]{1,0:T(4,128)}) custom-call(s32[6]{0:T(128)} %copy-done.2, s32[512]{0:T(512)} %slide_ref.5, bf16[16,2,16,512]{3,2,1,0:T(8,128)(2,1)} %bitcast.27, bf16[384,512]{1,0:T(8,128)(2,1)} %get-tuple-element.70.xt_in, ...), custom_call_target="tpu_custom_call" | custom-call | tf_op jit(solution)/shard_map/patch_backward/pallas_call | solution.py:630
  68.2 1.3 collective-permute-start
  69.4 1.4 copy-done
  70.8 0.1 bring_in.1
  71.0 1.7 %collective-permute-done = bf16[6144,128]{1,0:T(8,128)(2,1)S(1)} collective-permute-done((bf16[6144,128]{1,0:T(8,128)(2,1)}, bf16[6144,128]{1,0:T(8,128)(2,1)S(1)}, u32[]{:S(2)}, u32[]{:S(2)}) %collective-permute-start) | collective-permute-done | bytes 1572896 | tf_op jit(solution)/shard_map/ppermute | solution.py:731
  72.7 0.4 add_convert_fusion
  73.1 24.8 %all_to_all.25 = bf16[32,192,128]{2,1,0:T(8,128)(2,1)S(1)} all-to-all(bf16[32,192,128]{2,1,0:T(8,128)(2,1)S(1)} %bitcast.26), channel_id=1, replica_groups=mesh['zl'=2,'x'=4,'c'=2,'zh'=4,'y'=4] {'y','zl','x'}, dimensions={0} | all-to-all | bytes 3145728 | tf_op jit(solution)/shard_map/all_to_all | solution.py:727
  97.9 0.2 reduce_sum.12
  98.1 2.6 %collective-permute-start.3 = (bf16[192,128]{1,0:T(8,128)(2,1)S(1)}, bf16[192,128]{1,0:T(8,128)(2,1)S(1)}, u32[]{:S(2)}, u32[]{:S(2)}) collective-permute-start(bf16[192,128]{1,0:T(8,128)(2,1)S(1)} %reduce_sum.12), channel_id=1, source_target_pairs={{0,12},{4,8},{8,4},{12,0},{1,13},{5,9},{9,5},{13,1},{2,14},{6,10},... | collective-permute-start | bytes 147464 | tf_op jit(solution)/shard_map/ppermute | solution.py:743
  100.8 2.1 %collective-permute-start.2 = (bf16[192,128]{1,0:T(8,128)(2,1)S(1)}, bf16[192,128]{1,0:T(8,128)(2,1)S(1)}, u32[]{:S(2)}, u32[]{:S(2)}) collective-permute-start(bf16[192,128]{1,0:T(8,128)(2,1)S(1)} %reduce_sum.12), channel_id=1, source_target_pairs={{0,8},{4,12},{8,0},{12,4},{1,9},{5,13},{9,1},{13,5},{2,10},{6,14},... | collective-permute-start | bytes 147464 | tf_op jit(solution)/shard_map/ppermute | solution.py:743
  102.8 1.0 collective-permute-start.1
  103.9 0.0 collective-permute-done.3
  103.9 3.8 %collective-permute-done.2 = bf16[192,128]{1,0:T(8,128)(2,1)S(1)} collective-permute-done((bf16[192,128]{1,0:T(8,128)(2,1)S(1)}, bf16[192,128]{1,0:T(8,128)(2,1)S(1)}, u32[]{:S(2)}, u32[]{:S(2)}) %collective-permute-start.2) | collective-permute-done | bytes 49184 | tf_op jit(solution)/shard_map/ppermute | solution.py:743
  107.7 0.0 collective-permute-done.1
  107.7 0.3 broadcast_in_dim.2
  108.1 0.0 copy-start.3
  108.1 24.9 %all_to_all.26 = bf16[32,192,128]{2,1,0:T(8,128)(2,1)S(1)} all-to-all(bf16[32,192,128]{2,1,0:T(8,128)(2,1)S(1)} %broadcast_in_dim.2), channel_id=1, replica_groups=mesh['zl'=2,'x'=4,'c'=2,'zh'=4,'y'=4] {'y','zl','x'}, dimensions={0} | all-to-all | bytes 3145728 | tf_op jit(solution)/shard_map/all_to_all | solution.py:727
  133.0 4.4 %collective-permute-start.4 = (bf16[6144,128]{1,0:T(8,128)(2,1)S(1)}, bf16[6144,128]{1,0:T(8,128)(2,1)S(1)}, u32[]{:S(2)}, u32[]{:S(2)}) collective-permute-start(bf16[6144,128]{1,0:T(8,128)(2,1)S(1)} %bitcast.19), channel_id=1, source_target_pairs={{0,16},{16,0},{1,17},{17,1},{2,18},{18,2},{3,19},{19,3},{4,20},{20... | collective-permute-start | bytes 4718600 | tf_op jit(solution)/shard_map/ppermute | solution.py:731
  137.4 2.3 %unpack.2 = (f32[384,1536]{1,0:T(8,128)}, f32[1536,384]{1,0:T(8,128)}, f32[192,384]{1,0:T(8,128)}, f32[192,192]{1,0:T(8,128)}, f32[192,192]{1,0:T(8,128)}, /*ind...) custom-call(s32[6]{0:T(128)S(1)} %copy-done.3, ...), custom_call_target="tpu_custom_call" | custom-call | tf_op jit(solution)/shard_map/unpack/pallas_call | solution.py:694
  139.7 0.7 collective-permute-done.4.src_ref
  140.4 2.3 %unpack.3 = (f32[384,1536]{1,0:T(8,128)}, f32[1536,384]{1,0:T(8,128)}, f32[192,384]{1,0:T(8,128)}, f32[192,192]{1,0:T(8,128)}, f32[192,192]{1,0:T(8,128)}, /*ind...) custom-call(s32[6]{0:T(128)S(1)} %copy-done.3, ...), custom_call_target="tpu_custom_call", output_to_operand_aliasing={{0}: (2, {}), {1}: (3, {}), {2}: (4, {}), {3}: (5, {}), {4}... | custom-call | tf_op jit(solution)/shard_map/unpack/pallas_call | solution.py:694
  (15 shorter events, 0.1 us)
Async XLA Ops:
  0.6 11.9 %copy-start.8 = (f32[192,192]{1,0:T(8,128)S(1)}, f32[192,192]{1,0:T(8,128)}, u32[]{:S(2)}) copy-start(f32[192,192]{1,0:T(8,128)} %refs_4_.1) | copy-start | bytes 442372
  0.7 11.9 %copy-start.9 = (f32[192,192]{1,0:T(8,128)S(1)}, f32[192,192]{1,0:T(8,128)}, u32[]{:S(2)}) copy-start(f32[192,192]{1,0:T(8,128)} %refs_5_.1) | copy-start | bytes 442372
  0.7 11.9 %copy-start.10 = (bf16[192,192]{1,0:T(8,128)(2,1)S(1)}, bf16[192,192]{1,0:T(8,128)(2,1)}, u32[]{:S(2)}) copy-start(bf16[192,192]{1,0:T(8,128)(2,1)} %refs_0_.1) | copy-start | bytes 221188
  0.7 11.9 %copy-start.11 = (bf16[192,192]{1,0:T(8,128)(2,1)S(1)}, bf16[192,192]{1,0:T(8,128)(2,1)}, u32[]{:S(2)}) copy-start(bf16[192,192]{1,0:T(8,128)(2,1)} %refs_1_.1) | copy-start | bytes 221188
  0.7 11.9 %copy-start.12 = (bf16[192,192]{1,0:T(8,128)(2,1)S(1)}, bf16[192,192]{1,0:T(8,128)(2,1)}, u32[]{:S(2)}) copy-start(bf16[192,192]{1,0:T(8,128)(2,1)} %refs_2_.1) | copy-start | bytes 221188
  0.7 11.9 %copy-start.13 = (bf16[192,192]{1,0:T(8,128)(2,1)S(1)}, bf16[192,192]{1,0:T(8,128)(2,1)}, u32[]{:S(2)}) copy-start(bf16[192,192]{1,0:T(8,128)(2,1)} %refs_3_.1) | copy-start | bytes 221188
  5.3 14.3 %all-to-all-start = ((bf16[16,32,192]{2,1,0:T(8,128)(2,1)}), bf16[16,32,192]{2,1,0:T(8,128)(2,1)S(1)}, u32[]{:S(2)}, u32[]{:S(2)}) async-start(bf16[16,32,192]{2,1,0:T(8,128)(2,1)} %bitcast.34), calls=%async_computation | async-start | bytes 524288 | tf_op jit(solution)/shard_map/all_to_all | solution.py:727
  12.6 21.4 %copy-start.2 = (s32[6]{0:T(128)}, s32[6]{0:T(128)S(1)}, u32[]{:S(2)}) copy-start(s32[6]{0:T(128)S(1)} %stack.27.idx_ref) | copy-start | bytes 76
  12.6 7.0 %copy-start.1 = (s32[512,256]{1,0:T(8,128)S(1)}, s32[512,256]{1,0:T(8,128)}, u32[]{:S(2)}) copy-start(s32[512,256]{1,0:T(8,128)} %tis_ref.3) | copy-start | bytes 1572868
  12.6 7.0 %copy-start.4 = (s32[512]{0:T(512)S(1)}, s32[512]{0:T(512)}, u32[]{:S(2)}) copy-start(s32[512]{0:T(512)} %slide_ref.5) | copy-start | bytes 6148
  12.7 7.0 %copy-start.7 = (f32[192]{0:T(256)S(1)}, f32[192]{0:T(256)}, u32[]{:S(2)}) copy-start(f32[192]{0:T(256)} %param.27) | copy-start | bytes 2308
  12.7 21.3 %copy-start.5 = (f32[192,3]{0,1:T(4,128)S(1)}, f32[192,3]{0,1:T(4,128)}, u32[]{:S(2)}) copy-start(f32[192,3]{0,1:T(4,128)} %param.28) | copy-start | bytes 6916
  12.7 21.3 %copy-start.6 = (f32[4,3]{1,0:T(4,128)S(1)}, f32[4,3]{1,0:T(4,128)}, u32[]{:S(2)}) copy-start(f32[4,3]{1,0:T(4,128)} %gl_ref.3) | copy-start | bytes 148
  24.0 19.1 %all-to-all-start.1 = ((f32[16,8,128]{2,1,0:T(8,128)}), f32[16,8,128]{2,1,0:T(8,128)S(1)}, u32[]{:S(2)}, u32[]{:S(2)}) async-start(f32[16,8,128]{2,1,0:T(8,128)} %get-tuple-element.59), calls=%async_computation.1 | async-start | bytes 131072 | tf_op jit(solution)/shard_map/all_to_all | solution.py:727
  43.8 15.6 %all-to-all-start.2 = ((bf16[16,32,512]{2,1,0:T(8,128)(2,1)}), bf16[16,32,512]{2,1,0:T(8,128)(2,1)S(1)}, u32[]{:S(2)}, u32[]{:S(2)}) async-start(bf16[16,32,512]{2,1,0:T(8,128)(2,1)} %bitcast.28), calls=%async_computation.2 | async-start | bytes 1048576 | tf_op jit(solution)/shard_map/all_to_all | solution.py:727
  59.3 0.8 copy-start.14
  68.2 4.5 %collective-permute-start = (bf16[6144,128]{1,0:T(8,128)(2,1)}, bf16[6144,128]{1,0:T(8,128)(2,1)S(1)}, u32[]{:S(2)}, u32[]{:S(2)}) collective-permute-start(bf16[6144,128]{1,0:T(8,128)(2,1)} %get-tuple-element.78), channel_id=1, source_target_pairs={{0,16},{16,0},{1,17},{17,1},{2,18},{18,2},{3,19},{19,3},{4,20},{20... | collective-permute-start | bytes 4718600 | tf_op jit(solution)/shard_map/ppermute | solution.py:731
  69.4 1.4 copy-start
  98.1 5.7 %collective-permute-start.3 = (bf16[192,128]{1,0:T(8,128)(2,1)S(1)}, bf16[192,128]{1,0:T(8,128)(2,1)S(1)}, u32[]{:S(2)}, u32[]{:S(2)}) collective-permute-start(bf16[192,128]{1,0:T(8,128)(2,1)S(1)} %reduce_sum.12), channel_id=1, source_target_pairs={{0,12},{4,8},{8,4},{12,0},{1,13},{5,9},{9,5},{13,1},{2,14},{6,10},... | collective-permute-start | bytes 147464 | tf_op jit(solution)/shard_map/ppermute | solution.py:743
  100.8 6.9 %collective-permute-start.2 = (bf16[192,128]{1,0:T(8,128)(2,1)S(1)}, bf16[192,128]{1,0:T(8,128)(2,1)S(1)}, u32[]{:S(2)}, u32[]{:S(2)}) collective-permute-start(bf16[192,128]{1,0:T(8,128)(2,1)S(1)} %reduce_sum.12), channel_id=1, source_target_pairs={{0,8},{4,12},{8,0},{12,4},{1,9},{5,13},{9,1},{13,5},{2,10},{6,14},... | collective-permute-start | bytes 147464 | tf_op jit(solution)/shard_map/ppermute | solution.py:743
  102.8 4.8 %collective-permute-start.1 = (bf16[192,128]{1,0:T(8,128)(2,1)S(1)}, bf16[192,128]{1,0:T(8,128)(2,1)S(1)}, u32[]{:S(2)}, u32[]{:S(2)}) collective-permute-start(bf16[192,128]{1,0:T(8,128)(2,1)S(1)} %reduce_sum.12), channel_id=1, source_target_pairs={{0,4},{4,0},{8,12},{12,8},{1,5},{5,1},{9,13},{13,9},{2,6},{6,2},{1... | collective-permute-start | bytes 147464 | tf_op jit(solution)/shard_map/ppermute | solution.py:743
  108.1 29.3 %copy-start.3 = (s32[6]{0:T(128)S(1)}, s32[6]{0:T(128)}, u32[]{:S(2)}) copy-start(s32[6]{0:T(128)} %copy-done.2) | copy-start | bytes 76
  133.0 7.4 %collective-permute-start.4 = (bf16[6144,128]{1,0:T(8,128)(2,1)S(1)}, bf16[6144,128]{1,0:T(8,128)(2,1)S(1)}, u32[]{:S(2)}, u32[]{:S(2)}) collective-permute-start(bf16[6144,128]{1,0:T(8,128)(2,1)S(1)} %bitcast.19), channel_id=1, source_target_pairs={{0,16},{16,0},{1,17},{17,1},{2,18},{18,2},{3,19},{19,3},{4,20},{20... | collective-permute-start | bytes 4718600 | tf_op jit(solution)/shard_map/ppermute | solution.py:731
